TPU v7x, 32 devices: a whole 2x2x4 slice. The times are simulated.
32 devices in a mesh: seq: 8 (over z, x), blk: 4 (over y, core).
Axes of the slice: x: 2, y: 2, z: 4, core: 2. Of those that a mesh axis runs over, the one named last changes fastest.
Arguments:
- qkv: bfloat16 [4096, 3072], P(('seq', 'blk')), may hold values from -24 to 24
- kept_kv: bfloat16 [16, 2, 128, 1024], P('blk', None, None, 'seq'), may hold values from -24 to 24
- cur_list: int32 [32, 2], replicated, may hold values from 0 to 31, as said below
- kept_list: int32 [32, 12], replicated, may hold values from 0 to 15, as said below
- kept_count: int32 [32], replicated, may hold values from 1 to 12, as said below
Outputs:
- attn_out: bfloat16 [4096, 1024], P(('seq', 'blk'))
Inputs may be any that keep to these rules, and one draw needn't show every extreme that they name: `cur_list`: row t lists 2 different tiles t2 of tile t's spatial region, that is with (t2) % 4 equal to (t) % 4; the first entry is t itself. `kept_list`: each row names 12 different kept blocks. `kept_count`: some tile uses all 12 slots.
All inputs are finite; a program needn't handle non-finite values.
Results may differ from a plain program's by a relative error of at most 0.0025.
Values may be sent and summed in bfloat16 or wider, within the bound.
No kernel may reach another device: no remote copies, remote signals or barrier semaphores. Data moves between devices by JAX's collectives and lax.ppermute only.
A program may use at most 64 MiB of HBM per device.

v0:
```python
import math

import jax
import jax.numpy as jnp
from jax import lax
from jax.sharding import PartitionSpec as P

HEAD_DIM = 128


MASKED_SCORE = -1e30


def per_device(qkv, kept_kv, cur_list, kept_list, kept_count):
    seq_count = lax.axis_size("seq")
    blk_count = lax.axis_size("blk")
    tok_rows = qkv.shape[0]
    head_width = HEAD_DIM
    head_total = qkv.shape[1] // (3 * head_width)
    tile_len = kept_kv.shape[2]
    tiles_dev = tok_rows // tile_len
    shaped = qkv.reshape(tok_rows, 3, head_total, head_width)
    arrived = lax.all_to_all(shaped, "seq", split_axis=2, concat_axis=0, tiled=True)
    head_dev = arrived.shape[2]
    tile_mine = seq_count * tiles_dev
    grouped = arrived.reshape(tile_mine, tile_len, 3, head_dev, head_width)
    ordered = jnp.transpose(grouped, (2, 0, 3, 1, 4))
    queries_all = ordered[0]
    near_keys_all = ordered[1]
    near_values_all = ordered[2]
    kept_all = lax.all_gather(kept_kv, "blk", axis=0, tiled=True)
    kept_all = jnp.transpose(
        kept_all.reshape(kept_all.shape[0], 2, tile_len, head_dev, head_width), (0, 1, 3, 2, 4)
    )
    far_keys_all = kept_all[:, 0]
    far_values_all = kept_all[:, 1]
    region = lax.axis_index("blk")
    local_ids = jnp.arange(tile_mine, dtype=jnp.int32)
    tile_ids = (local_ids // tiles_dev * blk_count + region) * tiles_dev + local_ids % tiles_dev
    cur_ids = cur_list[tile_ids]
    cur_local = cur_ids // tiles_dev // blk_count * tiles_dev + cur_ids % tiles_dev
    kept_ids = kept_list[tile_ids]
    slot_counts = kept_count[tile_ids]
    score_scale = 1.0 / math.sqrt(head_width)
    window_slots = kept_ids.shape[1]
    near_count = cur_local.shape[1]
    tiles_step = 4
    step_total = tile_mine // tiles_step

    def attend(pieces):
        queries, cur_sel, kept_sel, slot_count = pieces
        near_keys = near_keys_all[cur_sel]
        near_values = near_values_all[cur_sel]
        near_scores = (
            jnp.einsum("bhid,bnhkd->bhink", queries, near_keys, preferred_element_type=jnp.float32)
            * score_scale
        )
        near_max = near_scores.max(axis=(3, 4))[..., None, None]
        far_keys = far_keys_all[kept_sel]
        far_values = far_values_all[kept_sel]
        far_scores = (
            jnp.einsum("bhid,bwhkd->bhiwk", queries, far_keys, preferred_element_type=jnp.float32)
            * score_scale
        )
        is_live = (jnp.arange(window_slots)[None, :] < slot_count[:, None])[:, None, None, :, None]
        far_scores = jnp.where(is_live, far_scores, MASKED_SCORE)
        row_max = jnp.maximum(near_max, far_scores.max(axis=(3, 4))[..., None, None])
        near_weights = jnp.exp(near_scores - row_max)
        far_weights = jnp.where(is_live, jnp.exp(far_scores - row_max), 0.0)
        row_total = near_weights.sum(axis=(3, 4)) + far_weights.sum(axis=(3, 4))
        mixture = jnp.einsum(
            "bhink,bnhkd->bhid",
            near_weights.astype(jnp.bfloat16),
            near_values,
            preferred_element_type=jnp.float32,
        )
        mixture = mixture + jnp.einsum(
            "bhiwk,bwhkd->bhid",
            far_weights.astype(jnp.bfloat16),
            far_values,
            preferred_element_type=jnp.float32,
        )
        result_rows = (mixture / row_total[..., None]).astype(jnp.bfloat16)
        return jnp.transpose(result_rows, (0, 2, 1, 3))

    attended = lax.map(
        attend,
        (
            queries_all.reshape(step_total, tiles_step, head_dev, tile_len, head_width),
            cur_local.reshape(step_total, tiles_step, near_count),
            kept_ids.reshape(step_total, tiles_step, window_slots),
            slot_counts.reshape(step_total, tiles_step),
        ),
    )
    attended = attended.reshape(seq_count * tok_rows, head_dev, head_width)
    returned = lax.all_to_all(attended, "seq", split_axis=0, concat_axis=1, tiled=True)
    return returned.reshape(tok_rows, head_total * head_width)


def solution(mesh):
    placed = (P(("seq", "blk"), None), P("blk", None, None, "seq"), P(), P(), P())
    return jax.shard_map(
        per_device, mesh=mesh, in_specs=placed, out_specs=P(("seq", "blk"), None), check_vma=False
    )
```

profile of v0, /device:TPU:0, one launch (start us, length us, event | category | flops | bytes accessed | tf_op | source)
XLA Modules:
  0.0 102.7 jit_solution(69293637863069503)
XLA Ops:
  6.5 1.5 %copy.58 = bf16[128,3072]{0,1:T(8,128)(2,1)S(1)} copy(bf16[128,3072]{1,0:T(8,128)(2,1)} %param.7) | data formatting | bytes 1572864 | tf_op args[0]
  8.1 1.0 copy.59
  9.1 7.3 %all-to-all-start = ((bf16[128,3,8,128]{0,3,1,2:T(8,128)(2,1)}), bf16[128,3,8,128]{0,3,1,2:T(8,128)(2,1)S(1)}, u32[]{:S(2)}, u32[]{:S(2)}) async-start(bf16[128,3,8,128]{0,3,1,2:T(8,128)(2,1)} %copy.59), calls=%async_computation | async-start | bytes 1572864 | tf_op jit(solution)/shard_map/all_to_all | solution.py:23
  16.4 0.7 copy.63
  17.1 0.1 copy.60
  17.2 0.6 gather_fusion.4
  17.8 0.1 copy.76
  17.9 0.1 copy.62
  18.0 0.6 gather_fusion.6
  18.5 0.6 gather_fusion.5
  19.2 0.1 reshape.193
  19.3 17.2 %all-to-all-done = bf16[128,3,8,128]{0,3,1,2:T(8,128)(2,1)S(1)} async-done(((bf16[128,3,8,128]{0,3,1,2:T(8,128)(2,1)}), bf16[128,3,8,128]{0,3,1,2:T(8,128)(2,1)S(1)}, u32[]{:S(2)}, u32[]{:S(2)}) %all-to-all-start) | async-done | bytes 786464 | tf_op jit(solution)/shard_map/all_to_all | solution.py:23
  36.6 0.9 copy.66
  37.4 0.9 copy.67
  38.3 2.3 %slice_bitcast_fusion = (bf16[16,1,128,128]{3,2,1,0:T(8,128)(2,1)}, bf16[16,1,128,128]{3,2,1,0:T(8,128)(2,1)}) fusion(bf16[16,2,1,128,128]{4,3,0,2,1:T(8,128)(2,1)} %bitcast.132), kind=kLoop, calls=%fused_computation.44 | loop fusion | bytes 2097152 | tf_op jit(solution)/shard_map/squeeze | solution.py:36
  40.6 38.3 %while.10 = (s32[]{:T(128)}, bf16[2,4,128,1,128]{4,2,1,3,0:T(8,128)(2,1)}, bf16[2,4,1,128,128]{3,4,1,0,2:T(8,128)(2,1)S(1)}, s32[2,4,2]{1,0,2:T(2,128)S(1)}, bf1...) while((s32[]{:T(128)}, ...), condition=%wide.region_5.6_spmd, body=%wide.region_0.5_spmd.sunk | while | flops 480969952 | bytes 27174448 | solution.py:86
  40.6 0.1 reshape.297
  40.7 3.0 %gather_fusion.2 = bf16[48,128,128]{2,1,0:T(8,128)(2,1)} fusion(bf16[16,128,128]{2,1,0:T(8,128)(2,1)} %bitcast.117, s32[1024]{0:T(1024)S(1)} %pad_clamp_fusion.6), kind=kCustom, calls=%fused_computation.1.clone.1 | custom fusion | bytes 3145920 | tf_op jit(solution)/shard_map/while/body/eval_jaxpr/gather | solution.py:59
  43.8 2.0 %fusion.65 = (f32[4,128]{1,0:T(4,128)S(1)}, f32[4,128,12,128]{1,3,2,0:T(8,128)S(1)}) fusion(pred[4,12]{1,0:T(4,128)(4,1)S(1)} %iota_compare_fusion.2, bf16[4,12,128,128]{3,2,1,0:T(8,128)(2,1)} %bitcast.121, bf16[2,4,1,128,128]{3,4,1,0,2:T(8,128)(2,1)S(1)} %get-tuple-element.230, s32[]{:T(128)} %get-tuple-element.217), kind=kOutput, calls=%fused_computation.9.clone.1 | convolution fusion | flops 203685376 | bytes 4852228 | tf_op jit(solution)/shard_map/while/body/eval_jaxpr/bhid,bwhkd->bhiwk/dot_general | solution.py:62
  45.8 0.1 copy.82
  45.9 0.1 reshape.296
  46.0 1.5 %gather_fusion.1 = bf16[8,128,128]{2,1,0:T(8,128)(2,1)S(1)} fusion(bf16[8,128,128]{2,1,0:T(8,128)(2,1)} %bitcast.127, s32[1024]{0:T(1024)S(1)} %pad_clamp_fusion.5), kind=kCustom, calls=%fused_computation.clone.1 | custom fusion | bytes 524320 | tf_op jit(solution)/shard_map/while/body/eval_jaxpr/gather | solution.py:52
  47.6 1.1 %fusion.63 = (f32[4,128]{1,0:T(4,128)S(1)}, f32[4,128,2,128]{1,3,2,0:T(8,128)S(1)}) fusion(bf16[4,2,128,128]{3,2,1,0:T(8,128)(2,1)S(1)} %bitcast.124, bf16[2,4,1,128,128]{3,4,1,0,2:T(8,128)(2,1)} %copy-done.2, s32[]{:T(128)} %get-tuple-element.217), kind=kOutput, calls=%fused_computation.55.clone.1 | convolution fusion | flops 33816064 | bytes 920064 | tf_op jit(solution)/shard_map/while/body/eval_jaxpr/bhid,bnhkd->bhink/dot_general | solution.py:55
  48.7 0.9 fusion.67
  49.7 0.1 fusion.66
  49.8 1.5 %gather_fusion = bf16[8,128,128]{2,1,0:T(8,128)(2,1)S(1)} fusion(bf16[8,128,128]{2,1,0:T(8,128)(2,1)} %bitcast.128, s32[1024]{0:T(1024)S(1)} %pad_clamp_fusion.5), kind=kCustom, calls=%fused_computation.2.clone.1 | custom fusion | bytes 524320 | tf_op jit(solution)/shard_map/while/body/eval_jaxpr/gather | solution.py:53
  51.4 2.1 %convolution_bitcast_fusion.2 = f32[4,128,128]{2,1,0:T(8,128)} fusion(bf16[4,2,128,128]{3,2,1,0:T(8,128)(2,1)S(1)} %bitcast.125, f32[4,128,2,128]{1,3,2,0:T(8,128)} %copy-done.1, f32[4,128]{1,0:T(4,128)S(1)} %max.9), kind=kOutput, calls=%fused_computation.15.clone.1 | convolution fusion | flops 33816576 | bytes 1050624 | tf_op jit(solution)/shard_map/while/body/eval_jaxpr/bhink,bnhkd->bhid/dot_general | solution.py:71
  53.4 3.0 %gather_fusion.3 = bf16[48,128,128]{2,1,0:T(8,128)(2,1)} fusion(bf16[16,128,128]{2,1,0:T(8,128)(2,1)} %bitcast.122, s32[1024]{0:T(1024)S(1)} %pad_clamp_fusion.6), kind=kCustom, calls=%fused_computation.3.clone.1 | custom fusion | bytes 3145920 | tf_op jit(solution)/shard_map/while/body/eval_jaxpr/gather | solution.py:60
  56.4 3.3 %fusion.68 = bf16[2,4,128,1,128]{4,2,1,3,0:T(8,128)(2,1)} fusion(bf16[2,4,128,1,128]{4,2,1,3,0:T(8,128)(2,1)} %get-tuple-element.218, s32[]{:T(128)} %get-tuple-element.217, f32[4,128,128]{2,1,0:T(8,128)} %convolution_bitcast_fusion.2, bf16[4,12,128,128]{3,2,1,0:T(8,128)(2,1)} %bitcast.123, f32[4,128,12,128]{1,3,2,0:T(8,128)S(1)} %get-tuple-element.205, ...), kind=kOutput, calls=%fused_computation.21.clone.1 | convolution fusion | flops 205455360 | bytes 5116464 | tf_op jit(solution)/shard_map/while/body/eval_jaxpr/bhiwk,bwhkd->bhid/dot_general | solution.py:77
  59.7 0.1 reshape.297
  59.8 3.0 %gather_fusion.2 = bf16[48,128,128]{2,1,0:T(8,128)(2,1)} fusion(bf16[16,128,128]{2,1,0:T(8,128)(2,1)} %bitcast.117, s32[1024]{0:T(1024)S(1)} %pad_clamp_fusion.6), kind=kCustom, calls=%fused_computation.1.clone.1 | custom fusion | bytes 3145920 | tf_op jit(solution)/shard_map/while/body/eval_jaxpr/gather | solution.py:59
  62.9 2.0 %fusion.65 = (f32[4,128]{1,0:T(4,128)S(1)}, f32[4,128,12,128]{1,3,2,0:T(8,128)S(1)}) fusion(pred[4,12]{1,0:T(4,128)(4,1)S(1)} %iota_compare_fusion.2, bf16[4,12,128,128]{3,2,1,0:T(8,128)(2,1)} %bitcast.121, bf16[2,4,1,128,128]{3,4,1,0,2:T(8,128)(2,1)S(1)} %get-tuple-element.230, s32[]{:T(128)} %get-tuple-element.217), kind=kOutput, calls=%fused_computation.9.clone.1 | convolution fusion | flops 203685376 | bytes 4852228 | tf_op jit(solution)/shard_map/while/body/eval_jaxpr/bhid,bwhkd->bhiwk/dot_general | solution.py:62
  65.0 0.1 copy.82
  65.1 0.1 reshape.296
  65.2 1.5 %gather_fusion.1 = bf16[8,128,128]{2,1,0:T(8,128)(2,1)S(1)} fusion(bf16[8,128,128]{2,1,0:T(8,128)(2,1)} %bitcast.127, s32[1024]{0:T(1024)S(1)} %pad_clamp_fusion.5), kind=kCustom, calls=%fused_computation.clone.1 | custom fusion | bytes 524320 | tf_op jit(solution)/shard_map/while/body/eval_jaxpr/gather | solution.py:52
  66.7 1.1 %fusion.63 = (f32[4,128]{1,0:T(4,128)S(1)}, f32[4,128,2,128]{1,3,2,0:T(8,128)S(1)}) fusion(bf16[4,2,128,128]{3,2,1,0:T(8,128)(2,1)S(1)} %bitcast.124, bf16[2,4,1,128,128]{3,4,1,0,2:T(8,128)(2,1)} %copy-done.2, s32[]{:T(128)} %get-tuple-element.217), kind=kOutput, calls=%fused_computation.55.clone.1 | convolution fusion | flops 33816064 | bytes 920064 | tf_op jit(solution)/shard_map/while/body/eval_jaxpr/bhid,bnhkd->bhink/dot_general | solution.py:55
  67.9 0.9 fusion.67
  68.8 0.1 fusion.66
  68.9 1.5 %gather_fusion = bf16[8,128,128]{2,1,0:T(8,128)(2,1)S(1)} fusion(bf16[8,128,128]{2,1,0:T(8,128)(2,1)} %bitcast.128, s32[1024]{0:T(1024)S(1)} %pad_clamp_fusion.5), kind=kCustom, calls=%fused_computation.2.clone.1 | custom fusion | bytes 524320 | tf_op jit(solution)/shard_map/while/body/eval_jaxpr/gather | solution.py:53
  70.5 2.1 %convolution_bitcast_fusion.2 = f32[4,128,128]{2,1,0:T(8,128)} fusion(bf16[4,2,128,128]{3,2,1,0:T(8,128)(2,1)S(1)} %bitcast.125, f32[4,128,2,128]{1,3,2,0:T(8,128)} %copy-done.1, f32[4,128]{1,0:T(4,128)S(1)} %max.9), kind=kOutput, calls=%fused_computation.15.clone.1 | convolution fusion | flops 33816576 | bytes 1050624 | tf_op jit(solution)/shard_map/while/body/eval_jaxpr/bhink,bnhkd->bhid/dot_general | solution.py:71
  72.5 3.0 %gather_fusion.3 = bf16[48,128,128]{2,1,0:T(8,128)(2,1)} fusion(bf16[16,128,128]{2,1,0:T(8,128)(2,1)} %bitcast.122, s32[1024]{0:T(1024)S(1)} %pad_clamp_fusion.6), kind=kCustom, calls=%fused_computation.3.clone.1 | custom fusion | bytes 3145920 | tf_op jit(solution)/shard_map/while/body/eval_jaxpr/gather | solution.py:60
  75.6 3.3 %fusion.68 = bf16[2,4,128,1,128]{4,2,1,3,0:T(8,128)(2,1)} fusion(bf16[2,4,128,1,128]{4,2,1,3,0:T(8,128)(2,1)} %get-tuple-element.218, s32[]{:T(128)} %get-tuple-element.217, f32[4,128,128]{2,1,0:T(8,128)} %convolution_bitcast_fusion.2, bf16[4,12,128,128]{3,2,1,0:T(8,128)(2,1)} %bitcast.123, f32[4,128,12,128]{1,3,2,0:T(8,128)S(1)} %get-tuple-element.205, ...), kind=kOutput, calls=%fused_computation.21.clone.1 | convolution fusion | flops 205455360 | bytes 5116464 | tf_op jit(solution)/shard_map/while/body/eval_jaxpr/bhiwk,bwhkd->bhid/dot_general | solution.py:77
  78.9 0.6 broadcast.241
  79.4 1.7 %reduce.8 = bf16[1024,128]{1,0:T(8,128)(2,1)S(1)} reduce(bf16[1024,1,128]{2,0,1:T(8,128)(2,1)} %bitcast.134, bf16[]{:T(256)} %broadcast.241), dimensions={1}, to_apply=%copy.68.reduce_sub_computation | reduce | bytes 524290 | tf_op jit(solution)/shard_map/reshape | solution.py:95
  81.3 13.2 %all_to_all.27 = bf16[8,2,8192]{2,1,0:T(2,128)(2,1)S(1)} all-to-all(bf16[8,2,8192]{2,1,0:T(2,128)(2,1)S(1)} %reshape.276), channel_id=1, replica_groups=mesh['seq'=8,'blk'=4] {'seq'}, dimensions={0} | all-to-all | bytes 524288 | tf_op jit(solution)/shard_map/all_to_all | solution.py:96
  94.5 0.3 reshape.277
  94.8 0.2 copy.69
  95.0 0.9 copy.70
  (48 shorter events, 0.5 us)
Async XLA Ops:
  6.5 12.0 %copy-start = (s32[32]{0:T(128)S(1)}, s32[32]{0:T(128)}, u32[]{:S(2)}) copy-start(s32[32]{0:T(128)} %param.11) | copy-start | bytes 388
  6.5 9.8 %copy-start.4 = (bf16[4,2,128,128]{3,2,1,0:T(8,128)(2,1)S(1)}, bf16[4,2,128,128]{3,2,1,0:T(8,128)(2,1)}, u32[]{:S(2)}) copy-start(bf16[4,2,128,128]{3,2,1,0:T(8,128)(2,1)} %param.8) | copy-start | bytes 786436
  6.5 10.6 %copy-start.6 = (s32[32,2]{0,1:T(2,128)S(1)}, s32[32,2]{0,1:T(2,128)}, u32[]{:S(2)}) copy-start(s32[32,2]{0,1:T(2,128)} %param.9) | copy-start | bytes 772
  6.5 11.4 %copy-start.5 = (s32[32,12]{0,1:T(8,128)S(1)}, s32[32,12]{0,1:T(8,128)}, u32[]{:S(2)}) copy-start(s32[32,12]{0,1:T(8,128)} %param.10) | copy-start | bytes 4612
  9.1 27.4 %all-to-all-start = ((bf16[128,3,8,128]{0,3,1,2:T(8,128)(2,1)}), bf16[128,3,8,128]{0,3,1,2:T(8,128)(2,1)S(1)}, u32[]{:S(2)}, u32[]{:S(2)}) async-start(bf16[128,3,8,128]{0,3,1,2:T(8,128)(2,1)} %copy.59), calls=%async_computation | async-start | bytes 1572864 | tf_op jit(solution)/shard_map/all_to_all | solution.py:23
  16.3 22.0 %all-gather.2.cloned.1.call-start = ((), (), s32[]{:S(2)}) async-start(), calls=%async_computation.2 | async-start | bytes 1310720 | tf_op jit(solution)/shard_map/all_gather | solution.py:31
  40.6 5.2 %copy-start.2 = (bf16[2,4,1,128,128]{3,4,1,0,2:T(8,128)(2,1)}, bf16[2,4,1,128,128]{3,4,1,0,2:T(8,128)(2,1)S(1)}, u32[]{:S(2)}) copy-start(bf16[2,4,1,128,128]{3,4,1,0,2:T(8,128)(2,1)S(1)} %get-tuple-element.230) | copy-start | bytes 786436 | tf_op jit(solution)/shard_map/while
  48.7 1.0 copy-start.1
  56.4 3.3 %copy-start.3 = (bf16[2,4,1,128,128]{3,4,1,0,2:T(8,128)(2,1)S(1)}, bf16[2,4,1,128,128]{3,4,1,0,2:T(8,128)(2,1)}, u32[]{:S(2)}) copy-start(bf16[2,4,1,128,128]{3,4,1,0,2:T(8,128)(2,1)} %copy-done.2) | copy-start | bytes 786436 | tf_op jit(solution)/shard_map/while
  59.7 5.2 %copy-start.2 = (bf16[2,4,1,128,128]{3,4,1,0,2:T(8,128)(2,1)}, bf16[2,4,1,128,128]{3,4,1,0,2:T(8,128)(2,1)S(1)}, u32[]{:S(2)}) copy-start(bf16[2,4,1,128,128]{3,4,1,0,2:T(8,128)(2,1)S(1)} %get-tuple-element.230) | copy-start | bytes 786436 | tf_op jit(solution)/shard_map/while
  67.9 1.0 copy-start.1
  75.6 3.3 %copy-start.3 = (bf16[2,4,1,128,128]{3,4,1,0,2:T(8,128)(2,1)S(1)}, bf16[2,4,1,128,128]{3,4,1,0,2:T(8,128)(2,1)}, u32[]{:S(2)}) copy-start(bf16[2,4,1,128,128]{3,4,1,0,2:T(8,128)(2,1)} %copy-done.2) | copy-start | bytes 786436 | tf_op jit(solution)/shard_map/while
Sparse Core Ops, SparseCore 0:
  18.7 18.1 all-gather.1
where the time goes:
time: 103 us
  local copies, waits for them, and re-layouts  30.2 us (29%)
  waiting for transfers between devices  17.2 us (17%)
  matrix products  17 us (17%)
  between operations  13.5 us (13%)
  blocking collectives  13.2 us (13%)
  starting transfers between devices  7.29 us (7%)
  other arithmetic  4.05 us (4%)
    all_to_all x1, waiting for transfers between devices, per_device(): lax.all_to_all(shaped, 'seq', split_axis=2, concat_axis=0, tiled=True)  17.2 us
    all_to_all x1, blocking collectives, per_device(): lax.all_to_all(attended, 'seq', split_axis=0, concat_axis=1, tiled=True)  13.2 us
    all_to_all x1, starting transfers between devices, per_device(): lax.all_to_all(shaped, 'seq', split_axis=2, concat_axis=0, tiled=True)  7.25 us
    dot_general x2, matrix products, attend(): jnp.einsum('bhiwk,bwhkd->bhid', far_weights.astype(jnp.bfloat16), far_val...  6.6 us
    gather x2, local copies, waits for them, and re-layouts, attend(): far_keys = far_keys_all[kept_sel]  6.04 us
    gather x2, local copies, waits for them, and re-layouts, attend(): far_values = far_values_all[kept_sel]  6.02 us
    dot_general x2, matrix products, attend(): jnp.einsum('bhink,bnhkd->bhid', near_weights.astype(jnp.bfloat16), near_v...  4.11 us
    dot_general x2, matrix products, attend(): jnp.einsum('bhid,bwhkd->bhiwk', queries, far_keys, preferred_element_type...  3.98 us
  transfers between devices with their start and end apart: 2, of which 1 were waited for; matrix products, arithmetic and copies ran while one was open for 5% of the time, Pallas kernels for 0%

commit v1 on v0

v1 whole, which is shorter than its diff:
```python
import functools
import math

import jax
import jax.numpy as jnp
from jax import lax
from jax.experimental import pallas as pl
from jax.experimental.pallas import tpu as pltpu
from jax.sharding import PartitionSpec as P

HEAD_DIM = 128
MASKED_SCORE = -1e30
CHUNK = 4
VMEM_BYTES = 40 * 1024 * 1024


def pack_kernel(qkv_ref, out_ref):
    dests, groups, _, width = out_ref.shape
    for dest in range(dests):
        for group in range(groups):
            start = (group * dests + dest) * width
            out_ref[dest, group] = qkv_ref[:, start : start + width]


def unpack_kernel(parts_ref, out_ref):
    sources, _, width = parts_ref.shape
    for source in range(sources):
        out_ref[:, source * width : (source + 1) * width] = parts_ref[source]


def attention_kernel(
    blk_count,
    tile_len,
    place_ref,
    cur_ref,
    kept_list_ref,
    kept_count_ref,
    span_hbm,
    *refs,
):
    kept_hbm = refs[:blk_count]
    out_ref, span, kept, scores, span_sem, kept_sem = refs[blk_count:]
    sources, _, tok_rows, width = span.shape
    tiles_dev = tok_rows // tile_len
    heads = width // HEAD_DIM
    kept_dev = kept_hbm[0].shape[0]
    near_count = cur_ref.shape[0]
    window = kept_list_ref.shape[0]
    region = place_ref[0]

    span_copy = pltpu.make_async_copy(span_hbm, span, span_sem)
    span_copy.start()
    kept_copies = []
    for i in range(blk_count):
        start = place_ref[1 + i] * kept_dev
        copy = pltpu.make_async_copy(kept_hbm[i], kept.at[pl.ds(start, kept_dev)], kept_sem.at[i])
        copy.start()
        kept_copies.append(copy)
    for copy in kept_copies:
        copy.wait()
    span_copy.wait()

    scale = 1.0 / math.sqrt(HEAD_DIM)
    chunks = [range(i, min(i + CHUNK, window)) for i in range(0, window, CHUNK)]

    def dot_keys(queries, keys):
        return lax.dot_general(
            queries, keys, (((1,), (1,)), ((), ())), preferred_element_type=jnp.float32
        ) * scale

    def one_tile(j, _):
        source = j // tiles_dev
        place = j % tiles_dev
        tile = (source * blk_count + region) * tiles_dev + place
        rows = pl.ds(pl.multiple_of(place * tile_len, tile_len), tile_len)
        count = kept_count_ref[tile]
        near = []
        for c in range(near_count):
            t2 = cur_ref[c, tile]
            near.append((t2 // tiles_dev // blk_count, t2 % tiles_dev))
        near_rows = [(s, pl.ds(pl.multiple_of(p * tile_len, tile_len), tile_len)) for s, p in near]
        far_ids = [kept_list_ref[w, tile] for w in range(window)]
        for h in range(heads):
            cols = slice(h * HEAD_DIM, (h + 1) * HEAD_DIM)
            queries = span[source, 0, rows, cols]

            def far_scores(slots):
                keys = jnp.concatenate([kept[far_ids[w], 0, :, cols] for w in slots], axis=0)
                raw = dot_keys(queries, keys)
                slot = lax.broadcasted_iota(jnp.int32, raw.shape, 1) // tile_len + slots[0]
                return jnp.where(slot < count, raw, MASKED_SCORE)

            def far_values(slots):
                return jnp.concatenate([kept[far_ids[w], 1, :, cols] for w in slots], axis=0)

            def weigh(raw, top, values):
                weights = jnp.exp(raw - top)
                total = jnp.sum(weights, axis=1, keepdims=True)
                mixed = jnp.dot(
                    weights.astype(jnp.bfloat16), values, preferred_element_type=jnp.float32
                )
                return total, mixed

            near_keys = jnp.concatenate([span[s, 1, r, cols] for s, r in near_rows], axis=0)
            near_raw = dot_keys(queries, near_keys)
            first_raw = far_scores(chunks[0])
            top = jnp.maximum(
                jnp.max(near_raw, axis=1, keepdims=True), jnp.max(first_raw, axis=1, keepdims=True)
            )
            for chunk in chunks[1:]:

                def more(top, chunk=chunk):
                    raw = far_scores(chunk)
                    scores[:, chunk[0] * tile_len : (chunk[-1] + 1) * tile_len] = raw
                    return jnp.maximum(top, jnp.max(raw, axis=1, keepdims=True))

                top = lax.cond(chunk[0] < count, more, lambda top: top, top)
            near_values = jnp.concatenate([span[s, 2, r, cols] for s, r in near_rows], axis=0)
            near_total, near_mixed = weigh(near_raw, top, near_values)
            first_total, first_mixed = weigh(first_raw, top, far_values(chunks[0]))
            total, mixed = near_total + first_total, near_mixed + first_mixed
            for chunk in chunks[1:]:

                def add(carry, chunk=chunk):
                    raw = scores[:, chunk[0] * tile_len : (chunk[-1] + 1) * tile_len]
                    more_total, more_mixed = weigh(raw, top, far_values(chunk))
                    return carry[0] + more_total, carry[1] + more_mixed

                total, mixed = lax.cond(
                    chunk[0] < count, add, lambda carry: carry, (total, mixed)
                )
            out_ref[source, rows, cols] = (mixed / total).astype(jnp.bfloat16)
        return 0

    lax.fori_loop(0, sources * tiles_dev, one_tile, 0)


def gather_kept(kept_kv, blk_count):
    me = lax.axis_index("blk")
    if blk_count % 2:
        pieces = [kept_kv]
        origins = [me]
        for d in range(1, blk_count):
            pieces.append(
                lax.ppermute(kept_kv, "blk", [(i, (i + d) % blk_count) for i in range(blk_count)])
            )
            origins.append((me - d) % blk_count)
        return pieces, origins
    pair = [(i, i ^ 1) for i in range(blk_count)]
    pieces, origins = [], []
    for d in range(0, blk_count, 2):
        if d:
            shift = [(i, (i + d) % blk_count) for i in range(blk_count)]
            piece = lax.ppermute(kept_kv, "blk", shift)
        else:
            piece = kept_kv
        pieces += [piece, lax.ppermute(piece, "blk", pair)]
        origins += [(me - d) % blk_count, ((me ^ 1) - d) % blk_count]
    return pieces, origins


def per_device(qkv, kept_kv, cur_list, kept_list, kept_count):
    seq_count = lax.axis_size("seq")
    blk_count = lax.axis_size("blk")
    tok_rows = qkv.shape[0]
    kept_dev, _, tile_len, width = kept_kv.shape
    dtype = qkv.dtype
    vmem = pl.BlockSpec(memory_space=pltpu.VMEM)
    smem = pl.BlockSpec(memory_space=pltpu.SMEM)
    anywhere = pl.BlockSpec(memory_space=pl.ANY)
    params = pltpu.CompilerParams(vmem_limit_bytes=VMEM_BYTES)

    packed = pl.pallas_call(
        pack_kernel,
        out_shape=jax.ShapeDtypeStruct((seq_count, 3, tok_rows, width), dtype),
        in_specs=[vmem],
        out_specs=vmem,
        compiler_params=params,
        name="pack",
    )(qkv)
    span = lax.all_to_all(packed, "seq", split_axis=0, concat_axis=0, tiled=True)
    pieces, origins = gather_kept(kept_kv, blk_count)
    place = jnp.stack([lax.axis_index("blk"), *origins]).astype(jnp.int32)

    attended = pl.pallas_call(
        functools.partial(attention_kernel, blk_count, tile_len),
        out_shape=jax.ShapeDtypeStruct((seq_count, tok_rows, width), dtype),
        in_specs=[smem] * 4 + [anywhere] * (1 + blk_count),
        out_specs=vmem,
        scratch_shapes=[
            pltpu.VMEM((seq_count, 3, tok_rows, width), dtype),
            pltpu.VMEM((blk_count * kept_dev, 2, tile_len, width), dtype),
            pltpu.VMEM((tile_len, kept_list.shape[1] * tile_len), jnp.float32),
            pltpu.SemaphoreType.DMA,
            pltpu.SemaphoreType.DMA((blk_count,)),
        ],
        compiler_params=params,
        name="attention",
    )(place, cur_list.T, kept_list.T, kept_count, span, *pieces)

    returned = lax.all_to_all(attended, "seq", split_axis=0, concat_axis=0, tiled=True)
    return pl.pallas_call(
        unpack_kernel,
        out_shape=jax.ShapeDtypeStruct((tok_rows, seq_count * width), dtype),
        in_specs=[vmem],
        out_specs=vmem,
        compiler_params=params,
        name="unpack",
    )(returned)


def solution(mesh):
    placed = (P(("seq", "blk"), None), P("blk", None, None, "seq"), P(), P(), P())
    return jax.shard_map(
        per_device, mesh=mesh, in_specs=placed, out_specs=P(("seq", "blk"), None), check_vma=False
    )
```

time: 103 us -> 49.9 us (0.48)
  local copies, waits for them, and re-layouts: 30.2 us -> 1.9 us
  matrix products: 17 us -> 0 us
  between operations: 13.5 us -> 0.02 us
  Pallas kernels: 0 us -> 8.43 us
  other arithmetic: 4.05 us -> 0 us
  starting transfers between devices: 7.29 us -> 8.97 us
  blocking collectives: 13.2 us -> 11.7 us
  waiting for transfers between devices: 17.2 us -> 18.5 us
    gather x12 -> x0, local copies, waits for them, and re-layouts: 20.1 us -> none  [the longest x2 6.04 us: attend(): far_keys = far_keys_all[kept_sel]]
    dot_general x8 -> x0, matrix products: 17 us -> none  [the longest x2 6.6 us: attend(): jnp.einsum('bhiwk,bwhkd->bhid', far_weights.astype(jnp.bfloat16), far_val...]
    pallas_call x0 -> x3, Pallas kernels: none -> 8.43 us  [the longest x1 6.63 us: per_device(): pl.pallas_call(functools.partial(attention_kernel, blk_count, tile_len),...]
    ppermute x0 -> x3, waiting for transfers between devices: none -> 7.69 us  [the longest x1 6.24 us: gather_kept(): piece = lax.ppermute(kept_kv, 'blk', shift)]
    all_to_all x1, waiting for transfers between devices: 17.2 us -> 10.8 us  [per_device(): lax.all_to_all(packed, 'seq', split_axis=0, concat_axis=0, tiled=True)]
    reshape x4 -> x0, local copies, waits for them, and re-layouts: 2.49 us -> none  [the longest x1 0.97 us: per_device(): shaped = qkv.reshape(tok_rows, 3, head_total, head_width)]
    squeeze x2 -> x0, local copies, waits for them, and re-layouts: 2.35 us -> none  [the longest x1 2.28 us: per_device(): far_values_all = kept_all[:, 1]]
    reduce_sum x4 -> x0, other arithmetic: 2.06 us -> none  [attend(): row_total = near_weights.sum(axis=(3, 4)) + far_weights.sum(axis=(3, 4))]
  transfers between devices with their start and end apart: 2 -> 4, of which waited for: 1 -> 3; matrix products, arithmetic and copies ran while one was open for 5% -> 0% of each run, Pallas kernels for 0% -> 0%
where the time goes in v1:
time: 49.9 us; the launch traced here: 49.5 us
  waiting for transfers between devices  18.5 us (37%)
  blocking collectives  11.7 us (23%)
  starting transfers between devices  8.97 us (18%)
  Pallas kernels  8.43 us (17%)
  local copies, waits for them, and re-layouts  1.9 us (4%)
    all_to_all x1, blocking collectives, per_device(): lax.all_to_all(attended, 'seq', split_axis=0, concat_axis=0, tiled=True)  11.7 us
    all_to_all x1, waiting for transfers between devices, per_device(): lax.all_to_all(packed, 'seq', split_axis=0, concat_axis=0, tiled=True)  10.8 us
    all_to_all x1, starting transfers between devices, per_device(): lax.all_to_all(packed, 'seq', split_axis=0, concat_axis=0, tiled=True)  7.38 us
    pallas_call x1, Pallas kernels, per_device(): pl.pallas_call(functools.partial(attention_kernel, blk_count, tile_len),...  6.63 us
    ppermute x1, waiting for transfers between devices, gather_kept(): piece = lax.ppermute(kept_kv, 'blk', shift)  6.24 us
    unnamed x10, local copies, waits for them, and re-layouts  1.82 us
    ppermute x1, starting transfers between devices, gather_kept(): piece = lax.ppermute(kept_kv, 'blk', shift)  1.58 us
    ppermute x2, waiting for transfers between devices, gather_kept(): pieces += [piece, lax.ppermute(piece, 'blk', pair)]  1.45 us
  transfers between devices with their start and end apart: 4, of which 3 were waited for; matrix products, arithmetic and copies ran while one was open for 0% of the time, Pallas kernels for 0%

profile of v1, /device:TPU:0, one launch (start us, length us, event | category | flops | bytes accessed | tf_op | source)
XLA Modules:
  0.0 49.5 jit_solution(2706760102270998811)
XLA Ops:
  0.0 0.0 copy-start
  0.0 1.1 %copy-done = bf16[128,3072]{1,0:T(8,128)(2,1)S(1)} copy-done((bf16[128,3072]{1,0:T(8,128)(2,1)S(1)}, bf16[128,3072]{1,0:T(8,128)(2,1)}, u32[]{:S(2)}) %copy-start) | copy-done | bytes 786456
  1.1 1.0 %pack.1 = bf16[8,3,128,128]{3,2,1,0:T(8,128)(2,1)} custom-call(bf16[128,3072]{1,0:T(8,128)(2,1)S(1)} %copy-done), custom_call_target="tpu_custom_call" | custom-call | tf_op jit(solution)/shard_map/pack/pallas_call | solution.py:173
  2.2 0.0 copy-start.1
  2.2 7.4 %all-to-all-start = ((bf16[8,3,128,128]{3,2,1,0:T(8,128)(2,1)}), bf16[8,3,128,128]{3,2,1,0:T(8,128)(2,1)S(1)}, u32[]{:S(2)}, u32[]{:S(2)}) async-start(bf16[8,3,128,128]{3,2,1,0:T(8,128)(2,1)} %pack.1), calls=%async_computation | async-start | bytes 1572864 | tf_op jit(solution)/shard_map/all_to_all | solution.py:181
  9.5 0.0 copy-done.1
  9.5 1.6 %collective-permute-start.1 = (bf16[4,2,128,128]{3,2,1,0:T(8,128)(2,1)S(1)}, bf16[4,2,128,128]{3,2,1,0:T(8,128)(2,1)S(1)}, u32[]{:S(2)}, u32[]{:S(2)}) collective-permute-start(bf16[4,2,128,128]{3,2,1,0:T(8,128)(2,1)S(1)} %copy-done.1), channel_id=1, source_target_pairs={{0,2},{1,3},{2,0},{3,1},{4,6},{5,7},{6,4},{7,5},{8,10},{9,11},{10,... | collective-permute-start | bytes 786440 | tf_op jit(solution)/shard_map/ppermute | solution.py:154
  11.1 0.0 collective-permute-start
  11.1 6.2 %collective-permute-done.1.refs_2_ = bf16[4,2,128,128]{3,2,1,0:T(8,128)(2,1)S(1)} collective-permute-done((bf16[4,2,128,128]{3,2,1,0:T(8,128)(2,1)S(1)}, bf16[4,2,128,128]{3,2,1,0:T(8,128)(2,1)S(1)}, u32[]{:S(2)}, u32[]{:S(2)}) %collective-permute-start.1) | collective-permute-done | bytes 262176 | tf_op jit(solution)/shard_map/ppermute | solution.py:154
  17.4 0.0 collective-permute-start.2
  17.4 0.0 copy-start.2
  17.4 0.1 stack.23.place_ref
  17.5 0.0 collective-permute-done.refs_1_
  17.5 1.4 %collective-permute-done.2.refs_3_ = bf16[4,2,128,128]{3,2,1,0:T(8,128)(2,1)S(1)} collective-permute-done((bf16[4,2,128,128]{3,2,1,0:T(8,128)(2,1)S(1)}, bf16[4,2,128,128]{3,2,1,0:T(8,128)(2,1)S(1)}, u32[]{:S(2)}, u32[]{:S(2)}) %collective-permute-start.2) | collective-permute-done | bytes 262176 | tf_op jit(solution)/shard_map/ppermute | solution.py:157
  18.9 10.8 %all-to-all-done.span_hbm = bf16[8,3,128,128]{3,2,1,0:T(8,128)(2,1)S(1)} async-done(((bf16[8,3,128,128]{3,2,1,0:T(8,128)(2,1)}), bf16[8,3,128,128]{3,2,1,0:T(8,128)(2,1)S(1)}, u32[]{:S(2)}, u32[]{:S(2)}) %all-to-all-start) | async-done | bytes 786464 | tf_op jit(solution)/shard_map/all_to_all | solution.py:181
  29.7 0.0 copy-start.3
  29.7 0.0 copy-start.4
  29.7 0.0 copy-done.2
  29.7 0.7 %copy-done.3 = s32[32,2]{0,1:T(2,128)S(1)} copy-done((s32[32,2]{0,1:T(2,128)S(1)}, s32[32,2]{0,1:T(2,128)}, u32[]{:S(2)}) %copy-start.3) | copy-done | bytes 280
  30.4 0.0 copy-done.4
  30.4 6.6 %attention.1 = bf16[8,128,128]{2,1,0:T(8,128)(2,1)S(1)} custom-call(s32[5]{0:T(128)S(1)} %stack.23.place_ref, s32[2,32]{1,0:T(2,128)S(1)} %bitcast.8, s32[12,32]{1,0:T(8,128)S(1)} %bitcast.7, s32[32]{0:T(128)S(1)} %copy-done.4, bf16[8,3,128,128]{3,2,1,0:T(8,128)(2,1)S(1)} %all-to-all-done.span_hbm, bf16[4,2,128,128]{3,2,1,0:T(8,128)(2,1)S(1)} %copy-done.1, ...), custom_call_target="tpu_custom_call" | custom-call | tf_op jit(solution)/shard_map/attention/pallas_call | solution.py:185
  37.0 11.7 %all_to_all.10.parts_ref = bf16[8,128,128]{2,1,0:T(8,128)(2,1)S(1)} all-to-all(bf16[8,128,128]{2,1,0:T(8,128)(2,1)S(1)} %attention.1), channel_id=1, replica_groups=mesh['seq'=8,'blk'=4] {'seq'}, dimensions={0} | all-to-all | bytes 524288 | tf_op jit(solution)/shard_map/all_to_all | solution.py:201
  48.8 0.8 %unpack.1 = bf16[128,1024]{1,0:T(8,128)(2,1)} custom-call(bf16[8,128,128]{2,1,0:T(8,128)(2,1)S(1)} %all_to_all.10.parts_ref), custom_call_target="tpu_custom_call" | custom-call | tf_op jit(solution)/shard_map/unpack/pallas_call | solution.py:202
Async XLA Ops:
  0.0 1.1 %copy-start = (bf16[128,3072]{1,0:T(8,128)(2,1)S(1)}, bf16[128,3072]{1,0:T(8,128)(2,1)}, u32[]{:S(2)}) copy-start(bf16[128,3072]{1,0:T(8,128)(2,1)} %qkv_ref.1) | copy-start | bytes 2359300
  2.2 7.4 %copy-start.1 = (bf16[4,2,128,128]{3,2,1,0:T(8,128)(2,1)S(1)}, bf16[4,2,128,128]{3,2,1,0:T(8,128)(2,1)}, u32[]{:S(2)}) copy-start(bf16[4,2,128,128]{3,2,1,0:T(8,128)(2,1)} %refs_0_.1) | copy-start | bytes 786436
  2.2 27.6 %all-to-all-start = ((bf16[8,3,128,128]{3,2,1,0:T(8,128)(2,1)}), bf16[8,3,128,128]{3,2,1,0:T(8,128)(2,1)S(1)}, u32[]{:S(2)}, u32[]{:S(2)}) async-start(bf16[8,3,128,128]{3,2,1,0:T(8,128)(2,1)} %pack.1), calls=%async_computation | async-start | bytes 1572864 | tf_op jit(solution)/shard_map/all_to_all | solution.py:181
  9.5 7.8 %collective-permute-start.1 = (bf16[4,2,128,128]{3,2,1,0:T(8,128)(2,1)S(1)}, bf16[4,2,128,128]{3,2,1,0:T(8,128)(2,1)S(1)}, u32[]{:S(2)}, u32[]{:S(2)}) collective-permute-start(bf16[4,2,128,128]{3,2,1,0:T(8,128)(2,1)S(1)} %copy-done.1), channel_id=1, source_target_pairs={{0,2},{1,3},{2,0},{3,1},{4,6},{5,7},{6,4},{7,5},{8,10},{9,11},{10,... | collective-permute-start | bytes 786440 | tf_op jit(solution)/shard_map/ppermute | solution.py:154
  11.1 6.3 %collective-permute-start = (bf16[4,2,128,128]{3,2,1,0:T(8,128)(2,1)S(1)}, bf16[4,2,128,128]{3,2,1,0:T(8,128)(2,1)S(1)}, u32[]{:S(2)}, u32[]{:S(2)}) collective-permute-start(bf16[4,2,128,128]{3,2,1,0:T(8,128)(2,1)S(1)} %copy-done.1), channel_id=1, source_target_pairs={{0,1},{1,0},{2,3},{3,2},{4,5},{5,4},{6,7},{7,6},{8,9},{9,8},{10,11... | collective-permute-start | bytes 786440 | tf_op jit(solution)/shard_map/ppermute | solution.py:157
  17.4 1.5 %collective-permute-start.2 = (bf16[4,2,128,128]{3,2,1,0:T(8,128)(2,1)S(1)}, bf16[4,2,128,128]{3,2,1,0:T(8,128)(2,1)S(1)}, u32[]{:S(2)}, u32[]{:S(2)}) collective-permute-start(bf16[4,2,128,128]{3,2,1,0:T(8,128)(2,1)S(1)} %collective-permute-done.1.refs_2_), channel_id=1, source_target_pairs={{0,1},{1,0},{2,3},{3,2},{4,5},{5,4},{6,7},{7,6},{8,9},{9,8},{10,11... | collective-permute-start | bytes 786440 | tf_op jit(solution)/shard_map/ppermute | solution.py:157
  17.4 12.3 %copy-start.2 = (s32[32,12]{0,1:T(8,128)S(1)}, s32[32,12]{0,1:T(8,128)}, u32[]{:S(2)}) copy-start(s32[32,12]{0,1:T(8,128)} %param.8) | copy-start | bytes 4612
  29.7 0.7 %copy-start.3 = (s32[32,2]{0,1:T(2,128)S(1)}, s32[32,2]{0,1:T(2,128)}, u32[]{:S(2)}) copy-start(s32[32,2]{0,1:T(2,128)} %param.7) | copy-start | bytes 772
  29.7 0.7 %copy-start.4 = (s32[32]{0:T(128)S(1)}, s32[32]{0:T(128)}, u32[]{:S(2)}) copy-start(s32[32]{0:T(128)} %kept_count_ref.1) | copy-start | bytes 388

commit v2 on v1

v2 whole, which is shorter than its diff:
```python
import functools
import math

import jax
import jax.numpy as jnp
from jax import lax
from jax.experimental import pallas as pl
from jax.experimental.pallas import tpu as pltpu
from jax.sharding import PartitionSpec as P

HEAD_DIM = 128
MASKED_SCORE = -1e30
CHUNK = 6
VMEM_BYTES = 40 * 1024 * 1024


def pack_kernel(qkv_ref, out_ref):
    dests, groups, _, width = out_ref.shape
    for dest in range(dests):
        for group in range(groups):
            start = (group * dests + dest) * width
            out_ref[dest, group] = qkv_ref[:, start : start + width]


def unpack_kernel(parts_ref, out_ref):
    sources, _, width = parts_ref.shape
    for source in range(sources):
        out_ref[:, source * width : (source + 1) * width] = parts_ref[source]


def rows_of(place, tile_len):
    return pl.ds(pl.multiple_of(place * tile_len, tile_len), tile_len)


def attention_kernel(blk_count, tile_len, near_count, lists_ref, span, *refs):
    kepts, (out_ref, kept, scores) = refs[:blk_count], refs[blk_count:]
    sources, _, tok_rows, width = span.shape
    tiles_dev = tok_rows // tile_len
    kept_dev = kepts[0].shape[0]
    window = lists_ref.shape[0] - near_count - 1
    unroll = scores.shape[0]
    region = lax.axis_index("blk")

    for step in range(blk_count):
        kept[pl.ds((region ^ step) * kept_dev, kept_dev)] = kepts[step][...]

    factor = math.log2(math.e) / math.sqrt(HEAD_DIM)
    first = range(min(CHUNK, window))
    later = [range(i, min(i + CHUNK, window)) for i in range(CHUNK, window, CHUNK)]

    def stack(pieces):
        return jnp.concatenate(pieces, axis=0)

    def dot_keys(queries, keys):
        raw = lax.dot_general(
            queries, keys, (((1,), (1,)), ((), ())), preferred_element_type=jnp.float32
        )
        return [raw[:, i : i + tile_len] for i in range(0, raw.shape[1], tile_len)]

    def one_group(group, _):
        for head in range(width // HEAD_DIM):
            cols = slice(head * HEAD_DIM, (head + 1) * HEAD_DIM)
            items = []
            for u in range(unroll):
                local = group * unroll + u
                source, place = local // tiles_dev, local % tiles_dev
                tile = (source * blk_count + region) * tiles_dev + place
                near = []
                for c in range(near_count):
                    other = lists_ref[c, tile]
                    near.append(
                        (other // (tiles_dev * blk_count), rows_of(other % tiles_dev, tile_len))
                    )
                far = [lists_ref[near_count + w, tile] for w in range(window)]
                items.append((source, rows_of(place, tile_len), lists_ref[near_count + window, tile], near, far))

            def masked(raws, slots, count):
                return [
                    r if w == 0 else jnp.where(w < count, r, MASKED_SCORE)
                    for w, r in zip(slots, raws)
                ]

            def store(u, start, raws):
                for i, r in enumerate(raws):
                    scores[u, :, (start + i) * tile_len : (start + i + 1) * tile_len] = r

            tops = []
            for u, (source, rows, count, near, far) in enumerate(items):
                keys = [span[s, 1, r, cols] for s, r in near]
                keys += [kept[far[w], 0, :, cols] for w in first]
                raws = dot_keys(span[source, 0, rows, cols], stack(keys))
                raws = raws[:near_count] + masked(raws[near_count:], first, count)
                store(u, 0, raws)
                tops.append(functools.reduce(jnp.maximum, raws))
            for u, (source, rows, count, near, far) in enumerate(items):
                for slots in later:

                    def more(top, u=u, slots=slots):
                        keys = [kept[items[u][4][w], 0, :, cols] for w in slots]
                        raws = dot_keys(span[items[u][0], 0, items[u][1], cols], stack(keys))
                        raws = masked(raws, slots, items[u][2])
                        store(u, near_count + slots[0], raws)
                        return functools.reduce(jnp.maximum, [top, *raws])

                    tops[u] = lax.cond(slots[0] < count, more, lambda top: top, tops[u])
            tops = [jnp.max(top, axis=1, keepdims=True) * factor for top in tops]

            def weigh(u, start, values):
                weights = []
                for i in range(len(values)):
                    r = scores[u, :, (start + i) * tile_len : (start + i + 1) * tile_len]
                    weights.append(jnp.exp2(r * factor - tops[u]))
                rounded = jnp.concatenate([w.astype(jnp.bfloat16) for w in weights], axis=1)
                mixed = jnp.dot(rounded, stack(values), preferred_element_type=jnp.float32)
                return functools.reduce(jnp.add, weights), mixed

            sums = []
            for u, (source, rows, count, near, far) in enumerate(items):
                values = [span[s, 2, r, cols] for s, r in near]
                values += [kept[far[w], 1, :, cols] for w in first]
                sums.append(weigh(u, 0, values))
            for u, (source, rows, count, near, far) in enumerate(items):
                for slots in later:

                    def add(carry, u=u, slots=slots):
                        values = [kept[items[u][4][w], 1, :, cols] for w in slots]
                        total, mixed = weigh(u, near_count + slots[0], values)
                        return carry[0] + total, carry[1] + mixed

                    sums[u] = lax.cond(slots[0] < count, add, lambda carry: carry, sums[u])
            for u, (source, rows, count, near, far) in enumerate(items):
                total = jnp.sum(sums[u][0], axis=1, keepdims=True)
                out_ref[source, rows, cols] = (sums[u][1] / total).astype(jnp.bfloat16)
        return 0

    lax.fori_loop(0, sources * tiles_dev // unroll, one_group, 0)


def swap(array, axis, step):
    if step == 0:
        return array
    count = lax.axis_size(axis)
    return lax.ppermute(array, axis, [(i, i ^ step) for i in range(count)])


def per_device(qkv, kept_kv, cur_list, kept_list, kept_count):
    seq_count = lax.axis_size("seq")
    blk_count = lax.axis_size("blk")
    tok_rows = qkv.shape[0]
    kept_dev, _, tile_len, width = kept_kv.shape
    dtype = qkv.dtype
    tiles = seq_count * (tok_rows // tile_len)
    unroll = math.gcd(tiles, 8)
    near_count, window = cur_list.shape[1], kept_list.shape[1]
    vmem = pl.BlockSpec(memory_space=pltpu.VMEM)
    smem = pl.BlockSpec(memory_space=pltpu.SMEM)
    params = pltpu.CompilerParams(vmem_limit_bytes=VMEM_BYTES)

    lists = jnp.concatenate([cur_list.T, kept_list.T, kept_count[None]], axis=0)
    kepts = [swap(kept_kv, "blk", step) for step in range(blk_count)]
    packed = pl.pallas_call(
        pack_kernel,
        out_shape=jax.ShapeDtypeStruct((seq_count, 3, tok_rows, width), dtype),
        in_specs=[vmem],
        out_specs=vmem,
        compiler_params=params,
        name="pack",
    )(qkv)
    span = lax.all_to_all(packed, "seq", split_axis=0, concat_axis=0, tiled=True)

    attended = pl.pallas_call(
        functools.partial(attention_kernel, blk_count, tile_len, near_count),
        out_shape=jax.ShapeDtypeStruct((seq_count, tok_rows, width), dtype),
        in_specs=[smem] + [vmem] * (1 + blk_count),
        out_specs=vmem,
        scratch_shapes=[
            pltpu.VMEM((blk_count * kept_dev, 2, tile_len, width), dtype),
            pltpu.VMEM((unroll, tile_len, (near_count + window) * tile_len), jnp.float32),
        ],
        compiler_params=params,
        name="attention",
    )(lists, span, *kepts)

    returned = lax.all_to_all(attended, "seq", split_axis=0, concat_axis=0, tiled=True)
    return pl.pallas_call(
        unpack_kernel,
        out_shape=jax.ShapeDtypeStruct((tok_rows, seq_count * width), dtype),
        in_specs=[vmem],
        out_specs=vmem,
        compiler_params=params,
        name="unpack",
    )(returned)


def solution(mesh):
    placed = (P(("seq", "blk"), None), P("blk", None, None, "seq"), P(), P(), P())
    return jax.shard_map(
        per_device, mesh=mesh, in_specs=placed, out_specs=P(("seq", "blk"), None), check_vma=False
    )
```

time: 49.9 us -> 46.9 us (0.940)
  Pallas kernels: 8.43 us -> 5.93 us
  waiting for transfers between devices: 18.5 us -> 17.5 us
    all_to_all x1, waiting for transfers between devices: 10.8 us -> 6.21 us  [per_device(): lax.all_to_all(packed, 'seq', split_axis=0, concat_axis=0, tiled=True)]
    ppermute x3, waiting for transfers between devices: 7.69 us -> 11.3 us  [swap(): return lax.ppermute(array, axis, [(i, i ^ step) for i in range(count)])]
    pallas_call x1, Pallas kernels: 6.63 us -> 4.13 us  [per_device(): pl.pallas_call(functools.partial(attention_kernel, blk_count, tile_len, n...]
where the time goes in v2:
time: 46.9 us; the launch traced here: 46.2 us
  waiting for transfers between devices  17.5 us (37%)
  blocking collectives  11.6 us (25%)
  starting transfers between devices  9.32 us (20%)
  Pallas kernels  5.93 us (13%)
  local copies, waits for them, and re-layouts  1.82 us (4%)
    all_to_all x1, blocking collectives, per_device(): lax.all_to_all(attended, 'seq', split_axis=0, concat_axis=0, tiled=True)  11.6 us
    ppermute x3, waiting for transfers between devices, swap(): return lax.ppermute(array, axis, [(i, i ^ step) for i in range(count)])  11.3 us
    all_to_all x1, starting transfers between devices, per_device(): lax.all_to_all(packed, 'seq', split_axis=0, concat_axis=0, tiled=True)  7.38 us
    all_to_all x1, waiting for transfers between devices, per_device(): lax.all_to_all(packed, 'seq', split_axis=0, concat_axis=0, tiled=True)  6.21 us
    pallas_call x1, Pallas kernels, per_device(): pl.pallas_call(functools.partial(attention_kernel, blk_count, tile_len, n...  4.13 us
    ppermute x3, starting transfers between devices, swap(): return lax.ppermute(array, axis, [(i, i ^ step) for i in range(count)])  1.93 us
    unnamed x10, local copies, waits for them, and re-layouts  1.82 us
    pallas_call x1, Pallas kernels, per_device(): pl.pallas_call(pack_kernel, out_shape=jax.ShapeDtypeStruct((seq_count, 3,...  1.02 us
  transfers between devices with their start and end apart: 4, of which 3 were waited for; matrix products, arithmetic and copies ran while one was open for 0% of the time, Pallas kernels for 0%

profile of v2, /device:TPU:0, one launch (start us, length us, event | category | flops | bytes accessed | tf_op | source)
XLA Modules:
  0.0 46.2 jit_solution(11578021563462692593)
XLA Ops:
  0.0 0.0 copy-start
  0.0 1.1 %copy-done = bf16[128,3072]{1,0:T(8,128)(2,1)S(1)} copy-done((bf16[128,3072]{1,0:T(8,128)(2,1)S(1)}, bf16[128,3072]{1,0:T(8,128)(2,1)}, u32[]{:S(2)}) %copy-start) | copy-done | bytes 786456
  1.1 1.0 %pack.1 = bf16[8,3,128,128]{3,2,1,0:T(8,128)(2,1)} custom-call(bf16[128,3072]{1,0:T(8,128)(2,1)S(1)} %copy-done), custom_call_target="tpu_custom_call" | custom-call | tf_op jit(solution)/shard_map/pack/pallas_call | solution.py:161
  2.2 0.0 copy-start.1
  2.2 0.0 copy-start.2
  2.2 7.4 %all-to-all-start = ((bf16[8,3,128,128]{3,2,1,0:T(8,128)(2,1)}), bf16[8,3,128,128]{3,2,1,0:T(8,128)(2,1)S(1)}, u32[]{:S(2)}, u32[]{:S(2)}) async-start(bf16[8,3,128,128]{3,2,1,0:T(8,128)(2,1)} %pack.1), calls=%async_computation | async-start | bytes 1572864 | tf_op jit(solution)/shard_map/all_to_all | solution.py:169
  9.5 0.0 copy-done.1
  9.6 0.1 collective-permute-start
  9.6 1.6 %collective-permute-start.1 = (bf16[4,2,128,128]{3,2,1,0:T(8,128)(2,1)S(1)}, bf16[4,2,128,128]{3,2,1,0:T(8,128)(2,1)S(1)}, u32[]{:S(2)}, u32[]{:S(2)}) collective-permute-start(bf16[4,2,128,128]{3,2,1,0:T(8,128)(2,1)S(1)} %copy-done.1), channel_id=1, source_target_pairs={{0,2},{1,3},{2,0},{3,1},{4,6},{5,7},{6,4},{7,5},{8,10},{9,11},{10,... | collective-permute-start | bytes 786440 | tf_op jit(solution)/shard_map/ppermute | solution.py:143
  11.2 0.3 collective-permute-start.2
  11.5 0.0 copy-start.3
  11.5 0.0 copy-start.4
  11.5 0.0 copy-done.2
  11.5 0.7 %copy-done.3 = s32[32,2]{0,1:T(2,128)S(1)} copy-done((s32[32,2]{0,1:T(2,128)S(1)}, s32[32,2]{0,1:T(2,128)}, u32[]{:S(2)}) %copy-start.3) | copy-done | bytes 280
  12.2 0.0 copy-done.4
  12.2 0.0 collective-permute-done.refs_1_
  12.2 6.6 %collective-permute-done.1.refs_2_ = bf16[4,2,128,128]{3,2,1,0:T(8,128)(2,1)S(1)} collective-permute-done((bf16[4,2,128,128]{3,2,1,0:T(8,128)(2,1)S(1)}, bf16[4,2,128,128]{3,2,1,0:T(8,128)(2,1)S(1)}, u32[]{:S(2)}, u32[]{:S(2)}) %collective-permute-start.1) | collective-permute-done | bytes 262176 | tf_op jit(solution)/shard_map/ppermute | solution.py:143
  18.8 4.7 %collective-permute-done.2.refs_3_ = bf16[4,2,128,128]{3,2,1,0:T(8,128)(2,1)S(1)} collective-permute-done((bf16[4,2,128,128]{3,2,1,0:T(8,128)(2,1)S(1)}, bf16[4,2,128,128]{3,2,1,0:T(8,128)(2,1)S(1)}, u32[]{:S(2)}, u32[]{:S(2)}) %collective-permute-start.2) | collective-permute-done | bytes 262176 | tf_op jit(solution)/shard_map/ppermute | solution.py:143
  23.5 6.2 %all-to-all-done.span = bf16[8,3,128,128]{3,2,1,0:T(8,128)(2,1)S(1)} async-done(((bf16[8,3,128,128]{3,2,1,0:T(8,128)(2,1)}), bf16[8,3,128,128]{3,2,1,0:T(8,128)(2,1)S(1)}, u32[]{:S(2)}, u32[]{:S(2)}) %all-to-all-start) | async-done | bytes 786464 | tf_op jit(solution)/shard_map/all_to_all | solution.py:169
  29.7 4.1 %attention.1 = bf16[8,128,128]{2,1,0:T(8,128)(2,1)S(1)} custom-call(s32[15,32]{1,0:T(8,128)S(1)} %pad_add_fusion.lists_ref, bf16[8,3,128,128]{3,2,1,0:T(8,128)(2,1)S(1)} %all-to-all-done.span, bf16[4,2,128,128]{3,2,1,0:T(8,128)(2,1)S(1)} %copy-done.1, bf16[4,2,128,128]{3,2,1,0:T(8,128)(2,1)S(1)} %collective-permute-done.refs_1_, ...), custom_call_target="tpu_custom_call" | custom-call | tf_op jit(solution)/shard_map/attention/pallas_call | solution.py:171
  33.9 11.6 %all_to_all.10.parts_ref = bf16[8,128,128]{2,1,0:T(8,128)(2,1)S(1)} all-to-all(bf16[8,128,128]{2,1,0:T(8,128)(2,1)S(1)} %attention.1), channel_id=1, replica_groups=mesh['seq'=8,'blk'=4] {'seq'}, dimensions={0} | all-to-all | bytes 524288 | tf_op jit(solution)/shard_map/all_to_all | solution.py:184
  45.4 0.8 %unpack.1 = bf16[128,1024]{1,0:T(8,128)(2,1)} custom-call(bf16[8,128,128]{2,1,0:T(8,128)(2,1)S(1)} %all_to_all.10.parts_ref), custom_call_target="tpu_custom_call" | custom-call | tf_op jit(solution)/shard_map/unpack/pallas_call | solution.py:185
  (1 shorter events, 0.0 us)
Async XLA Ops:
  0.0 1.1 %copy-start = (bf16[128,3072]{1,0:T(8,128)(2,1)S(1)}, bf16[128,3072]{1,0:T(8,128)(2,1)}, u32[]{:S(2)}) copy-start(bf16[128,3072]{1,0:T(8,128)(2,1)} %qkv_ref.1) | copy-start | bytes 2359300
  2.2 7.4 %copy-start.1 = (bf16[4,2,128,128]{3,2,1,0:T(8,128)(2,1)S(1)}, bf16[4,2,128,128]{3,2,1,0:T(8,128)(2,1)}, u32[]{:S(2)}) copy-start(bf16[4,2,128,128]{3,2,1,0:T(8,128)(2,1)} %refs_0_.1) | copy-start | bytes 786436
  2.2 9.3 %copy-start.2 = (s32[32,12]{0,1:T(8,128)S(1)}, s32[32,12]{0,1:T(8,128)}, u32[]{:S(2)}) copy-start(s32[32,12]{0,1:T(8,128)} %param.8) | copy-start | bytes 4612
  2.2 27.6 %all-to-all-start = ((bf16[8,3,128,128]{3,2,1,0:T(8,128)(2,1)}), bf16[8,3,128,128]{3,2,1,0:T(8,128)(2,1)S(1)}, u32[]{:S(2)}, u32[]{:S(2)}) async-start(bf16[8,3,128,128]{3,2,1,0:T(8,128)(2,1)} %pack.1), calls=%async_computation | async-start | bytes 1572864 | tf_op jit(solution)/shard_map/all_to_all | solution.py:169
  9.6 2.6 %collective-permute-start = (bf16[4,2,128,128]{3,2,1,0:T(8,128)(2,1)S(1)}, bf16[4,2,128,128]{3,2,1,0:T(8,128)(2,1)S(1)}, u32[]{:S(2)}, u32[]{:S(2)}) collective-permute-start(bf16[4,2,128,128]{3,2,1,0:T(8,128)(2,1)S(1)} %copy-done.1), channel_id=1, source_target_pairs={{0,1},{1,0},{2,3},{3,2},{4,5},{5,4},{6,7},{7,6},{8,9},{9,8},{10,11... | collective-permute-start | bytes 786440 | tf_op jit(solution)/shard_map/ppermute | solution.py:143
  9.6 9.2 %collective-permute-start.1 = (bf16[4,2,128,128]{3,2,1,0:T(8,128)(2,1)S(1)}, bf16[4,2,128,128]{3,2,1,0:T(8,128)(2,1)S(1)}, u32[]{:S(2)}, u32[]{:S(2)}) collective-permute-start(bf16[4,2,128,128]{3,2,1,0:T(8,128)(2,1)S(1)} %copy-done.1), channel_id=1, source_target_pairs={{0,2},{1,3},{2,0},{3,1},{4,6},{5,7},{6,4},{7,5},{8,10},{9,11},{10,... | collective-permute-start | bytes 786440 | tf_op jit(solution)/shard_map/ppermute | solution.py:143
  11.2 12.3 %collective-permute-start.2 = (bf16[4,2,128,128]{3,2,1,0:T(8,128)(2,1)S(1)}, bf16[4,2,128,128]{3,2,1,0:T(8,128)(2,1)S(1)}, u32[]{:S(2)}, u32[]{:S(2)}) collective-permute-start(bf16[4,2,128,128]{3,2,1,0:T(8,128)(2,1)S(1)} %copy-done.1), channel_id=1, source_target_pairs={{0,3},{1,2},{2,1},{3,0},{4,7},{5,6},{6,5},{7,4},{8,11},{9,10},{10,... | collective-permute-start | bytes 786440 | tf_op jit(solution)/shard_map/ppermute | solution.py:143
  11.5 0.7 %copy-start.3 = (s32[32,2]{0,1:T(2,128)S(1)}, s32[32,2]{0,1:T(2,128)}, u32[]{:S(2)}) copy-start(s32[32,2]{0,1:T(2,128)} %param.7) | copy-start | bytes 772
  11.5 0.7 %copy-start.4 = (s32[32]{0:T(128)S(1)}, s32[32]{0:T(128)}, u32[]{:S(2)}) copy-start(s32[32]{0:T(128)} %param.9) | copy-start | bytes 388

commit v3 on v2

--- a/solution.py
+++ b/solution.py
@@ -11,15 +11,31 @@
 HEAD_DIM = 128
 MASKED_SCORE = -1e30
 CHUNK = 6
+EARLY = 4
+COLLECT_FLOPS = 10**10
 VMEM_BYTES = 40 * 1024 * 1024
 
 
-def pack_kernel(qkv_ref, out_ref):
-    dests, groups, _, width = out_ref.shape
-    for dest in range(dests):
+def pack_kernel(steps, sources, qkv_ref, *refs):
+    outs = refs[len(refs) - len(steps) :]
+    groups, _, width = outs[0].shape
+    me = lax.axis_index("seq")
+    for step, out in zip(steps, outs):
         for group in range(groups):
-            start = (group * dests + dest) * width
-            out_ref[dest, group] = qkv_ref[:, start : start + width]
+            start = pl.multiple_of((group * sources + (me ^ step)) * width, width)
+            out[group] = qkv_ref[:, pl.ds(start, width)]
+
+
+def merge_kernel(count, *refs):
+    for i in range(count):
+        refs[-1][i] = refs[i][...]
+
+
+def collect_kernel(*refs):
+    spans, out_ref = refs[:-1], refs[-1]
+    me = lax.axis_index("seq")
+    for step, span in enumerate(spans):
+        out_ref[me ^ step] = span[...]
 
 
 def unpack_kernel(parts_ref, out_ref):
@@ -33,16 +49,19 @@
 
 
 def attention_kernel(blk_count, tile_len, near_count, lists_ref, span, *refs):
-    kepts, (out_ref, kept, scores) = refs[:blk_count], refs[blk_count:]
+    kepts, (out_ref, kept, scores) = refs[:-3], refs[-3:]
     sources, _, tok_rows, width = span.shape
     tiles_dev = tok_rows // tile_len
-    kept_dev = kepts[0].shape[0]
+    kept_dev = kept.shape[0] // blk_count
     window = lists_ref.shape[0] - near_count - 1
     unroll = scores.shape[0]
     region = lax.axis_index("blk")
 
-    for step in range(blk_count):
-        kept[pl.ds((region ^ step) * kept_dev, kept_dev)] = kepts[step][...]
+    pieces = []
+    for ref in kepts:
+        pieces += [ref] if len(ref.shape) == 4 else [ref.at[i] for i in range(ref.shape[0])]
+    for piece, step in zip(pieces, [*range(0, blk_count, 2), *range(1, blk_count, 2)]):
+        kept[pl.ds((region ^ step) * kept_dev, kept_dev)] = piece[...]
 
     factor = math.log2(math.e) / math.sqrt(HEAD_DIM)
     first = range(min(CHUNK, window))
@@ -143,6 +162,11 @@
     return lax.ppermute(array, axis, [(i, i ^ step) for i in range(count)])
 
 
+def sending_order(count):
+    near, far = list(range(1, count // 2)), list(range(count // 2, count))
+    return near[:1] + far[:1] + near[1:2] + far[1:] + near[2:]
+
+
 def per_device(qkv, kept_kv, cur_list, kept_list, kept_count):
     seq_count = lax.axis_size("seq")
     blk_count = lax.axis_size("blk")
@@ -153,25 +177,50 @@
     unroll = math.gcd(tiles, 8)
     near_count, window = cur_list.shape[1], kept_list.shape[1]
     vmem = pl.BlockSpec(memory_space=pltpu.VMEM)
+    anywhere = pl.BlockSpec(memory_space=pl.ANY)
     smem = pl.BlockSpec(memory_space=pltpu.SMEM)
     params = pltpu.CompilerParams(vmem_limit_bytes=VMEM_BYTES)
 
     lists = jnp.concatenate([cur_list.T, kept_list.T, kept_count[None]], axis=0)
-    kepts = [swap(kept_kv, "blk", step) for step in range(blk_count)]
-    packed = pl.pallas_call(
-        pack_kernel,
+    kepts = [swap(kept_kv, "blk", step) for step in range(0, blk_count, 2)]
+    order = sending_order(seq_count)
+    spans = [None] * seq_count
+    for steps, before in (([0, *order[:EARLY]], []), (order[EARLY:], kepts[1:])):
+        packed = pl.pallas_call(
+            functools.partial(pack_kernel, steps, seq_count),
+            out_shape=[jax.ShapeDtypeStruct((3, tok_rows, width), dtype)] * len(steps),
+            in_specs=[vmem] + [anywhere] * len(before),
+            out_specs=[vmem] * len(steps),
+            compiler_params=params,
+            name="pack",
+        )(qkv, *before)
+        for step, piece in zip(steps, packed):
+            spans[step] = swap(piece, "seq", step)
+    after = []
+    merged = pl.pallas_call(
+        functools.partial(merge_kernel, len(kepts)),
+        out_shape=jax.ShapeDtypeStruct((len(kepts), *kept_kv.shape), dtype),
+        in_specs=[vmem] * len(kepts) + [anywhere] * len(after),
+        out_specs=vmem,
+        compiler_params=params,
+        name="merge",
+    )(*kepts, *after)
+    kepts.append(swap(merged, "blk", 1))
+
+    span = pl.pallas_call(
+        collect_kernel,
         out_shape=jax.ShapeDtypeStruct((seq_count, 3, tok_rows, width), dtype),
-        in_specs=[vmem],
-        out_specs=vmem,
-        compiler_params=params,
-        name="pack",
-    )(qkv)
-    span = lax.all_to_all(packed, "seq", split_axis=0, concat_axis=0, tiled=True)
+        in_specs=[vmem] * seq_count,
+        out_specs=vmem,
+        compiler_params=params,
+        cost_estimate=pl.CostEstimate(flops=COLLECT_FLOPS, bytes_accessed=0, transcendentals=0),
+        name="collect",
+    )(*spans)
 
     attended = pl.pallas_call(
         functools.partial(attention_kernel, blk_count, tile_len, near_count),
         out_shape=jax.ShapeDtypeStruct((seq_count, tok_rows, width), dtype),
-        in_specs=[smem] + [vmem] * (1 + blk_count),
+        in_specs=[smem] + [vmem] * (1 + len(kepts)),
         out_specs=vmem,
         scratch_shapes=[
             pltpu.VMEM((blk_count * kept_dev, 2, tile_len, width), dtype),

time: 46.9 us -> 42.6 us (0.908)
  waiting for transfers between devices: 17.5 us -> 5.87 us
  starting transfers between devices: 9.32 us -> 14.8 us
  blocking collectives: 11.6 us -> 15.7 us
  Pallas kernels: 5.93 us -> 3.94 us
    ppermute x3 -> x9, starting transfers between devices: 1.93 us -> 14.8 us  [swap(): return lax.ppermute(array, axis, [(i, i ^ step) for i in range(count)])]
    all_to_all x1 -> x0, starting transfers between devices: 7.38 us -> none  [per_device(): lax.all_to_all(packed, 'seq', split_axis=0, concat_axis=0, tiled=True)]
    all_to_all x1 -> x0, waiting for transfers between devices: 6.21 us -> none  [per_device(): lax.all_to_all(packed, 'seq', split_axis=0, concat_axis=0, tiled=True)]
    ppermute x3 -> x9, waiting for transfers between devices: 11.3 us -> 5.87 us  [swap(): return lax.ppermute(array, axis, [(i, i ^ step) for i in range(count)])]
    all_to_all x1, blocking collectives: 11.6 us -> 15.7 us  [per_device(): lax.all_to_all(attended, 'seq', split_axis=0, concat_axis=0, tiled=True)]
    pallas_call x1, Pallas kernels: 4.13 us -> 2.86 us  [per_device(): pl.pallas_call(functools.partial(attention_kernel, blk_count, tile_len, n...]
    pallas_call x1 -> x4, Pallas kernels: 1.02 us -> 0.3 us  [the longest x2 0.2 us: per_device(): pl.pallas_call(functools.partial(pack_kernel, steps, seq_count), out_shap...]
  transfers between devices with their start and end apart: 4 -> 9, of which waited for: 3 -> 3; matrix products, arithmetic and copies ran while one was open for 0% -> 0% of each run, Pallas kernels for 0% -> 1%
where the time goes in v3:
time: 42.6 us; the launch traced here: 42.2 us
  blocking collectives  15.7 us (37%)
  starting transfers between devices  14.8 us (35%)
  waiting for transfers between devices  5.87 us (14%)
  Pallas kernels  3.94 us (9%)
  local copies, waits for them, and re-layouts  1.82 us (4%)
    all_to_all x1, blocking collectives, per_device(): lax.all_to_all(attended, 'seq', split_axis=0, concat_axis=0, tiled=True)  15.7 us
    ppermute x9, starting transfers between devices, swap(): return lax.ppermute(array, axis, [(i, i ^ step) for i in range(count)])  14.8 us
    ppermute x9, waiting for transfers between devices, swap(): return lax.ppermute(array, axis, [(i, i ^ step) for i in range(count)])  5.87 us
    pallas_call x1, Pallas kernels, per_device(): pl.pallas_call(functools.partial(attention_kernel, blk_count, tile_len, n...  2.86 us
    unnamed x10, local copies, waits for them, and re-layouts  1.82 us
  transfers between devices with their start and end apart: 9, of which 3 were waited for; matrix products, arithmetic and copies ran while one was open for 0% of the time, Pallas kernels for 1%

profile of v3, /device:TPU:0, one launch (start us, length us, event | category | flops | bytes accessed | tf_op | source)
XLA Modules:
  0.0 42.2 jit_solution(11020245315575879102)
XLA Ops:
  0.0 3.0 %collective-permute-start.2 = (bf16[4,2,128,128]{3,2,1,0:T(8,128)(2,1)}, bf16[4,2,128,128]{3,2,1,0:T(8,128)(2,1)S(1)}, u32[]{:S(2)}, u32[]{:S(2)}) collective-permute-start(bf16[4,2,128,128]{3,2,1,0:T(8,128)(2,1)} %refs_0_.3), channel_id=1, source_target_pairs={{0,2},{1,3},{2,0},{3,1},{4,6},{5,7},{6,4},{7,5},{8,10},{9,11},{10,... | collective-permute-start | bytes 786440 | tf_op jit(solution)/shard_map/ppermute | solution.py:162
  3.0 0.0 copy-start
  3.0 1.1 %copy-done = bf16[128,3072]{1,0:T(8,128)(2,1)S(1)} copy-done((bf16[128,3072]{1,0:T(8,128)(2,1)S(1)}, bf16[128,3072]{1,0:T(8,128)(2,1)}, u32[]{:S(2)}) %copy-start) | copy-done | bytes 786456
  4.1 0.1 pack.2
  4.2 1.6 %collective-permute-start = (bf16[3,128,128]{2,1,0:T(8,128)(2,1)S(1)}, bf16[3,128,128]{2,1,0:T(8,128)(2,1)S(1)}, u32[]{:S(2)}, u32[]{:S(2)}) collective-permute-start(bf16[3,128,128]{2,1,0:T(8,128)(2,1)S(1)} %get-tuple-element.14), channel_id=1, source_target_pairs={{0,4},{4,0},{8,12},{12,8},{16,20},{20,16},{24,28},{28,24},{1,5},{5... | collective-permute-start | bytes 294920 | tf_op jit(solution)/shard_map/ppermute | solution.py:162
  5.8 1.6 %collective-permute-start.1 = (bf16[3,128,128]{2,1,0:T(8,128)(2,1)S(1)}, bf16[3,128,128]{2,1,0:T(8,128)(2,1)S(1)}, u32[]{:S(2)}, u32[]{:S(2)}) collective-permute-start(bf16[3,128,128]{2,1,0:T(8,128)(2,1)S(1)} %get-tuple-element.15), channel_id=1, source_target_pairs={{0,8},{4,12},{8,0},{12,4},{16,24},{20,28},{24,16},{28,20},{1,9},{5... | collective-permute-start | bytes 294920 | tf_op jit(solution)/shard_map/ppermute | solution.py:162
  7.4 2.6 %collective-permute-start.4 = (bf16[3,128,128]{2,1,0:T(8,128)(2,1)S(1)}, bf16[3,128,128]{2,1,0:T(8,128)(2,1)S(1)}, u32[]{:S(2)}, u32[]{:S(2)}) collective-permute-start(bf16[3,128,128]{2,1,0:T(8,128)(2,1)S(1)} %get-tuple-element.17), channel_id=1, source_target_pairs={{0,16},{4,20},{8,24},{12,28},{16,0},{20,4},{24,8},{28,12},{1,17},{... | collective-permute-start | bytes 294920 | tf_op jit(solution)/shard_map/ppermute | solution.py:162
  10.0 0.0 copy-start.1
  10.0 0.3 collective-permute-start.5
  10.3 0.0 collective-permute-done.2.refs_0_.refs_1_
  10.3 0.1 pack.3
  10.3 0.0 copy-start.2
  10.4 2.0 %collective-permute-start.3 = (bf16[3,128,128]{2,1,0:T(8,128)(2,1)S(1)}, bf16[3,128,128]{2,1,0:T(8,128)(2,1)S(1)}, u32[]{:S(2)}, u32[]{:S(2)}) collective-permute-start(bf16[3,128,128]{2,1,0:T(8,128)(2,1)S(1)} %get-tuple-element.16), channel_id=1, source_target_pairs={{0,12},{4,8},{8,4},{12,0},{16,28},{20,24},{24,20},{28,16},{1,13},{... | collective-permute-start | bytes 294920 | tf_op jit(solution)/shard_map/ppermute | solution.py:162
  12.4 0.0 collective-permute-done.refs_1_
  12.4 3.0 %collective-permute-start.6 = (bf16[3,128,128]{2,1,0:T(8,128)(2,1)S(1)}, bf16[3,128,128]{2,1,0:T(8,128)(2,1)S(1)}, u32[]{:S(2)}, u32[]{:S(2)}) collective-permute-start(bf16[3,128,128]{2,1,0:T(8,128)(2,1)S(1)} %get-tuple-element.19), channel_id=1, source_target_pairs={{0,24},{4,28},{8,16},{12,20},{16,8},{20,12},{24,0},{28,4},{1,25},{... | collective-permute-start | bytes 294920 | tf_op jit(solution)/shard_map/ppermute | solution.py:162
  15.4 0.0 collective-permute-done.1.refs_2_
  15.4 0.8 %collective-permute-start.7 = (bf16[3,128,128]{2,1,0:T(8,128)(2,1)S(1)}, bf16[3,128,128]{2,1,0:T(8,128)(2,1)S(1)}, u32[]{:S(2)}, u32[]{:S(2)}) collective-permute-start(bf16[3,128,128]{2,1,0:T(8,128)(2,1)S(1)} %get-tuple-element.20), channel_id=1, source_target_pairs={{0,28},{4,24},{8,20},{12,16},{16,12},{20,8},{24,4},{28,0},{1,29},{... | collective-permute-start | bytes 294920 | tf_op jit(solution)/shard_map/ppermute | solution.py:162
  16.2 0.0 copy-start.3
  16.2 0.0 copy-start.4
  16.2 0.0 copy-done.2
  16.2 0.7 %copy-done.3 = s32[32,2]{0,1:T(2,128)S(1)} copy-done((s32[32,2]{0,1:T(2,128)S(1)}, s32[32,2]{0,1:T(2,128)}, u32[]{:S(2)}) %copy-start.3) | copy-done | bytes 280
  16.9 0.0 copy-done.4
  16.9 0.0 copy-done.1
  16.9 0.7 %collective-permute-done.4.refs_4_ = bf16[3,128,128]{2,1,0:T(8,128)(2,1)S(1)} collective-permute-done((bf16[3,128,128]{2,1,0:T(8,128)(2,1)S(1)}, bf16[3,128,128]{2,1,0:T(8,128)(2,1)S(1)}, u32[]{:S(2)}, u32[]{:S(2)}) %collective-permute-start.4) | collective-permute-done | bytes 98336 | tf_op jit(solution)/shard_map/ppermute | solution.py:162
  17.6 0.0 collective-permute-start.8
  17.6 4.0 %collective-permute-done.5.refs_5_ = bf16[3,128,128]{2,1,0:T(8,128)(2,1)S(1)} collective-permute-done((bf16[3,128,128]{2,1,0:T(8,128)(2,1)S(1)}, bf16[3,128,128]{2,1,0:T(8,128)(2,1)S(1)}, u32[]{:S(2)}, u32[]{:S(2)}) %collective-permute-start.5) | collective-permute-done | bytes 98336 | tf_op jit(solution)/shard_map/ppermute | solution.py:162
  21.6 0.0 collective-permute-done.3.refs_3_
  21.6 0.0 collective-permute-done.6.refs_6_
  21.6 1.2 %collective-permute-done.7.refs_7_ = bf16[3,128,128]{2,1,0:T(8,128)(2,1)S(1)} collective-permute-done((bf16[3,128,128]{2,1,0:T(8,128)(2,1)S(1)}, bf16[3,128,128]{2,1,0:T(8,128)(2,1)S(1)}, u32[]{:S(2)}, u32[]{:S(2)}) %collective-permute-start.7) | collective-permute-done | bytes 98336 | tf_op jit(solution)/shard_map/ppermute | solution.py:162
  22.8 0.1 collect.1.span
  22.9 0.0 collective-permute-done.8.refs_2_
  22.9 2.9 %attention.1 = bf16[8,128,128]{2,1,0:T(8,128)(2,1)S(1)} custom-call(s32[15,32]{1,0:T(8,128)S(1)} %pad_add_fusion.lists_ref, bf16[8,3,128,128]{3,2,1,0:T(8,128)(2,1)S(1)} %collect.1.span, bf16[4,2,128,128]{3,2,1,0:T(8,128)(2,1)S(1)} %copy-done.1, bf16[4,2,128,128]{3,2,1,0:T(8,128)(2,1)S(1)} %collective-permute-done.2.refs_0_.refs_1_, ...), custom_call_target="tpu_custom_call" | custom-call | tf_op jit(solution)/shard_map/attention/pallas_call | solution.py:220
  25.7 15.7 %all_to_all.5.parts_ref = bf16[8,128,128]{2,1,0:T(8,128)(2,1)S(1)} all-to-all(bf16[8,128,128]{2,1,0:T(8,128)(2,1)S(1)} %attention.1), channel_id=1, replica_groups=mesh['seq'=8,'blk'=4] {'seq'}, dimensions={0} | all-to-all | bytes 524288 | tf_op jit(solution)/shard_map/all_to_all | solution.py:233
  41.4 0.8 %unpack.1 = bf16[128,1024]{1,0:T(8,128)(2,1)} custom-call(bf16[8,128,128]{2,1,0:T(8,128)(2,1)S(1)} %all_to_all.5.parts_ref), custom_call_target="tpu_custom_call" | custom-call | tf_op jit(solution)/shard_map/unpack/pallas_call | solution.py:234
  (2 shorter events, 0.0 us)
Async XLA Ops:
  0.0 10.3 %collective-permute-start.2 = (bf16[4,2,128,128]{3,2,1,0:T(8,128)(2,1)}, bf16[4,2,128,128]{3,2,1,0:T(8,128)(2,1)S(1)}, u32[]{:S(2)}, u32[]{:S(2)}) collective-permute-start(bf16[4,2,128,128]{3,2,1,0:T(8,128)(2,1)} %refs_0_.3), channel_id=1, source_target_pairs={{0,2},{1,3},{2,0},{3,1},{4,6},{5,7},{6,4},{7,5},{8,10},{9,11},{10,... | collective-permute-start | bytes 786440 | tf_op jit(solution)/shard_map/ppermute | solution.py:162
  3.0 1.1 %copy-start = (bf16[128,3072]{1,0:T(8,128)(2,1)S(1)}, bf16[128,3072]{1,0:T(8,128)(2,1)}, u32[]{:S(2)}) copy-start(bf16[128,3072]{1,0:T(8,128)(2,1)} %qkv_ref.3) | copy-start | bytes 2359300
  4.2 8.1 %collective-permute-start = (bf16[3,128,128]{2,1,0:T(8,128)(2,1)S(1)}, bf16[3,128,128]{2,1,0:T(8,128)(2,1)S(1)}, u32[]{:S(2)}, u32[]{:S(2)}) collective-permute-start(bf16[3,128,128]{2,1,0:T(8,128)(2,1)S(1)} %get-tuple-element.14), channel_id=1, source_target_pairs={{0,4},{4,0},{8,12},{12,8},{16,20},{20,16},{24,28},{28,24},{1,5},{5... | collective-permute-start | bytes 294920 | tf_op jit(solution)/shard_map/ppermute | solution.py:162
  5.8 9.6 %collective-permute-start.1 = (bf16[3,128,128]{2,1,0:T(8,128)(2,1)S(1)}, bf16[3,128,128]{2,1,0:T(8,128)(2,1)S(1)}, u32[]{:S(2)}, u32[]{:S(2)}) collective-permute-start(bf16[3,128,128]{2,1,0:T(8,128)(2,1)S(1)} %get-tuple-element.15), channel_id=1, source_target_pairs={{0,8},{4,12},{8,0},{12,4},{16,24},{20,28},{24,16},{28,20},{1,9},{5... | collective-permute-start | bytes 294920 | tf_op jit(solution)/shard_map/ppermute | solution.py:162
  7.4 10.2 %collective-permute-start.4 = (bf16[3,128,128]{2,1,0:T(8,128)(2,1)S(1)}, bf16[3,128,128]{2,1,0:T(8,128)(2,1)S(1)}, u32[]{:S(2)}, u32[]{:S(2)}) collective-permute-start(bf16[3,128,128]{2,1,0:T(8,128)(2,1)S(1)} %get-tuple-element.17), channel_id=1, source_target_pairs={{0,16},{4,20},{8,24},{12,28},{16,0},{20,4},{24,8},{28,12},{1,17},{... | collective-permute-start | bytes 294920 | tf_op jit(solution)/shard_map/ppermute | solution.py:162
  10.0 6.9 %copy-start.1 = (bf16[4,2,128,128]{3,2,1,0:T(8,128)(2,1)S(1)}, bf16[4,2,128,128]{3,2,1,0:T(8,128)(2,1)}, u32[]{:S(2)}) copy-start(bf16[4,2,128,128]{3,2,1,0:T(8,128)(2,1)} %refs_0_.3) | copy-start | bytes 786436
  10.0 11.7 %collective-permute-start.5 = (bf16[3,128,128]{2,1,0:T(8,128)(2,1)S(1)}, bf16[3,128,128]{2,1,0:T(8,128)(2,1)S(1)}, u32[]{:S(2)}, u32[]{:S(2)}) collective-permute-start(bf16[3,128,128]{2,1,0:T(8,128)(2,1)S(1)} %get-tuple-element.18), channel_id=1, source_target_pairs={{0,20},{4,16},{8,28},{12,24},{16,4},{20,0},{24,12},{28,8},{1,21},{... | collective-permute-start | bytes 294920 | tf_op jit(solution)/shard_map/ppermute | solution.py:162
  10.3 5.8 %copy-start.2 = (s32[32,12]{0,1:T(8,128)S(1)}, s32[32,12]{0,1:T(8,128)}, u32[]{:S(2)}) copy-start(s32[32,12]{0,1:T(8,128)} %param.8) | copy-start | bytes 4612
  10.4 11.2 %collective-permute-start.3 = (bf16[3,128,128]{2,1,0:T(8,128)(2,1)S(1)}, bf16[3,128,128]{2,1,0:T(8,128)(2,1)S(1)}, u32[]{:S(2)}, u32[]{:S(2)}) collective-permute-start(bf16[3,128,128]{2,1,0:T(8,128)(2,1)S(1)} %get-tuple-element.16), channel_id=1, source_target_pairs={{0,12},{4,8},{8,4},{12,0},{16,28},{20,24},{24,20},{28,16},{1,13},{... | collective-permute-start | bytes 294920 | tf_op jit(solution)/shard_map/ppermute | solution.py:162
  12.4 9.2 %collective-permute-start.6 = (bf16[3,128,128]{2,1,0:T(8,128)(2,1)S(1)}, bf16[3,128,128]{2,1,0:T(8,128)(2,1)S(1)}, u32[]{:S(2)}, u32[]{:S(2)}) collective-permute-start(bf16[3,128,128]{2,1,0:T(8,128)(2,1)S(1)} %get-tuple-element.19), channel_id=1, source_target_pairs={{0,24},{4,28},{8,16},{12,20},{16,8},{20,12},{24,0},{28,4},{1,25},{... | collective-permute-start | bytes 294920 | tf_op jit(solution)/shard_map/ppermute | solution.py:162
  15.4 7.4 %collective-permute-start.7 = (bf16[3,128,128]{2,1,0:T(8,128)(2,1)S(1)}, bf16[3,128,128]{2,1,0:T(8,128)(2,1)S(1)}, u32[]{:S(2)}, u32[]{:S(2)}) collective-permute-start(bf16[3,128,128]{2,1,0:T(8,128)(2,1)S(1)} %get-tuple-element.20), channel_id=1, source_target_pairs={{0,28},{4,24},{8,20},{12,16},{16,12},{20,8},{24,4},{28,0},{1,29},{... | collective-permute-start | bytes 294920 | tf_op jit(solution)/shard_map/ppermute | solution.py:162
  16.2 0.7 %copy-start.3 = (s32[32,2]{0,1:T(2,128)S(1)}, s32[32,2]{0,1:T(2,128)}, u32[]{:S(2)}) copy-start(s32[32,2]{0,1:T(2,128)} %param.7) | copy-start | bytes 772
  16.2 0.7 %copy-start.4 = (s32[32]{0:T(128)S(1)}, s32[32]{0:T(128)}, u32[]{:S(2)}) copy-start(s32[32]{0:T(128)} %param.9) | copy-start | bytes 388
  17.6 5.3 %collective-permute-start.8 = (bf16[2,4,2,128,128]{4,3,2,1,0:T(8,128)(2,1)S(1)}, bf16[2,4,2,128,128]{4,3,2,1,0:T(8,128)(2,1)S(1)}, u32[]{:S(2)}, u32[]{:S(2)}) collective-permute-start(bf16[2,4,2,128,128]{4,3,2,1,0:T(8,128)(2,1)S(1)} %merge.1), channel_id=1, source_target_pairs={{0,1},{1,0},{2,3},{3,2},{4,5},{5,4},{6,7},{7,6},{8,9},{9,8},{10,11... | collective-permute-start | bytes 1572872 | tf_op jit(solution)/shard_map/ppermute | solution.py:162

commit v4 on v3

v4 whole, which is shorter than its diff:
```python
import functools
import math

import jax
import jax.numpy as jnp
from jax import lax
from jax.experimental import pallas as pl
from jax.experimental.pallas import tpu as pltpu
from jax.sharding import PartitionSpec as P

HEAD_DIM = 128
MASKED_SCORE = -1e30
CHUNK = 6
EARLY = 4
GROUP = 8
COLLECT_FLOPS = 10**10
GATHER_FLOPS = 10**10
VMEM_BYTES = 40 * 1024 * 1024


def pack_kernel(steps, sources, qkv_ref, *refs):
    outs = refs[len(refs) - len(steps) :]
    groups, _, width = outs[0].shape
    me = lax.axis_index("seq")
    for step, out in zip(steps, outs):
        for group in range(groups):
            start = pl.multiple_of((group * sources + (me ^ step)) * width, width)
            out[group] = qkv_ref[:, pl.ds(start, width)]


def merge_kernel(count, *refs):
    for i in range(count):
        refs[-1][i] = refs[i][...]


def collect_kernel(*refs):
    spans, out_ref = refs[:-1], refs[-1]
    for step, span in enumerate(spans):
        out_ref[step] = span[1:]


def order_kernel(blk_count, *refs):
    kepts, kept_ref = refs[:-1], refs[-1]
    region = lax.axis_index("blk")
    kept_dev = kept_ref.shape[0] // blk_count
    pieces = []
    for ref in kepts:
        pieces += [ref] if len(ref.shape) == 4 else [ref.at[i] for i in range(ref.shape[0])]
    for piece, step in zip(pieces, [*range(0, blk_count, 2), *range(1, blk_count, 2)]):
        kept_ref[pl.ds((region ^ step) * kept_dev, kept_dev)] = piece[...]


def relay_kernel(passed_ref, *refs):
    count = len(refs) // 2
    for i in range(count):
        refs[count + i][0] = refs[i][...]
        refs[count + i][1] = passed_ref[1 + i]


def gather_kernel(*refs):
    for i, ref in enumerate(refs[:-1]):
        refs[-1][i] = ref[...]


def unpack_kernel(sources, direct, paired, direct_ref, passed_ref, *refs):
    paired_refs, out_ref = refs[:-1], refs[-1]
    width = passed_ref.shape[2]
    me = lax.axis_index("seq")

    def put(step, part):
        out_ref[:, pl.ds(pl.multiple_of((me ^ step) * width, width), width)] = part

    for i, step in enumerate(direct):
        put(step, direct_ref[i])
    put(1, passed_ref[0])
    for step, ref in zip(paired, paired_refs):
        put(step, ref[0])
        put(step + 1, ref[1])


def stack(pieces):
    return jnp.concatenate(pieces, axis=0)


def attend(items, query_refs, span_ref, kept_ref, out_refs, scores, near_count, window):
    tile_len = scores.shape[1]
    factor = math.log2(math.e) / math.sqrt(HEAD_DIM)
    first = range(min(CHUNK, window))
    later = [range(i, min(i + CHUNK, window)) for i in range(CHUNK, window, CHUNK)]

    def dot_keys(queries, keys):
        raw = lax.dot_general(
            queries, keys, (((1,), (1,)), ((), ())), preferred_element_type=jnp.float32
        )
        return [raw[:, i : i + tile_len] for i in range(0, raw.shape[1], tile_len)]

    def masked(raws, slots, count):
        return [r if w == 0 else jnp.where(w < count, r, MASKED_SCORE) for w, r in zip(slots, raws)]

    def queries_of(u):
        step, rows, cols = items[u][:3]
        return query_refs[step][0, rows, cols]

    def far_blocks(u, kind, slots):
        _, _, cols, _, _, far = items[u]
        return [kept_ref[far[w], kind, :, cols] for w in slots]

    def near_blocks(u, kind):
        _, _, cols, _, near, _ = items[u]
        return [span_ref[s, kind, r, cols] for s, r in near]

    def store(u, start, raws):
        for i, r in enumerate(raws):
            scores[u, :, (start + i) * tile_len : (start + i + 1) * tile_len] = r

    def weigh(u, start, values):
        weights = []
        for i in range(len(values)):
            r = scores[u, :, (start + i) * tile_len : (start + i + 1) * tile_len]
            weights.append(jnp.exp2(r * factor - tops[u]))
        rounded = jnp.concatenate([w.astype(jnp.bfloat16) for w in weights], axis=1)
        mixed = jnp.dot(rounded, stack(values), preferred_element_type=jnp.float32)
        return functools.reduce(jnp.add, weights), mixed

    tops = []
    for u, (_, _, _, count, _, _) in enumerate(items):
        raws = dot_keys(queries_of(u), stack(near_blocks(u, 0) + far_blocks(u, 0, first)))
        raws = raws[:near_count] + masked(raws[near_count:], first, count)
        store(u, 0, raws)
        tops.append(functools.reduce(jnp.maximum, raws))
    for u, (_, _, _, count, _, _) in enumerate(items):
        for slots in later:

            def more(top, u=u, slots=slots, count=count):
                raws = dot_keys(queries_of(u), stack(far_blocks(u, 0, slots)))
                raws = masked(raws, slots, count)
                store(u, near_count + slots[0], raws)
                return functools.reduce(jnp.maximum, [top, *raws])

            tops[u] = lax.cond(slots[0] < count, more, lambda top: top, tops[u])
    tops = [jnp.max(top, axis=1, keepdims=True) * factor for top in tops]
    sums = [weigh(u, 0, near_blocks(u, 1) + far_blocks(u, 1, first)) for u in range(len(items))]
    for u, (_, _, _, count, _, _) in enumerate(items):
        for slots in later:

            def add(carry, u=u, slots=slots):
                total, mixed = weigh(u, near_count + slots[0], far_blocks(u, 1, slots))
                return carry[0] + total, carry[1] + mixed

            sums[u] = lax.cond(slots[0] < count, add, lambda carry: carry, sums[u])
    for u, (step, rows, cols, _, _, _) in enumerate(items):
        total = jnp.sum(sums[u][0], axis=1, keepdims=True)
        out_refs[step][rows, cols] = (sums[u][1] / total).astype(jnp.bfloat16)


def attention_kernel(places, blk_count, tile_len, near_count, lists_ref, span_ref, kept_ref, *refs):
    sources = span_ref.shape[0]
    query_refs, buffers, scores = refs[:sources], refs[sources:-1], refs[-1]
    out_refs = [buffers[i] if j is None else buffers[i].at[j] for i, j in places]
    _, _, tok_rows, width = span_ref.shape
    tiles_dev = tok_rows // tile_len
    window = lists_ref.shape[0] - near_count - 1
    me = lax.axis_index("seq")
    region = lax.axis_index("blk")
    items = []
    for step in range(sources):
        for place in range(tiles_dev):
            rows = slice(place * tile_len, (place + 1) * tile_len)
            tile = ((me ^ step) * blk_count + region) * tiles_dev + place
            near = []
            for c in range(near_count):
                other = lists_ref[c, tile]
                source = other // (tiles_dev * blk_count)
                start = pl.multiple_of(other % tiles_dev * tile_len, tile_len)
                near.append((source ^ me, pl.ds(start, tile_len)))
            far = [lists_ref[near_count + w, tile] for w in range(window)]
            count = lists_ref[near_count + window, tile]
            for head in range(width // HEAD_DIM):
                cols = slice(head * HEAD_DIM, (head + 1) * HEAD_DIM)
                items.append((step, rows, cols, count, near, far))

    for start in range(0, len(items), GROUP):
        attend(
            items[start : start + GROUP],
            query_refs,
            span_ref,
            kept_ref,
            out_refs,
            scores,
            near_count,
            window,
        )


def swap(array, axis, step):
    if step == 0:
        return array
    count = lax.axis_size(axis)
    return lax.ppermute(array, axis, [(i, i ^ step) for i in range(count)])


def sending_order(count):
    near, far = list(range(1, count // 2)), list(range(count // 2, count))
    return near[:1] + far[:1] + near[1:2] + far[1:] + near[2:]


def per_device(qkv, kept_kv, cur_list, kept_list, kept_count):
    seq_count = lax.axis_size("seq")
    blk_count = lax.axis_size("blk")
    tok_rows = qkv.shape[0]
    kept_dev, _, tile_len, width = kept_kv.shape
    dtype = qkv.dtype
    near_count, window = cur_list.shape[1], kept_list.shape[1]
    vmem = pl.BlockSpec(memory_space=pltpu.VMEM)
    anywhere = pl.BlockSpec(memory_space=pl.ANY)
    smem = pl.BlockSpec(memory_space=pltpu.SMEM)
    params = pltpu.CompilerParams(vmem_limit_bytes=VMEM_BYTES)

    lists = jnp.concatenate([cur_list.T, kept_list.T, kept_count[None]], axis=0)
    kepts = [swap(kept_kv, "blk", step) for step in range(0, blk_count, 2)]
    order = sending_order(seq_count)
    spans = [None] * seq_count
    for steps, before in (([0, *order[:EARLY]], []), (order[EARLY:], kepts[1:])):
        packed = pl.pallas_call(
            functools.partial(pack_kernel, steps, seq_count),
            out_shape=[jax.ShapeDtypeStruct((3, tok_rows, width), dtype)] * len(steps),
            in_specs=[vmem] + [anywhere] * len(before),
            out_specs=[vmem] * len(steps),
            compiler_params=params,
            name="pack",
        )(qkv, *before)
        for step, piece in zip(steps, packed):
            spans[step] = swap(piece, "seq", step)
    after = []
    merged = pl.pallas_call(
        functools.partial(merge_kernel, len(kepts)),
        out_shape=jax.ShapeDtypeStruct((len(kepts), *kept_kv.shape), dtype),
        in_specs=[vmem] * len(kepts) + [anywhere] * len(after),
        out_specs=vmem,
        compiler_params=params,
        name="merge",
    )(*kepts, *after)
    kepts.append(swap(merged, "blk", 1))

    kept = pl.pallas_call(
        functools.partial(order_kernel, blk_count),
        out_shape=jax.ShapeDtypeStruct((blk_count * kept_dev, 2, tile_len, width), dtype),
        in_specs=[vmem] * len(kepts),
        out_specs=vmem,
        compiler_params=params,
        name="order",
    )(*kepts)
    span = pl.pallas_call(
        collect_kernel,
        out_shape=jax.ShapeDtypeStruct((seq_count, 2, tok_rows, width), dtype),
        in_specs=[vmem] * seq_count,
        out_specs=vmem,
        compiler_params=params,
        cost_estimate=pl.CostEstimate(flops=COLLECT_FLOPS, bytes_accessed=0, transcendentals=0),
        name="collect",
    )(*spans)

    half = seq_count // 2
    direct = [0, half + 1, half]
    paired = [step for step in range(seq_count - 2, 0, -2) if step != half]
    passed = [1] + [step + 1 for step in paired]
    places = [None] * seq_count
    for i, step in enumerate(direct + paired):
        places[step] = (1 + i, None)
    for i, step in enumerate(passed):
        places[step] = (0, i)
    one = jax.ShapeDtypeStruct((tok_rows, width), dtype)
    two = jax.ShapeDtypeStruct((2, tok_rows, width), dtype)
    per_step = tok_rows // tile_len * (width // HEAD_DIM)
    sent, *outs = pl.pallas_call(
        functools.partial(attention_kernel, places, blk_count, tile_len, near_count),
        out_shape=[jax.ShapeDtypeStruct((len(passed), tok_rows, width), dtype)]
        + [one] * len(direct + paired),
        in_specs=[smem] + [vmem] * (2 + seq_count),
        out_specs=[vmem] * (1 + len(direct + paired)),
        scratch_shapes=[
            pltpu.VMEM(
                (min(GROUP, seq_count * per_step), tile_len, (near_count + window) * tile_len), jnp.float32
            )
        ],
        compiler_params=params,
        name="attention",
    )(lists, span, kept, *spans)

    sent = swap(sent, "seq", 1)
    outs = outs[:1] + [swap(out, "seq", step) for out, step in zip(outs[1:], direct[1:])] + outs[len(direct):]
    relayed = pl.pallas_call(
        relay_kernel,
        out_shape=[two] * len(paired),
        in_specs=[vmem] * (1 + len(paired)),
        out_specs=[vmem] * len(paired),
        compiler_params=params,
        name="relay",
    )(sent, *outs[len(direct):])
    relayed = [swap(buffer, "seq", step) for buffer, step in zip(relayed, paired)]
    gathered = pl.pallas_call(
        gather_kernel,
        out_shape=jax.ShapeDtypeStruct((len(direct), tok_rows, width), dtype),
        in_specs=[vmem] * len(direct),
        out_specs=vmem,
        compiler_params=params,
        cost_estimate=pl.CostEstimate(flops=GATHER_FLOPS, bytes_accessed=0, transcendentals=0),
        name="gather",
    )(*outs[: len(direct)])
    return pl.pallas_call(
        functools.partial(unpack_kernel, seq_count, direct, paired),
        out_shape=jax.ShapeDtypeStruct((tok_rows, seq_count * width), dtype),
        in_specs=[vmem] * (2 + len(paired)),
        out_specs=vmem,
        compiler_params=params,
        name="unpack",
    )(gathered, sent, *relayed)


def solution(mesh):
    placed = (P(("seq", "blk"), None), P("blk", None, None, "seq"), P(), P(), P())
    return jax.shard_map(
        per_device, mesh=mesh, in_specs=placed, out_specs=P(("seq", "blk"), None), check_vma=False
    )
```

time: 42.6 us -> 41.2 us (0.967)
  blocking collectives: 15.7 us -> 0 us
  starting transfers between devices: 14.8 us -> 25.9 us
  waiting for transfers between devices: 5.87 us -> 8.71 us
  Pallas kernels: 3.94 us -> 4.41 us
    all_to_all x1 -> x0, blocking collectives: 15.7 us -> none  [per_device(): lax.all_to_all(attended, 'seq', split_axis=0, concat_axis=0, tiled=True)]
    ppermute x9 -> x14, starting transfers between devices: 14.8 us -> 25.9 us  [swap(): return lax.ppermute(array, axis, [(i, i ^ step) for i in range(count)])]
    ppermute x9 -> x14, waiting for transfers between devices: 5.87 us -> 8.71 us  [swap(): return lax.ppermute(array, axis, [(i, i ^ step) for i in range(count)])]
    pallas_call x2 -> x5, Pallas kernels: 3.63 us -> 4.13 us  [the longest x1 3.26 us: per_device(): pl.pallas_call(functools.partial(attention_kernel, places, blk_count, til...]
  transfers between devices with their start and end apart: 9 -> 14, of which waited for: 3 -> 6; matrix products, arithmetic and copies ran while one was open for 0% -> 0% of each run, Pallas kernels for 1% -> 1%
where the time goes in v4:
time: 41.2 us; the launch traced here: 40.9 us
  starting transfers between devices  25.9 us (63%)
  waiting for transfers between devices  8.71 us (21%)
  Pallas kernels  4.41 us (11%)
  local copies, waits for them, and re-layouts  1.82 us (4%)
    ppermute x14, starting transfers between devices, swap(): return lax.ppermute(array, axis, [(i, i ^ step) for i in range(count)])  25.9 us
    ppermute x14, waiting for transfers between devices, swap(): return lax.ppermute(array, axis, [(i, i ^ step) for i in range(count)])  8.71 us
    pallas_call x1, Pallas kernels, per_device(): pl.pallas_call(functools.partial(attention_kernel, places, blk_count, til...  3.26 us
    unnamed x10, local copies, waits for them, and re-layouts  1.82 us
  transfers between devices with their start and end apart: 14, of which 6 were waited for; matrix products, arithmetic and copies ran while one was open for 0% of the time, Pallas kernels for 1%

profile of v4, /device:TPU:0, one launch (start us, length us, event | category | flops | bytes accessed | tf_op | source)
XLA Modules:
  0.0 40.9 jit_solution(14972422133641726252)
XLA Ops:
  0.0 3.0 %collective-permute-start.2 = (bf16[4,2,128,128]{3,2,1,0:T(8,128)(2,1)}, bf16[4,2,128,128]{3,2,1,0:T(8,128)(2,1)S(1)}, u32[]{:S(2)}, u32[]{:S(2)}) collective-permute-start(bf16[4,2,128,128]{3,2,1,0:T(8,128)(2,1)} %refs_0_.3), channel_id=1, source_target_pairs={{0,2},{1,3},{2,0},{3,1},{4,6},{5,7},{6,4},{7,5},{8,10},{9,11},{10,... | collective-permute-start | bytes 786440 | tf_op jit(solution)/shard_map/ppermute | solution.py:199
  3.0 0.0 copy-start
  3.0 1.1 %copy-done = bf16[128,3072]{1,0:T(8,128)(2,1)S(1)} copy-done((bf16[128,3072]{1,0:T(8,128)(2,1)S(1)}, bf16[128,3072]{1,0:T(8,128)(2,1)}, u32[]{:S(2)}) %copy-start) | copy-done | bytes 786456
  4.1 0.1 pack.2
  4.2 1.6 %collective-permute-start = (bf16[3,128,128]{2,1,0:T(8,128)(2,1)S(1)}, bf16[3,128,128]{2,1,0:T(8,128)(2,1)S(1)}, u32[]{:S(2)}, u32[]{:S(2)}) collective-permute-start(bf16[3,128,128]{2,1,0:T(8,128)(2,1)S(1)} %get-tuple-element.22), channel_id=1, source_target_pairs={{0,4},{4,0},{8,12},{12,8},{16,20},{20,16},{24,28},{28,24},{1,5},{5... | collective-permute-start | bytes 294920 | tf_op jit(solution)/shard_map/ppermute | solution.py:199
  5.8 1.6 %collective-permute-start.1 = (bf16[3,128,128]{2,1,0:T(8,128)(2,1)S(1)}, bf16[3,128,128]{2,1,0:T(8,128)(2,1)S(1)}, u32[]{:S(2)}, u32[]{:S(2)}) collective-permute-start(bf16[3,128,128]{2,1,0:T(8,128)(2,1)S(1)} %get-tuple-element.23), channel_id=1, source_target_pairs={{0,8},{4,12},{8,0},{12,4},{16,24},{20,28},{24,16},{28,20},{1,9},{5... | collective-permute-start | bytes 294920 | tf_op jit(solution)/shard_map/ppermute | solution.py:199
  7.4 2.6 %collective-permute-start.4 = (bf16[3,128,128]{2,1,0:T(8,128)(2,1)S(1)}, bf16[3,128,128]{2,1,0:T(8,128)(2,1)S(1)}, u32[]{:S(2)}, u32[]{:S(2)}) collective-permute-start(bf16[3,128,128]{2,1,0:T(8,128)(2,1)S(1)} %get-tuple-element.25), channel_id=1, source_target_pairs={{0,16},{4,20},{8,24},{12,28},{16,0},{20,4},{24,8},{28,12},{1,17},{... | collective-permute-start | bytes 294920 | tf_op jit(solution)/shard_map/ppermute | solution.py:199
  10.0 0.0 copy-start.1
  10.0 0.3 collective-permute-start.5
  10.3 0.0 collective-permute-done.2.refs_0_.refs_1_
  10.3 0.1 pack.3
  10.3 0.0 copy-start.2
  10.4 2.0 %collective-permute-start.3 = (bf16[3,128,128]{2,1,0:T(8,128)(2,1)S(1)}, bf16[3,128,128]{2,1,0:T(8,128)(2,1)S(1)}, u32[]{:S(2)}, u32[]{:S(2)}) collective-permute-start(bf16[3,128,128]{2,1,0:T(8,128)(2,1)S(1)} %get-tuple-element.24), channel_id=1, source_target_pairs={{0,12},{4,8},{8,4},{12,0},{16,28},{20,24},{24,20},{28,16},{1,13},{... | collective-permute-start | bytes 294920 | tf_op jit(solution)/shard_map/ppermute | solution.py:199
  12.4 0.0 collective-permute-done.refs_1_
  12.4 3.0 %collective-permute-start.6 = (bf16[3,128,128]{2,1,0:T(8,128)(2,1)S(1)}, bf16[3,128,128]{2,1,0:T(8,128)(2,1)S(1)}, u32[]{:S(2)}, u32[]{:S(2)}) collective-permute-start(bf16[3,128,128]{2,1,0:T(8,128)(2,1)S(1)} %get-tuple-element.27), channel_id=1, source_target_pairs={{0,24},{4,28},{8,16},{12,20},{16,8},{20,12},{24,0},{28,4},{1,25},{... | collective-permute-start | bytes 294920 | tf_op jit(solution)/shard_map/ppermute | solution.py:199
  15.4 0.0 collective-permute-done.1.refs_2_
  15.4 0.8 %collective-permute-start.7 = (bf16[3,128,128]{2,1,0:T(8,128)(2,1)S(1)}, bf16[3,128,128]{2,1,0:T(8,128)(2,1)S(1)}, u32[]{:S(2)}, u32[]{:S(2)}) collective-permute-start(bf16[3,128,128]{2,1,0:T(8,128)(2,1)S(1)} %get-tuple-element.28), channel_id=1, source_target_pairs={{0,28},{4,24},{8,20},{12,16},{16,12},{20,8},{24,4},{28,0},{1,29},{... | collective-permute-start | bytes 294920 | tf_op jit(solution)/shard_map/ppermute | solution.py:199
  16.2 0.0 copy-start.3
  16.2 0.0 copy-start.4
  16.2 0.0 copy-done.2
  16.2 0.7 %copy-done.3 = s32[32,2]{0,1:T(2,128)S(1)} copy-done((s32[32,2]{0,1:T(2,128)S(1)}, s32[32,2]{0,1:T(2,128)}, u32[]{:S(2)}) %copy-start.3) | copy-done | bytes 280
  16.9 0.0 copy-done.4
  16.9 0.0 copy-done.1
  16.9 0.7 %collective-permute-done.4.refs_4_ = bf16[3,128,128]{2,1,0:T(8,128)(2,1)S(1)} collective-permute-done((bf16[3,128,128]{2,1,0:T(8,128)(2,1)S(1)}, bf16[3,128,128]{2,1,0:T(8,128)(2,1)S(1)}, u32[]{:S(2)}, u32[]{:S(2)}) %collective-permute-start.4) | collective-permute-done | bytes 98336 | tf_op jit(solution)/shard_map/ppermute | solution.py:199
  17.6 0.0 collective-permute-start.8
  17.6 4.0 %collective-permute-done.5.refs_5_ = bf16[3,128,128]{2,1,0:T(8,128)(2,1)S(1)} collective-permute-done((bf16[3,128,128]{2,1,0:T(8,128)(2,1)S(1)}, bf16[3,128,128]{2,1,0:T(8,128)(2,1)S(1)}, u32[]{:S(2)}, u32[]{:S(2)}) %collective-permute-start.5) | collective-permute-done | bytes 98336 | tf_op jit(solution)/shard_map/ppermute | solution.py:199
  21.6 0.0 collective-permute-done.3.refs_3_
  21.6 0.0 collective-permute-done.6.refs_6_
  21.6 1.2 %collective-permute-done.7.refs_7_ = bf16[3,128,128]{2,1,0:T(8,128)(2,1)S(1)} collective-permute-done((bf16[3,128,128]{2,1,0:T(8,128)(2,1)S(1)}, bf16[3,128,128]{2,1,0:T(8,128)(2,1)S(1)}, u32[]{:S(2)}, u32[]{:S(2)}) %collective-permute-start.7) | collective-permute-done | bytes 98336 | tf_op jit(solution)/shard_map/ppermute | solution.py:199
  22.8 0.0 collective-permute-done.8.refs_2_
  22.8 0.1 order.1.kept_ref
  22.9 3.3 %attention.1 = (bf16[3,128,128]{2,1,0:T(8,128)(2,1)S(1)}, bf16[128,128]{1,0:T(8,128)(2,1)S(1)}, bf16[128,128]{1,0:T(8,128)(2,1)S(1)}, bf16[128,128]{1,0:T(8,128)...) custom-call(s32[15,32]{1,0:T(8,128)S(1)} %pad_add_fusion.lists_ref, ...), custom_call_target="tpu_custom_call" | custom-call | tf_op jit(solution)/shard_map/attention/pallas_call | solution.py:275
  26.2 2.2 %collective-permute-start.11 = (bf16[3,128,128]{2,1,0:T(8,128)(2,1)S(1)}, bf16[3,128,128]{2,1,0:T(8,128)(2,1)S(1)}, u32[]{:S(2)}, u32[]{:S(2)}) collective-permute-start(bf16[3,128,128]{2,1,0:T(8,128)(2,1)S(1)} %get-tuple-element.32), channel_id=1, source_target_pairs={{0,4},{4,0},{8,12},{12,8},{16,20},{20,16},{24,28},{28,24},{1,5},{5... | collective-permute-start | bytes 294920 | tf_op jit(solution)/shard_map/ppermute | solution.py:199
  28.4 4.8 %collective-permute-start.10 = (bf16[128,128]{1,0:T(8,128)(2,1)S(1)}, bf16[128,128]{1,0:T(8,128)(2,1)S(1)}, u32[]{:S(2)}, u32[]{:S(2)}) collective-permute-start(bf16[128,128]{1,0:T(8,128)(2,1)S(1)} %get-tuple-element.31), channel_id=1, source_target_pairs={{0,16},{4,20},{8,24},{12,28},{16,0},{20,4},{24,8},{28,12},{1,17},{... | collective-permute-start | bytes 98312 | tf_op jit(solution)/shard_map/ppermute | solution.py:199
  33.2 0.0 collective-permute-start.9
  33.2 0.0 collective-permute-done.11.passed_ref
  33.2 1.4 %collective-permute-start.12 = (bf16[2,128,128]{2,1,0:T(8,128)(2,1)S(1)}, bf16[2,128,128]{2,1,0:T(8,128)(2,1)S(1)}, u32[]{:S(2)}, u32[]{:S(2)}) collective-permute-start(bf16[2,128,128]{2,1,0:T(8,128)(2,1)S(1)} %get-tuple-element.35), channel_id=1, source_target_pairs={{0,24},{4,28},{8,16},{12,20},{16,8},{20,12},{24,0},{28,4},{1,25},{... | collective-permute-start | bytes 196616 | tf_op jit(solution)/shard_map/ppermute | solution.py:199
  34.7 2.7 %collective-permute-start.13 = (bf16[2,128,128]{2,1,0:T(8,128)(2,1)S(1)}, bf16[2,128,128]{2,1,0:T(8,128)(2,1)S(1)}, u32[]{:S(2)}, u32[]{:S(2)}) collective-permute-start(bf16[2,128,128]{2,1,0:T(8,128)(2,1)S(1)} %get-tuple-element.36), channel_id=1, source_target_pairs={{0,8},{4,12},{8,0},{12,4},{16,24},{20,28},{24,16},{28,20},{1,9},{5... | collective-permute-start | bytes 196616 | tf_op jit(solution)/shard_map/ppermute | solution.py:199
  37.3 0.0 collective-permute-done.10.refs_2_
  37.3 1.6 %collective-permute-done.9.refs_1_ = bf16[128,128]{1,0:T(8,128)(2,1)S(1)} collective-permute-done((bf16[128,128]{1,0:T(8,128)(2,1)S(1)}, bf16[128,128]{1,0:T(8,128)(2,1)S(1)}, u32[]{:S(2)}, u32[]{:S(2)}) %collective-permute-start.9) | collective-permute-done | bytes 32800 | tf_op jit(solution)/shard_map/ppermute | solution.py:199
  38.9 0.6 %collective-permute-done.12.refs_0_ = bf16[2,128,128]{2,1,0:T(8,128)(2,1)S(1)} collective-permute-done((bf16[2,128,128]{2,1,0:T(8,128)(2,1)S(1)}, bf16[2,128,128]{2,1,0:T(8,128)(2,1)S(1)}, u32[]{:S(2)}, u32[]{:S(2)}) %collective-permute-start.12) | collective-permute-done | bytes 65568 | tf_op jit(solution)/shard_map/ppermute | solution.py:199
  39.5 0.6 %collective-permute-done.13.refs_1_ = bf16[2,128,128]{2,1,0:T(8,128)(2,1)S(1)} collective-permute-done((bf16[2,128,128]{2,1,0:T(8,128)(2,1)S(1)}, bf16[2,128,128]{2,1,0:T(8,128)(2,1)S(1)}, u32[]{:S(2)}, u32[]{:S(2)}) %collective-permute-start.13) | collective-permute-done | bytes 65568 | tf_op jit(solution)/shard_map/ppermute | solution.py:199
  40.2 0.8 %unpack.1 = bf16[128,1024]{1,0:T(8,128)(2,1)} custom-call(bf16[3,128,128]{2,1,0:T(8,128)(2,1)S(1)} %gather.1.direct_ref, bf16[3,128,128]{2,1,0:T(8,128)(2,1)S(1)} %collective-permute-done.11.passed_ref, bf16[2,128,128]{2,1,0:T(8,128)(2,1)S(1)} %collective-permute-done.12.refs_0_, bf16[2,128,128]{2,1,0:T(8,128)(2,1)S(1)} %collective-permute-done.13.refs_1_), custom_call_target="tpu_custom_call" | custom-call | tf_op jit(solution)/shard_map/unpack/pallas_call | solution.py:310
  (5 shorter events, 0.1 us)
Async XLA Ops:
  0.0 10.3 %collective-permute-start.2 = (bf16[4,2,128,128]{3,2,1,0:T(8,128)(2,1)}, bf16[4,2,128,128]{3,2,1,0:T(8,128)(2,1)S(1)}, u32[]{:S(2)}, u32[]{:S(2)}) collective-permute-start(bf16[4,2,128,128]{3,2,1,0:T(8,128)(2,1)} %refs_0_.3), channel_id=1, source_target_pairs={{0,2},{1,3},{2,0},{3,1},{4,6},{5,7},{6,4},{7,5},{8,10},{9,11},{10,... | collective-permute-start | bytes 786440 | tf_op jit(solution)/shard_map/ppermute | solution.py:199
  3.0 1.1 %copy-start = (bf16[128,3072]{1,0:T(8,128)(2,1)S(1)}, bf16[128,3072]{1,0:T(8,128)(2,1)}, u32[]{:S(2)}) copy-start(bf16[128,3072]{1,0:T(8,128)(2,1)} %qkv_ref.3) | copy-start | bytes 2359300
  4.2 8.1 %collective-permute-start = (bf16[3,128,128]{2,1,0:T(8,128)(2,1)S(1)}, bf16[3,128,128]{2,1,0:T(8,128)(2,1)S(1)}, u32[]{:S(2)}, u32[]{:S(2)}) collective-permute-start(bf16[3,128,128]{2,1,0:T(8,128)(2,1)S(1)} %get-tuple-element.22), channel_id=1, source_target_pairs={{0,4},{4,0},{8,12},{12,8},{16,20},{20,16},{24,28},{28,24},{1,5},{5... | collective-permute-start | bytes 294920 | tf_op jit(solution)/shard_map/ppermute | solution.py:199
  5.8 9.6 %collective-permute-start.1 = (bf16[3,128,128]{2,1,0:T(8,128)(2,1)S(1)}, bf16[3,128,128]{2,1,0:T(8,128)(2,1)S(1)}, u32[]{:S(2)}, u32[]{:S(2)}) collective-permute-start(bf16[3,128,128]{2,1,0:T(8,128)(2,1)S(1)} %get-tuple-element.23), channel_id=1, source_target_pairs={{0,8},{4,12},{8,0},{12,4},{16,24},{20,28},{24,16},{28,20},{1,9},{5... | collective-permute-start | bytes 294920 | tf_op jit(solution)/shard_map/ppermute | solution.py:199
  7.4 10.2 %collective-permute-start.4 = (bf16[3,128,128]{2,1,0:T(8,128)(2,1)S(1)}, bf16[3,128,128]{2,1,0:T(8,128)(2,1)S(1)}, u32[]{:S(2)}, u32[]{:S(2)}) collective-permute-start(bf16[3,128,128]{2,1,0:T(8,128)(2,1)S(1)} %get-tuple-element.25), channel_id=1, source_target_pairs={{0,16},{4,20},{8,24},{12,28},{16,0},{20,4},{24,8},{28,12},{1,17},{... | collective-permute-start | bytes 294920 | tf_op jit(solution)/shard_map/ppermute | solution.py:199
  10.0 6.9 %copy-start.1 = (bf16[4,2,128,128]{3,2,1,0:T(8,128)(2,1)S(1)}, bf16[4,2,128,128]{3,2,1,0:T(8,128)(2,1)}, u32[]{:S(2)}) copy-start(bf16[4,2,128,128]{3,2,1,0:T(8,128)(2,1)} %refs_0_.3) | copy-start | bytes 786436
  10.0 11.7 %collective-permute-start.5 = (bf16[3,128,128]{2,1,0:T(8,128)(2,1)S(1)}, bf16[3,128,128]{2,1,0:T(8,128)(2,1)S(1)}, u32[]{:S(2)}, u32[]{:S(2)}) collective-permute-start(bf16[3,128,128]{2,1,0:T(8,128)(2,1)S(1)} %get-tuple-element.26), channel_id=1, source_target_pairs={{0,20},{4,16},{8,28},{12,24},{16,4},{20,0},{24,12},{28,8},{1,21},{... | collective-permute-start | bytes 294920 | tf_op jit(solution)/shard_map/ppermute | solution.py:199
  10.3 5.8 %copy-start.2 = (s32[32,12]{0,1:T(8,128)S(1)}, s32[32,12]{0,1:T(8,128)}, u32[]{:S(2)}) copy-start(s32[32,12]{0,1:T(8,128)} %param.8) | copy-start | bytes 4612
  10.4 11.2 %collective-permute-start.3 = (bf16[3,128,128]{2,1,0:T(8,128)(2,1)S(1)}, bf16[3,128,128]{2,1,0:T(8,128)(2,1)S(1)}, u32[]{:S(2)}, u32[]{:S(2)}) collective-permute-start(bf16[3,128,128]{2,1,0:T(8,128)(2,1)S(1)} %get-tuple-element.24), channel_id=1, source_target_pairs={{0,12},{4,8},{8,4},{12,0},{16,28},{20,24},{24,20},{28,16},{1,13},{... | collective-permute-start | bytes 294920 | tf_op jit(solution)/shard_map/ppermute | solution.py:199
  12.4 9.2 %collective-permute-start.6 = (bf16[3,128,128]{2,1,0:T(8,128)(2,1)S(1)}, bf16[3,128,128]{2,1,0:T(8,128)(2,1)S(1)}, u32[]{:S(2)}, u32[]{:S(2)}) collective-permute-start(bf16[3,128,128]{2,1,0:T(8,128)(2,1)S(1)} %get-tuple-element.27), channel_id=1, source_target_pairs={{0,24},{4,28},{8,16},{12,20},{16,8},{20,12},{24,0},{28,4},{1,25},{... | collective-permute-start | bytes 294920 | tf_op jit(solution)/shard_map/ppermute | solution.py:199
  15.4 7.4 %collective-permute-start.7 = (bf16[3,128,128]{2,1,0:T(8,128)(2,1)S(1)}, bf16[3,128,128]{2,1,0:T(8,128)(2,1)S(1)}, u32[]{:S(2)}, u32[]{:S(2)}) collective-permute-start(bf16[3,128,128]{2,1,0:T(8,128)(2,1)S(1)} %get-tuple-element.28), channel_id=1, source_target_pairs={{0,28},{4,24},{8,20},{12,16},{16,12},{20,8},{24,4},{28,0},{1,29},{... | collective-permute-start | bytes 294920 | tf_op jit(solution)/shard_map/ppermute | solution.py:199
  16.2 0.7 %copy-start.3 = (s32[32,2]{0,1:T(2,128)S(1)}, s32[32,2]{0,1:T(2,128)}, u32[]{:S(2)}) copy-start(s32[32,2]{0,1:T(2,128)} %param.7) | copy-start | bytes 772
  16.2 0.7 %copy-start.4 = (s32[32]{0:T(128)S(1)}, s32[32]{0:T(128)}, u32[]{:S(2)}) copy-start(s32[32]{0:T(128)} %param.9) | copy-start | bytes 388
  17.6 5.2 %collective-permute-start.8 = (bf16[2,4,2,128,128]{4,3,2,1,0:T(8,128)(2,1)S(1)}, bf16[2,4,2,128,128]{4,3,2,1,0:T(8,128)(2,1)S(1)}, u32[]{:S(2)}, u32[]{:S(2)}) collective-permute-start(bf16[2,4,2,128,128]{4,3,2,1,0:T(8,128)(2,1)S(1)} %merge.1), channel_id=1, source_target_pairs={{0,1},{1,0},{2,3},{3,2},{4,5},{5,4},{6,7},{7,6},{8,9},{9,8},{10,11... | collective-permute-start | bytes 1572872 | tf_op jit(solution)/shard_map/ppermute | solution.py:199
  26.2 7.0 %collective-permute-start.11 = (bf16[3,128,128]{2,1,0:T(8,128)(2,1)S(1)}, bf16[3,128,128]{2,1,0:T(8,128)(2,1)S(1)}, u32[]{:S(2)}, u32[]{:S(2)}) collective-permute-start(bf16[3,128,128]{2,1,0:T(8,128)(2,1)S(1)} %get-tuple-element.32), channel_id=1, source_target_pairs={{0,4},{4,0},{8,12},{12,8},{16,20},{20,16},{24,28},{28,24},{1,5},{5... | collective-permute-start | bytes 294920 | tf_op jit(solution)/shard_map/ppermute | solution.py:199
  28.4 9.0 %collective-permute-start.10 = (bf16[128,128]{1,0:T(8,128)(2,1)S(1)}, bf16[128,128]{1,0:T(8,128)(2,1)S(1)}, u32[]{:S(2)}, u32[]{:S(2)}) collective-permute-start(bf16[128,128]{1,0:T(8,128)(2,1)S(1)} %get-tuple-element.31), channel_id=1, source_target_pairs={{0,16},{4,20},{8,24},{12,28},{16,0},{20,4},{24,8},{28,12},{1,17},{... | collective-permute-start | bytes 98312 | tf_op jit(solution)/shard_map/ppermute | solution.py:199
  33.2 5.7 %collective-permute-start.9 = (bf16[128,128]{1,0:T(8,128)(2,1)S(1)}, bf16[128,128]{1,0:T(8,128)(2,1)S(1)}, u32[]{:S(2)}, u32[]{:S(2)}) collective-permute-start(bf16[128,128]{1,0:T(8,128)(2,1)S(1)} %get-tuple-element.30), channel_id=1, source_target_pairs={{0,20},{4,16},{8,28},{12,24},{16,4},{20,0},{24,12},{28,8},{1,21},{... | collective-permute-start | bytes 98312 | tf_op jit(solution)/shard_map/ppermute | solution.py:199
  33.2 6.3 %collective-permute-start.12 = (bf16[2,128,128]{2,1,0:T(8,128)(2,1)S(1)}, bf16[2,128,128]{2,1,0:T(8,128)(2,1)S(1)}, u32[]{:S(2)}, u32[]{:S(2)}) collective-permute-start(bf16[2,128,128]{2,1,0:T(8,128)(2,1)S(1)} %get-tuple-element.35), channel_id=1, source_target_pairs={{0,24},{4,28},{8,16},{12,20},{16,8},{20,12},{24,0},{28,4},{1,25},{... | collective-permute-start | bytes 196616 | tf_op jit(solution)/shard_map/ppermute | solution.py:199
  34.7 5.5 %collective-permute-start.13 = (bf16[2,128,128]{2,1,0:T(8,128)(2,1)S(1)}, bf16[2,128,128]{2,1,0:T(8,128)(2,1)S(1)}, u32[]{:S(2)}, u32[]{:S(2)}) collective-permute-start(bf16[2,128,128]{2,1,0:T(8,128)(2,1)S(1)} %get-tuple-element.36), channel_id=1, source_target_pairs={{0,8},{4,12},{8,0},{12,4},{16,24},{20,28},{24,16},{28,20},{1,9},{5... | collective-permute-start | bytes 196616 | tf_op jit(solution)/shard_map/ppermute | solution.py:199

commit v5 on v4

--- a/solution.py
+++ b/solution.py
@@ -28,9 +28,23 @@
             out[group] = qkv_ref[:, pl.ds(start, width)]
 
 
-def merge_kernel(count, *refs):
+def merge_kernel(count, blk_count, tiles_dev, *refs):
+    pieces, (cur_ref, kept_list_ref, kept_count_ref) = refs[:count], refs[count : count + 3]
+    merged_ref, lists_ref = refs[-2:]
     for i in range(count):
-        refs[-1][i] = refs[i][...]
+        merged_ref[i] = pieces[i][...]
+    me = lax.axis_index("seq")
+    region = lax.axis_index("blk")
+    for at in range(lists_ref.shape[0]):
+        step, place = at // tiles_dev, at % tiles_dev
+        tile = ((me ^ step) * blk_count + region) * tiles_dev + place
+        near = [cur_ref[c, tile] for c in range(cur_ref.shape[0])]
+        entries = [other // (tiles_dev * blk_count) ^ me for other in near]
+        entries += [other % tiles_dev for other in near]
+        entries += [kept_list_ref[w, tile] for w in range(kept_list_ref.shape[0])]
+        entries.append(kept_count_ref[0, tile])
+        for i, entry in enumerate(entries):
+            lists_ref[at, i : i + 1] = jnp.full((1, lists_ref.shape[2]), entry, jnp.int32)
 
 
 def collect_kernel(*refs):
@@ -82,7 +96,8 @@
     return jnp.concatenate(pieces, axis=0)
 
 
-def attend(items, query_refs, span_ref, kept_ref, out_refs, scores, near_count, window):
+def attend(items, query_refs, span_ref, kept_ref, out_refs, scratch, near_count, window):
+    scores, tops_ref, totals_ref, mixed_ref = scratch
     tile_len = scores.shape[1]
     factor = math.log2(math.e) / math.sqrt(HEAD_DIM)
     first = range(min(CHUNK, window))
@@ -113,71 +128,72 @@
         for i, r in enumerate(raws):
             scores[u, :, (start + i) * tile_len : (start + i + 1) * tile_len] = r
 
-    def weigh(u, start, values):
+    def weigh(u, start, top, values):
         weights = []
         for i in range(len(values)):
             r = scores[u, :, (start + i) * tile_len : (start + i + 1) * tile_len]
-            weights.append(jnp.exp2(r * factor - tops[u]))
+            weights.append(jnp.exp2(r * factor - top))
         rounded = jnp.concatenate([w.astype(jnp.bfloat16) for w in weights], axis=1)
         mixed = jnp.dot(rounded, stack(values), preferred_element_type=jnp.float32)
         return functools.reduce(jnp.add, weights), mixed
 
-    tops = []
     for u, (_, _, _, count, _, _) in enumerate(items):
         raws = dot_keys(queries_of(u), stack(near_blocks(u, 0) + far_blocks(u, 0, first)))
         raws = raws[:near_count] + masked(raws[near_count:], first, count)
         store(u, 0, raws)
-        tops.append(functools.reduce(jnp.maximum, raws))
+        tops_ref[u] = functools.reduce(jnp.maximum, raws)
     for u, (_, _, _, count, _, _) in enumerate(items):
         for slots in later:
 
-            def more(top, u=u, slots=slots, count=count):
+            @pl.when(slots[0] < count)
+            def _(u=u, slots=slots, count=count):
                 raws = dot_keys(queries_of(u), stack(far_blocks(u, 0, slots)))
                 raws = masked(raws, slots, count)
                 store(u, near_count + slots[0], raws)
-                return functools.reduce(jnp.maximum, [top, *raws])
-
-            tops[u] = lax.cond(slots[0] < count, more, lambda top: top, tops[u])
-    tops = [jnp.max(top, axis=1, keepdims=True) * factor for top in tops]
-    sums = [weigh(u, 0, near_blocks(u, 1) + far_blocks(u, 1, first)) for u in range(len(items))]
+                tops_ref[u] = functools.reduce(jnp.maximum, [tops_ref[u], *raws])
+
+    tops = []
+    for u in range(len(items)):
+        top = jnp.max(tops_ref[u], axis=1, keepdims=True) * factor
+        tops_ref[u] = jnp.broadcast_to(top, tops_ref.shape[1:])
+        tops.append(top)
+    for u in range(len(items)):
+        total, mixed = weigh(u, 0, tops[u], near_blocks(u, 1) + far_blocks(u, 1, first))
+        totals_ref[u], mixed_ref[u] = total, mixed
     for u, (_, _, _, count, _, _) in enumerate(items):
         for slots in later:
 
-            def add(carry, u=u, slots=slots):
-                total, mixed = weigh(u, near_count + slots[0], far_blocks(u, 1, slots))
-                return carry[0] + total, carry[1] + mixed
-
-            sums[u] = lax.cond(slots[0] < count, add, lambda carry: carry, sums[u])
+            @pl.when(slots[0] < count)
+            def _(u=u, slots=slots):
+                values = far_blocks(u, 1, slots)
+                total, mixed = weigh(u, near_count + slots[0], tops_ref[u], values)
+                totals_ref[u] += total
+                mixed_ref[u] += mixed
+
     for u, (step, rows, cols, _, _, _) in enumerate(items):
-        total = jnp.sum(sums[u][0], axis=1, keepdims=True)
-        out_refs[step][rows, cols] = (sums[u][1] / total).astype(jnp.bfloat16)
-
-
-def attention_kernel(places, blk_count, tile_len, near_count, lists_ref, span_ref, kept_ref, *refs):
+        total = jnp.sum(totals_ref[u], axis=1, keepdims=True)
+        out_refs[step][rows, cols] = (mixed_ref[u] / total).astype(jnp.bfloat16)
+
+
+def attention_kernel(places, tile_len, near_count, window, lists_ref, span_ref, kept_ref, *refs):
     sources = span_ref.shape[0]
-    query_refs, buffers, scores = refs[:sources], refs[sources:-1], refs[-1]
+    query_refs, buffers, scratch = refs[:sources], refs[sources:-4], refs[-4:]
     out_refs = [buffers[i] if j is None else buffers[i].at[j] for i, j in places]
     _, _, tok_rows, width = span_ref.shape
     tiles_dev = tok_rows // tile_len
-    window = lists_ref.shape[0] - near_count - 1
-    me = lax.axis_index("seq")
-    region = lax.axis_index("blk")
     items = []
-    for step in range(sources):
-        for place in range(tiles_dev):
-            rows = slice(place * tile_len, (place + 1) * tile_len)
-            tile = ((me ^ step) * blk_count + region) * tiles_dev + place
-            near = []
-            for c in range(near_count):
-                other = lists_ref[c, tile]
-                source = other // (tiles_dev * blk_count)
-                start = pl.multiple_of(other % tiles_dev * tile_len, tile_len)
-                near.append((source ^ me, pl.ds(start, tile_len)))
-            far = [lists_ref[near_count + w, tile] for w in range(window)]
-            count = lists_ref[near_count + window, tile]
-            for head in range(width // HEAD_DIM):
-                cols = slice(head * HEAD_DIM, (head + 1) * HEAD_DIM)
-                items.append((step, rows, cols, count, near, far))
+    for at in range(sources * tiles_dev):
+        step, place = at // tiles_dev, at % tiles_dev
+        rows = slice(place * tile_len, (place + 1) * tile_len)
+        near = []
+        for c in range(near_count):
+            start = pl.multiple_of(lists_ref[at, near_count + c, 0] * tile_len, tile_len)
+            near.append((lists_ref[at, c, 0], pl.ds(start, tile_len)))
+        far = [lists_ref[at, 2 * near_count + w, 0] for w in range(window)]
+        count = lists_ref[at, 2 * near_count + window, 0]
+        for head in range(width // HEAD_DIM):
+            cols = slice(head * HEAD_DIM, (head + 1) * HEAD_DIM)
+            items.append((step, rows, cols, count, near, far))
 
     for start in range(0, len(items), GROUP):
         attend(
@@ -186,7 +202,7 @@
             span_ref,
             kept_ref,
             out_refs,
-            scores,
+            scratch,
             near_count,
             window,
         )
@@ -216,7 +232,6 @@
     smem = pl.BlockSpec(memory_space=pltpu.SMEM)
     params = pltpu.CompilerParams(vmem_limit_bytes=VMEM_BYTES)
 
-    lists = jnp.concatenate([cur_list.T, kept_list.T, kept_count[None]], axis=0)
     kepts = [swap(kept_kv, "blk", step) for step in range(0, blk_count, 2)]
     order = sending_order(seq_count)
     spans = [None] * seq_count
@@ -232,14 +247,20 @@
         for step, piece in zip(steps, packed):
             spans[step] = swap(piece, "seq", step)
     after = []
-    merged = pl.pallas_call(
-        functools.partial(merge_kernel, len(kepts)),
-        out_shape=jax.ShapeDtypeStruct((len(kepts), *kept_kv.shape), dtype),
-        in_specs=[vmem] * len(kepts) + [anywhere] * len(after),
-        out_specs=vmem,
+    tiles_dev = tok_rows // tile_len
+    merged, lists = pl.pallas_call(
+        functools.partial(merge_kernel, len(kepts), blk_count, tiles_dev),
+        out_shape=[
+            jax.ShapeDtypeStruct((len(kepts), *kept_kv.shape), dtype),
+            jax.ShapeDtypeStruct(
+                (seq_count * tiles_dev, 2 * near_count + window + 1, HEAD_DIM), jnp.int32
+            ),
+        ],
+        in_specs=[vmem] * len(kepts) + [smem] * 3,
+        out_specs=[vmem] * 2,
         compiler_params=params,
         name="merge",
-    )(*kepts, *after)
+    )(*kepts, cur_list.T, kept_list.T, kept_count[None])
     kepts.append(swap(merged, "blk", 1))
 
     kept = pl.pallas_call(
@@ -272,16 +293,16 @@
     one = jax.ShapeDtypeStruct((tok_rows, width), dtype)
     two = jax.ShapeDtypeStruct((2, tok_rows, width), dtype)
     per_step = tok_rows // tile_len * (width // HEAD_DIM)
+    group = min(GROUP, seq_count * per_step)
     sent, *outs = pl.pallas_call(
-        functools.partial(attention_kernel, places, blk_count, tile_len, near_count),
+        functools.partial(attention_kernel, places, tile_len, near_count, window),
         out_shape=[jax.ShapeDtypeStruct((len(passed), tok_rows, width), dtype)]
         + [one] * len(direct + paired),
-        in_specs=[smem] + [vmem] * (2 + seq_count),
+        in_specs=[vmem] * (3 + seq_count),
         out_specs=[vmem] * (1 + len(direct + paired)),
         scratch_shapes=[
-            pltpu.VMEM(
-                (min(GROUP, seq_count * per_step), tile_len, (near_count + window) * tile_len), jnp.float32
-            )
+            pltpu.VMEM((group, tile_len, (near_count + window) * tile_len), jnp.float32),
+            *[pltpu.VMEM((group, tile_len, tile_len), jnp.float32)] * 3,
         ],
         compiler_params=params,
         name="attention",

time: 41.2 us -> 40.8 us (level)
  Pallas kernels: 4.41 us -> 5.35 us
  waiting for transfers between devices: 8.71 us -> 7.93 us
    pallas_call x2, Pallas kernels: 3.3 us -> 4.25 us  [the longest x1 3.37 us: per_device(): pl.pallas_call(functools.partial(attention_kernel, places, tile_len, near...]
    ppermute x14, waiting for transfers between devices: 8.71 us -> 7.93 us  [swap(): return lax.ppermute(array, axis, [(i, i ^ step) for i in range(count)])]
    unnamed x10 -> x12, local copies, waits for them, and re-layouts: 1.82 us -> 1.82 us
  transfers between devices with their start and end apart: 14 -> 14, of which waited for: 6 -> 5; matrix products, arithmetic and copies ran while one was open for 0% -> 0% of each run, Pallas kernels for 1% -> 3%
where the time goes in v5:
time: 40.8 us
  starting transfers between devices  25.6 us (63%)
  waiting for transfers between devices  7.93 us (19%)
  Pallas kernels  5.35 us (13%)
  local copies, waits for them, and re-layouts  1.82 us (4%)
    ppermute x14, starting transfers between devices, swap(): return lax.ppermute(array, axis, [(i, i ^ step) for i in range(count)])  25.6 us
    ppermute x14, waiting for transfers between devices, swap(): return lax.ppermute(array, axis, [(i, i ^ step) for i in range(count)])  7.93 us
    pallas_call x1, Pallas kernels, per_device(): pl.pallas_call(functools.partial(attention_kernel, places, tile_len, near...  3.37 us
    unnamed x12, local copies, waits for them, and re-layouts  1.82 us
    pallas_call x1, Pallas kernels, per_device(): pl.pallas_call(functools.partial(merge_kernel, len(kepts), blk_count, til...  0.87 us
  transfers between devices with their start and end apart: 14, of which 5 were waited for; matrix products, arithmetic and copies ran while one was open for 0% of the time, Pallas kernels for 3%

profile of v5, /device:TPU:0, one launch (start us, length us, event | category | flops | bytes accessed | tf_op | source)
XLA Modules:
  0.0 40.8 jit_solution(18009773037557147780)
XLA Ops:
  0.0 3.0 %collective-permute-start = (bf16[4,2,128,128]{3,2,1,0:T(8,128)(2,1)}, bf16[4,2,128,128]{3,2,1,0:T(8,128)(2,1)S(1)}, u32[]{:S(2)}, u32[]{:S(2)}) collective-permute-start(bf16[4,2,128,128]{3,2,1,0:T(8,128)(2,1)} %refs_0_.3), channel_id=1, source_target_pairs={{0,2},{1,3},{2,0},{3,1},{4,6},{5,7},{6,4},{7,5},{8,10},{9,11},{10,... | collective-permute-start | bytes 786440 | tf_op jit(solution)/shard_map/ppermute | solution.py:215
  3.0 0.0 copy-start
  3.0 1.1 %copy-done = bf16[128,3072]{1,0:T(8,128)(2,1)S(1)} copy-done((bf16[128,3072]{1,0:T(8,128)(2,1)S(1)}, bf16[128,3072]{1,0:T(8,128)(2,1)}, u32[]{:S(2)}) %copy-start) | copy-done | bytes 786456
  4.1 0.0 copy-start.1
  4.1 0.1 pack.2
  4.2 1.6 %collective-permute-start.1 = (bf16[3,128,128]{2,1,0:T(8,128)(2,1)S(1)}, bf16[3,128,128]{2,1,0:T(8,128)(2,1)S(1)}, u32[]{:S(2)}, u32[]{:S(2)}) collective-permute-start(bf16[3,128,128]{2,1,0:T(8,128)(2,1)S(1)} %get-tuple-element.25), channel_id=1, source_target_pairs={{0,4},{4,0},{8,12},{12,8},{16,20},{20,16},{24,28},{28,24},{1,5},{5... | collective-permute-start | bytes 294920 | tf_op jit(solution)/shard_map/ppermute | solution.py:215
  5.8 1.6 %collective-permute-start.2 = (bf16[3,128,128]{2,1,0:T(8,128)(2,1)S(1)}, bf16[3,128,128]{2,1,0:T(8,128)(2,1)S(1)}, u32[]{:S(2)}, u32[]{:S(2)}) collective-permute-start(bf16[3,128,128]{2,1,0:T(8,128)(2,1)S(1)} %get-tuple-element.26), channel_id=1, source_target_pairs={{0,8},{4,12},{8,0},{12,4},{16,24},{20,28},{24,16},{28,20},{1,9},{5... | collective-permute-start | bytes 294920 | tf_op jit(solution)/shard_map/ppermute | solution.py:215
  7.4 2.6 %collective-permute-start.4 = (bf16[3,128,128]{2,1,0:T(8,128)(2,1)S(1)}, bf16[3,128,128]{2,1,0:T(8,128)(2,1)S(1)}, u32[]{:S(2)}, u32[]{:S(2)}) collective-permute-start(bf16[3,128,128]{2,1,0:T(8,128)(2,1)S(1)} %get-tuple-element.28), channel_id=1, source_target_pairs={{0,16},{4,20},{8,24},{12,28},{16,0},{20,4},{24,8},{28,12},{1,17},{... | collective-permute-start | bytes 294920 | tf_op jit(solution)/shard_map/ppermute | solution.py:215
  10.0 0.0 copy-start.2
  10.0 0.3 collective-permute-start.5
  10.3 0.0 collective-permute-done.refs_1_.refs_0_
  10.3 0.0 copy-done.1
  10.3 0.1 pack.3
  10.4 0.0 copy-start.3
  10.4 2.0 %collective-permute-start.3 = (bf16[3,128,128]{2,1,0:T(8,128)(2,1)S(1)}, bf16[3,128,128]{2,1,0:T(8,128)(2,1)S(1)}, u32[]{:S(2)}, u32[]{:S(2)}) collective-permute-start(bf16[3,128,128]{2,1,0:T(8,128)(2,1)S(1)} %get-tuple-element.27), channel_id=1, source_target_pairs={{0,12},{4,8},{8,4},{12,0},{16,28},{20,24},{24,20},{28,16},{1,13},{... | collective-permute-start | bytes 294920 | tf_op jit(solution)/shard_map/ppermute | solution.py:215
  12.4 0.0 collective-permute-done.1.refs_1_
  12.4 3.0 %collective-permute-start.6 = (bf16[3,128,128]{2,1,0:T(8,128)(2,1)S(1)}, bf16[3,128,128]{2,1,0:T(8,128)(2,1)S(1)}, u32[]{:S(2)}, u32[]{:S(2)}) collective-permute-start(bf16[3,128,128]{2,1,0:T(8,128)(2,1)S(1)} %get-tuple-element.30), channel_id=1, source_target_pairs={{0,24},{4,28},{8,16},{12,20},{16,8},{20,12},{24,0},{28,4},{1,25},{... | collective-permute-start | bytes 294920 | tf_op jit(solution)/shard_map/ppermute | solution.py:215
  15.4 0.0 collective-permute-done.2.refs_2_
  15.4 0.8 %collective-permute-start.7 = (bf16[3,128,128]{2,1,0:T(8,128)(2,1)S(1)}, bf16[3,128,128]{2,1,0:T(8,128)(2,1)S(1)}, u32[]{:S(2)}, u32[]{:S(2)}) collective-permute-start(bf16[3,128,128]{2,1,0:T(8,128)(2,1)S(1)} %get-tuple-element.31), channel_id=1, source_target_pairs={{0,28},{4,24},{8,20},{12,16},{16,12},{20,8},{24,4},{28,0},{1,29},{... | collective-permute-start | bytes 294920 | tf_op jit(solution)/shard_map/ppermute | solution.py:215
  16.2 0.0 copy-start.4
  16.2 0.0 copy-start.5
  16.2 0.0 copy-done.2
  16.2 0.0 copy-done.3
  16.2 0.7 %copy-done.4 = s32[32,2]{0,1:T(2,128)S(1)} copy-done((s32[32,2]{0,1:T(2,128)S(1)}, s32[32,2]{0,1:T(2,128)}, u32[]{:S(2)}) %copy-start.4) | copy-done | bytes 280
  16.9 0.0 copy-done.5
  16.9 0.9 %merge.1 = (bf16[2,4,2,128,128]{4,3,2,1,0:T(8,128)(2,1)S(1)}, s32[8,17,128]{2,1,0:T(8,128)S(1)}) custom-call(bf16[4,2,128,128]{3,2,1,0:T(8,128)(2,1)S(1)} %copy-done.2, bf16[4,2,128,128]{3,2,1,0:T(8,128)(2,1)S(1)} %collective-permute-done.refs_1_.refs_0_, s32[2,32]{1,0:T(2,128)S(1)} %bitcast.4, s32[12,32]{1,0:T(8,128)S(1)} %bitcast.3, s32[1,32]{1,0:T(1,128)S(1)} %bitcast.5), custom_call_target="tpu_custom_call" | custom-call | tf_op jit(solution)/shard_map/merge/pallas_call | solution.py:251
  17.7 0.0 collective-permute-done.4.refs_4_
  17.7 0.1 collective-permute-start.8
  17.8 3.8 %collective-permute-done.5.refs_5_ = bf16[3,128,128]{2,1,0:T(8,128)(2,1)S(1)} collective-permute-done((bf16[3,128,128]{2,1,0:T(8,128)(2,1)S(1)}, bf16[3,128,128]{2,1,0:T(8,128)(2,1)S(1)}, u32[]{:S(2)}, u32[]{:S(2)}) %collective-permute-start.5) | collective-permute-done | bytes 98336 | tf_op jit(solution)/shard_map/ppermute | solution.py:215
  21.6 0.0 collective-permute-done.3.refs_3_
  21.6 0.0 collective-permute-done.6.refs_6_
  21.6 1.2 %collective-permute-done.7.refs_7_ = bf16[3,128,128]{2,1,0:T(8,128)(2,1)S(1)} collective-permute-done((bf16[3,128,128]{2,1,0:T(8,128)(2,1)S(1)}, bf16[3,128,128]{2,1,0:T(8,128)(2,1)S(1)}, u32[]{:S(2)}, u32[]{:S(2)}) %collective-permute-start.7) | collective-permute-done | bytes 98336 | tf_op jit(solution)/shard_map/ppermute | solution.py:215
  22.8 0.0 collective-permute-done.8.refs_2_
  22.8 0.1 order.1.kept_ref
  22.9 3.4 %attention.1 = (bf16[3,128,128]{2,1,0:T(8,128)(2,1)S(1)}, bf16[128,128]{1,0:T(8,128)(2,1)S(1)}, bf16[128,128]{1,0:T(8,128)(2,1)S(1)}, bf16[128,128]{1,0:T(8,128)...) custom-call(s32[8,17,128]{2,1,0:T(8,128)S(1)} %get-tuple-element.23.lists_ref, ...), custom_call_target="tpu_custom_call" | custom-call | tf_op jit(solution)/shard_map/attention/pallas_call | solution.py:297
  26.3 2.2 %collective-permute-start.11 = (bf16[3,128,128]{2,1,0:T(8,128)(2,1)S(1)}, bf16[3,128,128]{2,1,0:T(8,128)(2,1)S(1)}, u32[]{:S(2)}, u32[]{:S(2)}) collective-permute-start(bf16[3,128,128]{2,1,0:T(8,128)(2,1)S(1)} %get-tuple-element.36), channel_id=1, source_target_pairs={{0,4},{4,0},{8,12},{12,8},{16,20},{20,16},{24,28},{28,24},{1,5},{5... | collective-permute-start | bytes 294920 | tf_op jit(solution)/shard_map/ppermute | solution.py:215
  28.5 4.8 %collective-permute-start.9 = (bf16[128,128]{1,0:T(8,128)(2,1)S(1)}, bf16[128,128]{1,0:T(8,128)(2,1)S(1)}, u32[]{:S(2)}, u32[]{:S(2)}) collective-permute-start(bf16[128,128]{1,0:T(8,128)(2,1)S(1)} %get-tuple-element.34), channel_id=1, source_target_pairs={{0,20},{4,16},{8,28},{12,24},{16,4},{20,0},{24,12},{28,8},{1,21},{... | collective-permute-start | bytes 98312 | tf_op jit(solution)/shard_map/ppermute | solution.py:215
  33.3 0.0 collective-permute-start.10
  33.3 0.0 collective-permute-done.11.passed_ref
  33.3 1.8 %collective-permute-start.12 = (bf16[2,128,128]{2,1,0:T(8,128)(2,1)S(1)}, bf16[2,128,128]{2,1,0:T(8,128)(2,1)S(1)}, u32[]{:S(2)}, u32[]{:S(2)}) collective-permute-start(bf16[2,128,128]{2,1,0:T(8,128)(2,1)S(1)} %get-tuple-element.39), channel_id=1, source_target_pairs={{0,24},{4,28},{8,16},{12,20},{16,8},{20,12},{24,0},{28,4},{1,25},{... | collective-permute-start | bytes 196616 | tf_op jit(solution)/shard_map/ppermute | solution.py:215
  35.1 2.0 %collective-permute-start.13 = (bf16[2,128,128]{2,1,0:T(8,128)(2,1)S(1)}, bf16[2,128,128]{2,1,0:T(8,128)(2,1)S(1)}, u32[]{:S(2)}, u32[]{:S(2)}) collective-permute-start(bf16[2,128,128]{2,1,0:T(8,128)(2,1)S(1)} %get-tuple-element.40), channel_id=1, source_target_pairs={{0,8},{4,12},{8,0},{12,4},{16,24},{20,28},{24,16},{28,20},{1,9},{5... | collective-permute-start | bytes 196616 | tf_op jit(solution)/shard_map/ppermute | solution.py:215
  37.1 0.0 collective-permute-done.9.refs_1_
  37.1 1.0 %collective-permute-done.10.refs_2_ = bf16[128,128]{1,0:T(8,128)(2,1)S(1)} collective-permute-done((bf16[128,128]{1,0:T(8,128)(2,1)S(1)}, bf16[128,128]{1,0:T(8,128)(2,1)S(1)}, u32[]{:S(2)}, u32[]{:S(2)}) %collective-permute-start.10) | collective-permute-done | bytes 32800 | tf_op jit(solution)/shard_map/ppermute | solution.py:215
  38.1 1.5 %collective-permute-done.12.refs_0_ = bf16[2,128,128]{2,1,0:T(8,128)(2,1)S(1)} collective-permute-done((bf16[2,128,128]{2,1,0:T(8,128)(2,1)S(1)}, bf16[2,128,128]{2,1,0:T(8,128)(2,1)S(1)}, u32[]{:S(2)}, u32[]{:S(2)}) %collective-permute-start.12) | collective-permute-done | bytes 65568 | tf_op jit(solution)/shard_map/ppermute | solution.py:215
  39.6 0.5 %collective-permute-done.13.refs_1_ = bf16[2,128,128]{2,1,0:T(8,128)(2,1)S(1)} collective-permute-done((bf16[2,128,128]{2,1,0:T(8,128)(2,1)S(1)}, bf16[2,128,128]{2,1,0:T(8,128)(2,1)S(1)}, u32[]{:S(2)}, u32[]{:S(2)}) %collective-permute-start.13) | collective-permute-done | bytes 65568 | tf_op jit(solution)/shard_map/ppermute | solution.py:215
  40.1 0.8 %unpack.1 = bf16[128,1024]{1,0:T(8,128)(2,1)} custom-call(bf16[3,128,128]{2,1,0:T(8,128)(2,1)S(1)} %gather.1.direct_ref, bf16[3,128,128]{2,1,0:T(8,128)(2,1)S(1)} %collective-permute-done.11.passed_ref, bf16[2,128,128]{2,1,0:T(8,128)(2,1)S(1)} %collective-permute-done.12.refs_0_, bf16[2,128,128]{2,1,0:T(8,128)(2,1)S(1)} %collective-permute-done.13.refs_1_), custom_call_target="tpu_custom_call" | custom-call | tf_op jit(solution)/shard_map/unpack/pallas_call | solution.py:331
  (3 shorter events, 0.1 us)
Async XLA Ops:
  0.0 10.3 %collective-permute-start = (bf16[4,2,128,128]{3,2,1,0:T(8,128)(2,1)}, bf16[4,2,128,128]{3,2,1,0:T(8,128)(2,1)S(1)}, u32[]{:S(2)}, u32[]{:S(2)}) collective-permute-start(bf16[4,2,128,128]{3,2,1,0:T(8,128)(2,1)} %refs_0_.3), channel_id=1, source_target_pairs={{0,2},{1,3},{2,0},{3,1},{4,6},{5,7},{6,4},{7,5},{8,10},{9,11},{10,... | collective-permute-start | bytes 786440 | tf_op jit(solution)/shard_map/ppermute | solution.py:215
  3.0 1.1 %copy-start = (bf16[128,3072]{1,0:T(8,128)(2,1)S(1)}, bf16[128,3072]{1,0:T(8,128)(2,1)}, u32[]{:S(2)}) copy-start(bf16[128,3072]{1,0:T(8,128)(2,1)} %qkv_ref.3) | copy-start | bytes 2359300
  4.1 6.2 %copy-start.1 = (bf16[128,3072]{1,0:T(8,128)(2,1)S(1)}, bf16[128,3072]{1,0:T(8,128)(2,1)}, u32[]{:S(2)}) copy-start(bf16[128,3072]{1,0:T(8,128)(2,1)} %qkv_ref.3) | copy-start | bytes 2359300
  4.2 8.1 %collective-permute-start.1 = (bf16[3,128,128]{2,1,0:T(8,128)(2,1)S(1)}, bf16[3,128,128]{2,1,0:T(8,128)(2,1)S(1)}, u32[]{:S(2)}, u32[]{:S(2)}) collective-permute-start(bf16[3,128,128]{2,1,0:T(8,128)(2,1)S(1)} %get-tuple-element.25), channel_id=1, source_target_pairs={{0,4},{4,0},{8,12},{12,8},{16,20},{20,16},{24,28},{28,24},{1,5},{5... | collective-permute-start | bytes 294920 | tf_op jit(solution)/shard_map/ppermute | solution.py:215
  5.8 9.6 %collective-permute-start.2 = (bf16[3,128,128]{2,1,0:T(8,128)(2,1)S(1)}, bf16[3,128,128]{2,1,0:T(8,128)(2,1)S(1)}, u32[]{:S(2)}, u32[]{:S(2)}) collective-permute-start(bf16[3,128,128]{2,1,0:T(8,128)(2,1)S(1)} %get-tuple-element.26), channel_id=1, source_target_pairs={{0,8},{4,12},{8,0},{12,4},{16,24},{20,28},{24,16},{28,20},{1,9},{5... | collective-permute-start | bytes 294920 | tf_op jit(solution)/shard_map/ppermute | solution.py:215
  7.4 10.4 %collective-permute-start.4 = (bf16[3,128,128]{2,1,0:T(8,128)(2,1)S(1)}, bf16[3,128,128]{2,1,0:T(8,128)(2,1)S(1)}, u32[]{:S(2)}, u32[]{:S(2)}) collective-permute-start(bf16[3,128,128]{2,1,0:T(8,128)(2,1)S(1)} %get-tuple-element.28), channel_id=1, source_target_pairs={{0,16},{4,20},{8,24},{12,28},{16,0},{20,4},{24,8},{28,12},{1,17},{... | collective-permute-start | bytes 294920 | tf_op jit(solution)/shard_map/ppermute | solution.py:215
  10.0 6.2 %copy-start.2 = (bf16[4,2,128,128]{3,2,1,0:T(8,128)(2,1)S(1)}, bf16[4,2,128,128]{3,2,1,0:T(8,128)(2,1)}, u32[]{:S(2)}) copy-start(bf16[4,2,128,128]{3,2,1,0:T(8,128)(2,1)} %refs_0_.3) | copy-start | bytes 786436
  10.0 11.7 %collective-permute-start.5 = (bf16[3,128,128]{2,1,0:T(8,128)(2,1)S(1)}, bf16[3,128,128]{2,1,0:T(8,128)(2,1)S(1)}, u32[]{:S(2)}, u32[]{:S(2)}) collective-permute-start(bf16[3,128,128]{2,1,0:T(8,128)(2,1)S(1)} %get-tuple-element.29), channel_id=1, source_target_pairs={{0,20},{4,16},{8,28},{12,24},{16,4},{20,0},{24,12},{28,8},{1,21},{... | collective-permute-start | bytes 294920 | tf_op jit(solution)/shard_map/ppermute | solution.py:215
  10.4 5.8 %copy-start.3 = (s32[32,12]{0,1:T(8,128)S(1)}, s32[32,12]{0,1:T(8,128)}, u32[]{:S(2)}) copy-start(s32[32,12]{0,1:T(8,128)} %param.8) | copy-start | bytes 4612
  10.4 11.2 %collective-permute-start.3 = (bf16[3,128,128]{2,1,0:T(8,128)(2,1)S(1)}, bf16[3,128,128]{2,1,0:T(8,128)(2,1)S(1)}, u32[]{:S(2)}, u32[]{:S(2)}) collective-permute-start(bf16[3,128,128]{2,1,0:T(8,128)(2,1)S(1)} %get-tuple-element.27), channel_id=1, source_target_pairs={{0,12},{4,8},{8,4},{12,0},{16,28},{20,24},{24,20},{28,16},{1,13},{... | collective-permute-start | bytes 294920 | tf_op jit(solution)/shard_map/ppermute | solution.py:215
  12.4 9.2 %collective-permute-start.6 = (bf16[3,128,128]{2,1,0:T(8,128)(2,1)S(1)}, bf16[3,128,128]{2,1,0:T(8,128)(2,1)S(1)}, u32[]{:S(2)}, u32[]{:S(2)}) collective-permute-start(bf16[3,128,128]{2,1,0:T(8,128)(2,1)S(1)} %get-tuple-element.30), channel_id=1, source_target_pairs={{0,24},{4,28},{8,16},{12,20},{16,8},{20,12},{24,0},{28,4},{1,25},{... | collective-permute-start | bytes 294920 | tf_op jit(solution)/shard_map/ppermute | solution.py:215
  15.4 7.4 %collective-permute-start.7 = (bf16[3,128,128]{2,1,0:T(8,128)(2,1)S(1)}, bf16[3,128,128]{2,1,0:T(8,128)(2,1)S(1)}, u32[]{:S(2)}, u32[]{:S(2)}) collective-permute-start(bf16[3,128,128]{2,1,0:T(8,128)(2,1)S(1)} %get-tuple-element.31), channel_id=1, source_target_pairs={{0,28},{4,24},{8,20},{12,16},{16,12},{20,8},{24,4},{28,0},{1,29},{... | collective-permute-start | bytes 294920 | tf_op jit(solution)/shard_map/ppermute | solution.py:215
  16.2 0.7 %copy-start.4 = (s32[32,2]{0,1:T(2,128)S(1)}, s32[32,2]{0,1:T(2,128)}, u32[]{:S(2)}) copy-start(s32[32,2]{0,1:T(2,128)} %param.7) | copy-start | bytes 772
  16.2 0.7 %copy-start.5 = (s32[32]{0:T(128)S(1)}, s32[32]{0:T(128)}, u32[]{:S(2)}) copy-start(s32[32]{0:T(128)} %param.9) | copy-start | bytes 388
  17.7 5.1 %collective-permute-start.8 = (bf16[2,4,2,128,128]{4,3,2,1,0:T(8,128)(2,1)S(1)}, bf16[2,4,2,128,128]{4,3,2,1,0:T(8,128)(2,1)S(1)}, u32[]{:S(2)}, u32[]{:S(2)}) collective-permute-start(bf16[2,4,2,128,128]{4,3,2,1,0:T(8,128)(2,1)S(1)} %get-tuple-element.32), channel_id=1, source_target_pairs={{0,1},{1,0},{2,3},{3,2},{4,5},{5,4},{6,7},{7,6},{8,9},{9,8},{10,11... | collective-permute-start | bytes 1572872 | tf_op jit(solution)/shard_map/ppermute | solution.py:215
  26.3 7.0 %collective-permute-start.11 = (bf16[3,128,128]{2,1,0:T(8,128)(2,1)S(1)}, bf16[3,128,128]{2,1,0:T(8,128)(2,1)S(1)}, u32[]{:S(2)}, u32[]{:S(2)}) collective-permute-start(bf16[3,128,128]{2,1,0:T(8,128)(2,1)S(1)} %get-tuple-element.36), channel_id=1, source_target_pairs={{0,4},{4,0},{8,12},{12,8},{16,20},{20,16},{24,28},{28,24},{1,5},{5... | collective-permute-start | bytes 294920 | tf_op jit(solution)/shard_map/ppermute | solution.py:215
  28.5 8.6 %collective-permute-start.9 = (bf16[128,128]{1,0:T(8,128)(2,1)S(1)}, bf16[128,128]{1,0:T(8,128)(2,1)S(1)}, u32[]{:S(2)}, u32[]{:S(2)}) collective-permute-start(bf16[128,128]{1,0:T(8,128)(2,1)S(1)} %get-tuple-element.34), channel_id=1, source_target_pairs={{0,20},{4,16},{8,28},{12,24},{16,4},{20,0},{24,12},{28,8},{1,21},{... | collective-permute-start | bytes 98312 | tf_op jit(solution)/shard_map/ppermute | solution.py:215
  33.3 4.8 %collective-permute-start.10 = (bf16[128,128]{1,0:T(8,128)(2,1)S(1)}, bf16[128,128]{1,0:T(8,128)(2,1)S(1)}, u32[]{:S(2)}, u32[]{:S(2)}) collective-permute-start(bf16[128,128]{1,0:T(8,128)(2,1)S(1)} %get-tuple-element.35), channel_id=1, source_target_pairs={{0,16},{4,20},{8,24},{12,28},{16,0},{20,4},{24,8},{28,12},{1,17},{... | collective-permute-start | bytes 98312 | tf_op jit(solution)/shard_map/ppermute | solution.py:215
  33.3 6.2 %collective-permute-start.12 = (bf16[2,128,128]{2,1,0:T(8,128)(2,1)S(1)}, bf16[2,128,128]{2,1,0:T(8,128)(2,1)S(1)}, u32[]{:S(2)}, u32[]{:S(2)}) collective-permute-start(bf16[2,128,128]{2,1,0:T(8,128)(2,1)S(1)} %get-tuple-element.39), channel_id=1, source_target_pairs={{0,24},{4,28},{8,16},{12,20},{16,8},{20,12},{24,0},{28,4},{1,25},{... | collective-permute-start | bytes 196616 | tf_op jit(solution)/shard_map/ppermute | solution.py:215
  35.1 5.0 %collective-permute-start.13 = (bf16[2,128,128]{2,1,0:T(8,128)(2,1)S(1)}, bf16[2,128,128]{2,1,0:T(8,128)(2,1)S(1)}, u32[]{:S(2)}, u32[]{:S(2)}) collective-permute-start(bf16[2,128,128]{2,1,0:T(8,128)(2,1)S(1)} %get-tuple-element.40), channel_id=1, source_target_pairs={{0,8},{4,12},{8,0},{12,4},{16,24},{20,28},{24,16},{28,20},{1,9},{5... | collective-permute-start | bytes 196616 | tf_op jit(solution)/shard_map/ppermute | solution.py:215

commit v6 on v5

--- a/solution.py
+++ b/solution.py
@@ -14,7 +14,7 @@
 EARLY = 4
 GROUP = 8
 COLLECT_FLOPS = 10**10
-GATHER_FLOPS = 10**10
+FIRST_FLOPS = 10**10
 VMEM_BYTES = 40 * 1024 * 1024
 
 
@@ -47,10 +47,9 @@
             lists_ref[at, i : i + 1] = jnp.full((1, lists_ref.shape[2]), entry, jnp.int32)
 
 
-def collect_kernel(*refs):
-    spans, out_ref = refs[:-1], refs[-1]
-    for step, span in enumerate(spans):
-        out_ref[step] = span[1:]
+def collect_kernel(order, *refs):
+    for step, span in zip(order, refs):
+        refs[-1][step] = span[1:]
 
 
 def order_kernel(blk_count, *refs):
@@ -71,25 +70,28 @@
         refs[count + i][1] = passed_ref[1 + i]
 
 
-def gather_kernel(*refs):
-    for i, ref in enumerate(refs[:-1]):
-        refs[-1][i] = ref[...]
-
-
-def unpack_kernel(sources, direct, paired, direct_ref, passed_ref, *refs):
-    paired_refs, out_ref = refs[:-1], refs[-1]
-    width = passed_ref.shape[2]
+def write_columns(tiles, out_ref, sems):
     me = lax.axis_index("seq")
-
-    def put(step, part):
-        out_ref[:, pl.ds(pl.multiple_of((me ^ step) * width, width), width)] = part
-
-    for i, step in enumerate(direct):
-        put(step, direct_ref[i])
-    put(1, passed_ref[0])
-    for step, ref in zip(paired, paired_refs):
-        put(step, ref[0])
-        put(step + 1, ref[1])
+    copies = []
+    for i, (step, tile) in enumerate(tiles):
+        width = tile.shape[1]
+        columns = pl.ds(pl.multiple_of((me ^ step) * width, width), width)
+        copies.append(pltpu.make_async_copy(tile, out_ref.at[:, columns], sems.at[i]))
+        copies[-1].start()
+    for copy in copies:
+        copy.wait()
+
+
+def first_kernel(direct, passed_ref, *refs):
+    tiles = [(1, passed_ref.at[0]), *zip(direct, refs[:-2])]
+    write_columns(tiles, refs[-2], refs[-1])
+
+
+def last_kernel(paired, begun_ref, *refs):
+    tiles = []
+    for step, ref in zip(paired, refs[:-2]):
+        tiles += [(step, ref.at[0]), (step + 1, ref.at[1])]
+    write_columns(tiles, refs[-2], refs[-1])
 
 
 def stack(pieces):
@@ -217,7 +219,7 @@
 
 def sending_order(count):
     near, far = list(range(1, count // 2)), list(range(count // 2, count))
-    return near[:1] + far[:1] + near[1:2] + far[1:] + near[2:]
+    return near[:1] + far[:1] + near[1:2] + far[1:2] + near[2:] + far[2:]
 
 
 def per_device(qkv, kept_kv, cur_list, kept_list, kept_count):
@@ -235,7 +237,8 @@
     kepts = [swap(kept_kv, "blk", step) for step in range(0, blk_count, 2)]
     order = sending_order(seq_count)
     spans = [None] * seq_count
-    for steps, before in (([0, *order[:EARLY]], []), (order[EARLY:], kepts[1:])):
+    for steps in ([0, *order[:EARLY]], order[EARLY:]):
+        before = [] if 0 in steps else [*kepts[1:], spans[order[0]]]
         packed = pl.pallas_call(
             functools.partial(pack_kernel, steps, seq_count),
             out_shape=[jax.ShapeDtypeStruct((3, tok_rows, width), dtype)] * len(steps),
@@ -272,14 +275,14 @@
         name="order",
     )(*kepts)
     span = pl.pallas_call(
-        collect_kernel,
+        functools.partial(collect_kernel, [0, *order]),
         out_shape=jax.ShapeDtypeStruct((seq_count, 2, tok_rows, width), dtype),
         in_specs=[vmem] * seq_count,
         out_specs=vmem,
         compiler_params=params,
         cost_estimate=pl.CostEstimate(flops=COLLECT_FLOPS, bytes_accessed=0, transcendentals=0),
         name="collect",
-    )(*spans)
+    )(*[spans[step] for step in [0, *order]])
 
     half = seq_count // 2
     direct = [0, half + 1, half]
@@ -319,23 +322,27 @@
         name="relay",
     )(sent, *outs[len(direct):])
     relayed = [swap(buffer, "seq", step) for buffer, step in zip(relayed, paired)]
-    gathered = pl.pallas_call(
-        gather_kernel,
-        out_shape=jax.ShapeDtypeStruct((len(direct), tok_rows, width), dtype),
-        in_specs=[vmem] * len(direct),
-        out_specs=vmem,
-        compiler_params=params,
-        cost_estimate=pl.CostEstimate(flops=GATHER_FLOPS, bytes_accessed=0, transcendentals=0),
-        name="gather",
-    )(*outs[: len(direct)])
+    whole = jax.ShapeDtypeStruct((tok_rows, seq_count * width), dtype)
+    begun = pl.pallas_call(
+        functools.partial(first_kernel, direct),
+        out_shape=whole,
+        in_specs=[vmem] * (1 + len(direct)),
+        out_specs=anywhere,
+        scratch_shapes=[pltpu.SemaphoreType.DMA((1 + len(direct),))],
+        compiler_params=params,
+        cost_estimate=pl.CostEstimate(flops=FIRST_FLOPS, bytes_accessed=0, transcendentals=0),
+        name="first",
+    )(sent, *outs[: len(direct)])
     return pl.pallas_call(
-        functools.partial(unpack_kernel, seq_count, direct, paired),
-        out_shape=jax.ShapeDtypeStruct((tok_rows, seq_count * width), dtype),
-        in_specs=[vmem] * (2 + len(paired)),
-        out_specs=vmem,
-        compiler_params=params,
-        name="unpack",
-    )(gathered, sent, *relayed)
+        functools.partial(last_kernel, paired),
+        out_shape=whole,
+        in_specs=[anywhere] + [vmem] * len(paired),
+        out_specs=anywhere,
+        scratch_shapes=[pltpu.SemaphoreType.DMA((2 * len(paired),))],
+        compiler_params=params,
+        input_output_aliases={0: 0},
+        name="last",
+    )(begun, *relayed)
 
 
 def solution(mesh):

time: 40.8 us -> 39.6 us (0.971); the launches traced: 40.8 us -> 39.2 us
  waiting for transfers between devices: 7.93 us -> 5.12 us
  starting transfers between devices: 25.6 us -> 27.4 us
  Pallas kernels: 5.35 us -> 4.68 us
    ppermute x14, waiting for transfers between devices: 7.93 us -> 5.12 us  [swap(): return lax.ppermute(array, axis, [(i, i ^ step) for i in range(count)])]
    ppermute x14, starting transfers between devices: 25.6 us -> 27.4 us  [swap(): return lax.ppermute(array, axis, [(i, i ^ step) for i in range(count)])]
    pallas_call x1, Pallas kernels: 3.37 us -> 2.11 us  [per_device(): pl.pallas_call(functools.partial(attention_kernel, places, tile_len, near...]
    pallas_call x3, Pallas kernels: 0.82 us -> 1.4 us  [the longest x1 0.68 us: per_device(): pl.pallas_call(functools.partial(first_kernel, direct), out_shape=whole,...]
  transfers between devices with their start and end apart: 14 -> 14, of which waited for: 5 -> 5; matrix products, arithmetic and copies ran while one was open for 0% -> 0% of each run, Pallas kernels for 3% -> 5%
where the time goes in v6:
time: 39.6 us; the launch traced here: 39.2 us
  starting transfers between devices  27.4 us (69%)
  waiting for transfers between devices  5.12 us (13%)
  Pallas kernels  4.68 us (12%)
  local copies, waits for them, and re-layouts  1.82 us (5%)
    ppermute x14, starting transfers between devices, swap(): return lax.ppermute(array, axis, [(i, i ^ step) for i in range(count)])  27.4 us
    ppermute x14, waiting for transfers between devices, swap(): return lax.ppermute(array, axis, [(i, i ^ step) for i in range(count)])  5.12 us
    pallas_call x1, Pallas kernels, per_device(): pl.pallas_call(functools.partial(attention_kernel, places, tile_len, near...  2.11 us
    unnamed x12, local copies, waits for them, and re-layouts  1.82 us
    pallas_call x1, Pallas kernels, per_device(): pl.pallas_call(functools.partial(merge_kernel, len(kepts), blk_count, til...  0.87 us
  transfers between devices with their start and end apart: 14, of which 5 were waited for; matrix products, arithmetic and copies ran while one was open for 0% of the time, Pallas kernels for 5%

profile of v6, /device:TPU:0, one launch (start us, length us, event | category | flops | bytes accessed | tf_op | source)
XLA Modules:
  0.0 39.2 jit_solution(5698101368144844526)
XLA Ops:
  0.0 3.0 %collective-permute-start = (bf16[4,2,128,128]{3,2,1,0:T(8,128)(2,1)}, bf16[4,2,128,128]{3,2,1,0:T(8,128)(2,1)S(1)}, u32[]{:S(2)}, u32[]{:S(2)}) collective-permute-start(bf16[4,2,128,128]{3,2,1,0:T(8,128)(2,1)} %refs_0_.3), channel_id=1, source_target_pairs={{0,2},{1,3},{2,0},{3,1},{4,6},{5,7},{6,4},{7,5},{8,10},{9,11},{10,... | collective-permute-start | bytes 786440 | tf_op jit(solution)/shard_map/ppermute | solution.py:217
  3.0 0.0 copy-start
  3.0 1.1 %copy-done = bf16[128,3072]{1,0:T(8,128)(2,1)S(1)} copy-done((bf16[128,3072]{1,0:T(8,128)(2,1)S(1)}, bf16[128,3072]{1,0:T(8,128)(2,1)}, u32[]{:S(2)}) %copy-start) | copy-done | bytes 786456
  4.1 0.0 copy-start.1
  4.1 0.1 pack.2
  4.2 1.6 %collective-permute-start.1 = (bf16[3,128,128]{2,1,0:T(8,128)(2,1)S(1)}, bf16[3,128,128]{2,1,0:T(8,128)(2,1)S(1)}, u32[]{:S(2)}, u32[]{:S(2)}) collective-permute-start(bf16[3,128,128]{2,1,0:T(8,128)(2,1)S(1)} %get-tuple-element.25), channel_id=1, source_target_pairs={{0,4},{4,0},{8,12},{12,8},{16,20},{20,16},{24,28},{28,24},{1,5},{5... | collective-permute-start | bytes 294920 | tf_op jit(solution)/shard_map/ppermute | solution.py:217
  5.8 2.6 %collective-permute-start.2 = (bf16[3,128,128]{2,1,0:T(8,128)(2,1)S(1)}, bf16[3,128,128]{2,1,0:T(8,128)(2,1)S(1)}, u32[]{:S(2)}, u32[]{:S(2)}) collective-permute-start(bf16[3,128,128]{2,1,0:T(8,128)(2,1)S(1)} %get-tuple-element.26), channel_id=1, source_target_pairs={{0,16},{4,20},{8,24},{12,28},{16,0},{20,4},{24,8},{28,12},{1,17},{... | collective-permute-start | bytes 294920 | tf_op jit(solution)/shard_map/ppermute | solution.py:217
  8.4 1.6 %collective-permute-start.3 = (bf16[3,128,128]{2,1,0:T(8,128)(2,1)S(1)}, bf16[3,128,128]{2,1,0:T(8,128)(2,1)S(1)}, u32[]{:S(2)}, u32[]{:S(2)}) collective-permute-start(bf16[3,128,128]{2,1,0:T(8,128)(2,1)S(1)} %get-tuple-element.27), channel_id=1, source_target_pairs={{0,8},{4,12},{8,0},{12,4},{16,24},{20,28},{24,16},{28,20},{1,9},{5... | collective-permute-start | bytes 294920 | tf_op jit(solution)/shard_map/ppermute | solution.py:217
  10.0 0.0 copy-start.2
  10.0 0.3 collective-permute-start.4
  10.3 0.0 collective-permute-done.1.refs_1_
  10.3 0.0 collective-permute-done.refs_1_.refs_0_
  10.3 0.0 copy-done.1
  10.3 0.1 pack.3
  10.4 0.0 copy-start.3
  10.4 2.0 %collective-permute-start.5 = (bf16[3,128,128]{2,1,0:T(8,128)(2,1)S(1)}, bf16[3,128,128]{2,1,0:T(8,128)(2,1)S(1)}, u32[]{:S(2)}, u32[]{:S(2)}) collective-permute-start(bf16[3,128,128]{2,1,0:T(8,128)(2,1)S(1)} %get-tuple-element.29), channel_id=1, source_target_pairs={{0,12},{4,8},{8,4},{12,0},{16,28},{20,24},{24,20},{28,16},{1,13},{... | collective-permute-start | bytes 294920 | tf_op jit(solution)/shard_map/ppermute | solution.py:217
  12.4 3.1 %collective-permute-start.6 = (bf16[3,128,128]{2,1,0:T(8,128)(2,1)S(1)}, bf16[3,128,128]{2,1,0:T(8,128)(2,1)S(1)}, u32[]{:S(2)}, u32[]{:S(2)}) collective-permute-start(bf16[3,128,128]{2,1,0:T(8,128)(2,1)S(1)} %get-tuple-element.30), channel_id=1, source_target_pairs={{0,24},{4,28},{8,16},{12,20},{16,8},{20,12},{24,0},{28,4},{1,25},{... | collective-permute-start | bytes 294920 | tf_op jit(solution)/shard_map/ppermute | solution.py:217
  15.4 0.0 collective-permute-done.2.refs_2_.refs_4_
  15.4 2.9 %collective-permute-start.7 = (bf16[3,128,128]{2,1,0:T(8,128)(2,1)S(1)}, bf16[3,128,128]{2,1,0:T(8,128)(2,1)S(1)}, u32[]{:S(2)}, u32[]{:S(2)}) collective-permute-start(bf16[3,128,128]{2,1,0:T(8,128)(2,1)S(1)} %get-tuple-element.31), channel_id=1, source_target_pairs={{0,28},{4,24},{8,20},{12,16},{16,12},{20,8},{24,4},{28,0},{1,29},{... | collective-permute-start | bytes 294920 | tf_op jit(solution)/shard_map/ppermute | solution.py:217
  18.3 0.0 copy-start.4
  18.3 0.0 copy-start.5
  18.3 0.0 copy-done.2
  18.4 0.0 copy-done.3
  18.4 0.7 %copy-done.4 = s32[32,2]{0,1:T(2,128)S(1)} copy-done((s32[32,2]{0,1:T(2,128)S(1)}, s32[32,2]{0,1:T(2,128)}, u32[]{:S(2)}) %copy-start.4) | copy-done | bytes 280
  19.0 0.0 copy-done.5
  19.0 0.9 %merge.1 = (bf16[2,4,2,128,128]{4,3,2,1,0:T(8,128)(2,1)S(1)}, s32[8,17,128]{2,1,0:T(8,128)S(1)}) custom-call(bf16[4,2,128,128]{3,2,1,0:T(8,128)(2,1)S(1)} %copy-done.2, bf16[4,2,128,128]{3,2,1,0:T(8,128)(2,1)S(1)} %collective-permute-done.refs_1_.refs_0_, s32[2,32]{1,0:T(2,128)S(1)} %bitcast.4, s32[12,32]{1,0:T(8,128)S(1)} %bitcast.3, s32[1,32]{1,0:T(1,128)S(1)} %bitcast.5), custom_call_target="tpu_custom_call" | custom-call | tf_op jit(solution)/shard_map/merge/pallas_call | solution.py:254
  19.9 0.0 collective-permute-done.3.refs_3_.refs_2_
  19.9 0.1 collective-permute-start.8
  20.0 1.7 %collective-permute-done.4.refs_4_.refs_5_ = bf16[3,128,128]{2,1,0:T(8,128)(2,1)S(1)} collective-permute-done((bf16[3,128,128]{2,1,0:T(8,128)(2,1)S(1)}, bf16[3,128,128]{2,1,0:T(8,128)(2,1)S(1)}, u32[]{:S(2)}, u32[]{:S(2)}) %collective-permute-start.4) | collective-permute-done | bytes 98336 | tf_op jit(solution)/shard_map/ppermute | solution.py:217
  21.7 0.0 collective-permute-done.5.refs_5_.refs_3_
  21.7 0.0 collective-permute-done.6.refs_6_
  21.7 1.2 %collective-permute-done.7.refs_7_ = bf16[3,128,128]{2,1,0:T(8,128)(2,1)S(1)} collective-permute-done((bf16[3,128,128]{2,1,0:T(8,128)(2,1)S(1)}, bf16[3,128,128]{2,1,0:T(8,128)(2,1)S(1)}, u32[]{:S(2)}, u32[]{:S(2)}) %collective-permute-start.7) | collective-permute-done | bytes 98336 | tf_op jit(solution)/shard_map/ppermute | solution.py:217
  22.9 0.0 collective-permute-done.8.refs_2_
  22.9 0.1 order.1.kept_ref
  23.0 2.1 %attention.1 = (bf16[3,128,128]{2,1,0:T(8,128)(2,1)S(1)}, bf16[128,128]{1,0:T(8,128)(2,1)S(1)}, bf16[128,128]{1,0:T(8,128)(2,1)S(1)}, bf16[128,128]{1,0:T(8,128)...) custom-call(s32[8,17,128]{2,1,0:T(8,128)S(1)} %get-tuple-element.23.lists_ref, ...), custom_call_target="tpu_custom_call" | custom-call | tf_op jit(solution)/shard_map/attention/pallas_call | solution.py:300
  25.1 1.0 %collective-permute-start.9 = (bf16[3,128,128]{2,1,0:T(8,128)(2,1)S(1)}, bf16[3,128,128]{2,1,0:T(8,128)(2,1)S(1)}, u32[]{:S(2)}, u32[]{:S(2)}) collective-permute-start(bf16[3,128,128]{2,1,0:T(8,128)(2,1)S(1)} %get-tuple-element.33), channel_id=1, source_target_pairs={{0,4},{4,0},{8,12},{12,8},{16,20},{20,16},{24,28},{28,24},{1,5},{5... | collective-permute-start | bytes 294920 | tf_op jit(solution)/shard_map/ppermute | solution.py:217
  26.1 5.7 %collective-permute-start.10 = (bf16[128,128]{1,0:T(8,128)(2,1)S(1)}, bf16[128,128]{1,0:T(8,128)(2,1)S(1)}, u32[]{:S(2)}, u32[]{:S(2)}) collective-permute-start(bf16[128,128]{1,0:T(8,128)(2,1)S(1)} %get-tuple-element.35), channel_id=1, source_target_pairs={{0,20},{4,16},{8,28},{12,24},{16,4},{20,0},{24,12},{28,8},{1,21},{... | collective-permute-start | bytes 98312 | tf_op jit(solution)/shard_map/ppermute | solution.py:217
  31.8 0.0 collective-permute-start.11
  31.8 0.0 collective-permute-done.9.passed_ref
  31.8 1.4 %collective-permute-start.12 = (bf16[2,128,128]{2,1,0:T(8,128)(2,1)S(1)}, bf16[2,128,128]{2,1,0:T(8,128)(2,1)S(1)}, u32[]{:S(2)}, u32[]{:S(2)}) collective-permute-start(bf16[2,128,128]{2,1,0:T(8,128)(2,1)S(1)} %get-tuple-element.39), channel_id=1, source_target_pairs={{0,24},{4,28},{8,16},{12,20},{16,8},{20,12},{24,0},{28,4},{1,25},{... | collective-permute-start | bytes 196616 | tf_op jit(solution)/shard_map/ppermute | solution.py:217
  33.2 2.4 %collective-permute-start.13 = (bf16[2,128,128]{2,1,0:T(8,128)(2,1)S(1)}, bf16[2,128,128]{2,1,0:T(8,128)(2,1)S(1)}, u32[]{:S(2)}, u32[]{:S(2)}) collective-permute-start(bf16[2,128,128]{2,1,0:T(8,128)(2,1)S(1)} %get-tuple-element.40), channel_id=1, source_target_pairs={{0,8},{4,12},{8,0},{12,4},{16,24},{20,28},{24,16},{28,20},{1,9},{5... | collective-permute-start | bytes 196616 | tf_op jit(solution)/shard_map/ppermute | solution.py:217
  35.6 0.0 collective-permute-done.10.refs_1_
  35.6 1.2 %collective-permute-done.11.refs_2_ = bf16[128,128]{1,0:T(8,128)(2,1)S(1)} collective-permute-done((bf16[128,128]{1,0:T(8,128)(2,1)S(1)}, bf16[128,128]{1,0:T(8,128)(2,1)S(1)}, u32[]{:S(2)}, u32[]{:S(2)}) %collective-permute-start.11) | collective-permute-done | bytes 32800 | tf_op jit(solution)/shard_map/ppermute | solution.py:217
  36.7 0.7 %first.1.begun_ref = bf16[128,1024]{1,0:T(8,128)(2,1)} custom-call(bf16[3,128,128]{2,1,0:T(8,128)(2,1)S(1)} %collective-permute-done.9.passed_ref, bf16[128,128]{1,0:T(8,128)(2,1)S(1)} %get-tuple-element.34.refs_0_, bf16[128,128]{1,0:T(8,128)(2,1)S(1)} %collective-permute-done.10.refs_1_, bf16[128,128]{1,0:T(8,128)(2,1)S(1)} %collective-permute-done.11.refs_2_), custom_call_target="tpu_custom_call" | custom-call | flops 10000000000 | tf_op jit(solution)/shard_map/first/pallas_call | solution.py:326
  37.4 0.7 %collective-permute-done.12.refs_0_ = bf16[2,128,128]{2,1,0:T(8,128)(2,1)S(1)} collective-permute-done((bf16[2,128,128]{2,1,0:T(8,128)(2,1)S(1)}, bf16[2,128,128]{2,1,0:T(8,128)(2,1)S(1)}, u32[]{:S(2)}, u32[]{:S(2)}) %collective-permute-start.12) | collective-permute-done | bytes 65568 | tf_op jit(solution)/shard_map/ppermute | solution.py:217
  38.1 0.4 %collective-permute-done.13.refs_1_ = bf16[2,128,128]{2,1,0:T(8,128)(2,1)S(1)} collective-permute-done((bf16[2,128,128]{2,1,0:T(8,128)(2,1)S(1)}, bf16[2,128,128]{2,1,0:T(8,128)(2,1)S(1)}, u32[]{:S(2)}, u32[]{:S(2)}) %collective-permute-start.13) | collective-permute-done | bytes 65568 | tf_op jit(solution)/shard_map/ppermute | solution.py:217
  38.5 0.7 %last.1 = bf16[128,1024]{1,0:T(8,128)(2,1)} custom-call(bf16[128,1024]{1,0:T(8,128)(2,1)} %first.1.begun_ref, bf16[2,128,128]{2,1,0:T(8,128)(2,1)S(1)} %collective-permute-done.12.refs_0_, bf16[2,128,128]{2,1,0:T(8,128)(2,1)S(1)} %collective-permute-done.13.refs_1_), custom_call_target="tpu_custom_call", output_to_operand_aliasing={{}: (0, {})} | custom-call | tf_op jit(solution)/shard_map/last/pallas_call | solution.py:336
  (2 shorter events, 0.0 us)
Async XLA Ops:
  0.0 10.3 %collective-permute-start = (bf16[4,2,128,128]{3,2,1,0:T(8,128)(2,1)}, bf16[4,2,128,128]{3,2,1,0:T(8,128)(2,1)S(1)}, u32[]{:S(2)}, u32[]{:S(2)}) collective-permute-start(bf16[4,2,128,128]{3,2,1,0:T(8,128)(2,1)} %refs_0_.3), channel_id=1, source_target_pairs={{0,2},{1,3},{2,0},{3,1},{4,6},{5,7},{6,4},{7,5},{8,10},{9,11},{10,... | collective-permute-start | bytes 786440 | tf_op jit(solution)/shard_map/ppermute | solution.py:217
  3.0 1.1 %copy-start = (bf16[128,3072]{1,0:T(8,128)(2,1)S(1)}, bf16[128,3072]{1,0:T(8,128)(2,1)}, u32[]{:S(2)}) copy-start(bf16[128,3072]{1,0:T(8,128)(2,1)} %qkv_ref.3) | copy-start | bytes 2359300
  4.1 6.2 %copy-start.1 = (bf16[128,3072]{1,0:T(8,128)(2,1)S(1)}, bf16[128,3072]{1,0:T(8,128)(2,1)}, u32[]{:S(2)}) copy-start(bf16[128,3072]{1,0:T(8,128)(2,1)} %qkv_ref.3) | copy-start | bytes 2359300
  4.2 6.0 %collective-permute-start.1 = (bf16[3,128,128]{2,1,0:T(8,128)(2,1)S(1)}, bf16[3,128,128]{2,1,0:T(8,128)(2,1)S(1)}, u32[]{:S(2)}, u32[]{:S(2)}) collective-permute-start(bf16[3,128,128]{2,1,0:T(8,128)(2,1)S(1)} %get-tuple-element.25), channel_id=1, source_target_pairs={{0,4},{4,0},{8,12},{12,8},{16,20},{20,16},{24,28},{28,24},{1,5},{5... | collective-permute-start | bytes 294920 | tf_op jit(solution)/shard_map/ppermute | solution.py:217
  5.8 9.6 %collective-permute-start.2 = (bf16[3,128,128]{2,1,0:T(8,128)(2,1)S(1)}, bf16[3,128,128]{2,1,0:T(8,128)(2,1)S(1)}, u32[]{:S(2)}, u32[]{:S(2)}) collective-permute-start(bf16[3,128,128]{2,1,0:T(8,128)(2,1)S(1)} %get-tuple-element.26), channel_id=1, source_target_pairs={{0,16},{4,20},{8,24},{12,28},{16,0},{20,4},{24,8},{28,12},{1,17},{... | collective-permute-start | bytes 294920 | tf_op jit(solution)/shard_map/ppermute | solution.py:217
  8.4 11.5 %collective-permute-start.3 = (bf16[3,128,128]{2,1,0:T(8,128)(2,1)S(1)}, bf16[3,128,128]{2,1,0:T(8,128)(2,1)S(1)}, u32[]{:S(2)}, u32[]{:S(2)}) collective-permute-start(bf16[3,128,128]{2,1,0:T(8,128)(2,1)S(1)} %get-tuple-element.27), channel_id=1, source_target_pairs={{0,8},{4,12},{8,0},{12,4},{16,24},{20,28},{24,16},{28,20},{1,9},{5... | collective-permute-start | bytes 294920 | tf_op jit(solution)/shard_map/ppermute | solution.py:217
  10.0 8.4 %copy-start.2 = (bf16[4,2,128,128]{3,2,1,0:T(8,128)(2,1)S(1)}, bf16[4,2,128,128]{3,2,1,0:T(8,128)(2,1)}, u32[]{:S(2)}) copy-start(bf16[4,2,128,128]{3,2,1,0:T(8,128)(2,1)} %refs_0_.3) | copy-start | bytes 786436
  10.0 11.7 %collective-permute-start.4 = (bf16[3,128,128]{2,1,0:T(8,128)(2,1)S(1)}, bf16[3,128,128]{2,1,0:T(8,128)(2,1)S(1)}, u32[]{:S(2)}, u32[]{:S(2)}) collective-permute-start(bf16[3,128,128]{2,1,0:T(8,128)(2,1)S(1)} %get-tuple-element.28), channel_id=1, source_target_pairs={{0,20},{4,16},{8,28},{12,24},{16,4},{20,0},{24,12},{28,8},{1,21},{... | collective-permute-start | bytes 294920 | tf_op jit(solution)/shard_map/ppermute | solution.py:217
  10.4 8.0 %copy-start.3 = (s32[32,12]{0,1:T(8,128)S(1)}, s32[32,12]{0,1:T(8,128)}, u32[]{:S(2)}) copy-start(s32[32,12]{0,1:T(8,128)} %param.8) | copy-start | bytes 4612
  10.4 11.3 %collective-permute-start.5 = (bf16[3,128,128]{2,1,0:T(8,128)(2,1)S(1)}, bf16[3,128,128]{2,1,0:T(8,128)(2,1)S(1)}, u32[]{:S(2)}, u32[]{:S(2)}) collective-permute-start(bf16[3,128,128]{2,1,0:T(8,128)(2,1)S(1)} %get-tuple-element.29), channel_id=1, source_target_pairs={{0,12},{4,8},{8,4},{12,0},{16,28},{20,24},{24,20},{28,16},{1,13},{... | collective-permute-start | bytes 294920 | tf_op jit(solution)/shard_map/ppermute | solution.py:217
  12.4 9.3 %collective-permute-start.6 = (bf16[3,128,128]{2,1,0:T(8,128)(2,1)S(1)}, bf16[3,128,128]{2,1,0:T(8,128)(2,1)S(1)}, u32[]{:S(2)}, u32[]{:S(2)}) collective-permute-start(bf16[3,128,128]{2,1,0:T(8,128)(2,1)S(1)} %get-tuple-element.30), channel_id=1, source_target_pairs={{0,24},{4,28},{8,16},{12,20},{16,8},{20,12},{24,0},{28,4},{1,25},{... | collective-permute-start | bytes 294920 | tf_op jit(solution)/shard_map/ppermute | solution.py:217
  15.4 7.4 %collective-permute-start.7 = (bf16[3,128,128]{2,1,0:T(8,128)(2,1)S(1)}, bf16[3,128,128]{2,1,0:T(8,128)(2,1)S(1)}, u32[]{:S(2)}, u32[]{:S(2)}) collective-permute-start(bf16[3,128,128]{2,1,0:T(8,128)(2,1)S(1)} %get-tuple-element.31), channel_id=1, source_target_pairs={{0,28},{4,24},{8,20},{12,16},{16,12},{20,8},{24,4},{28,0},{1,29},{... | collective-permute-start | bytes 294920 | tf_op jit(solution)/shard_map/ppermute | solution.py:217
  18.3 0.7 %copy-start.4 = (s32[32,2]{0,1:T(2,128)S(1)}, s32[32,2]{0,1:T(2,128)}, u32[]{:S(2)}) copy-start(s32[32,2]{0,1:T(2,128)} %param.7) | copy-start | bytes 772
  18.3 0.7 %copy-start.5 = (s32[32]{0:T(128)S(1)}, s32[32]{0:T(128)}, u32[]{:S(2)}) copy-start(s32[32]{0:T(128)} %param.9) | copy-start | bytes 388
  19.9 3.0 %collective-permute-start.8 = (bf16[2,4,2,128,128]{4,3,2,1,0:T(8,128)(2,1)S(1)}, bf16[2,4,2,128,128]{4,3,2,1,0:T(8,128)(2,1)S(1)}, u32[]{:S(2)}, u32[]{:S(2)}) collective-permute-start(bf16[2,4,2,128,128]{4,3,2,1,0:T(8,128)(2,1)S(1)} %get-tuple-element.32), channel_id=1, source_target_pairs={{0,1},{1,0},{2,3},{3,2},{4,5},{5,4},{6,7},{7,6},{8,9},{9,8},{10,11... | collective-permute-start | bytes 1572872 | tf_op jit(solution)/shard_map/ppermute | solution.py:217
  25.1 6.7 %collective-permute-start.9 = (bf16[3,128,128]{2,1,0:T(8,128)(2,1)S(1)}, bf16[3,128,128]{2,1,0:T(8,128)(2,1)S(1)}, u32[]{:S(2)}, u32[]{:S(2)}) collective-permute-start(bf16[3,128,128]{2,1,0:T(8,128)(2,1)S(1)} %get-tuple-element.33), channel_id=1, source_target_pairs={{0,4},{4,0},{8,12},{12,8},{16,20},{20,16},{24,28},{28,24},{1,5},{5... | collective-permute-start | bytes 294920 | tf_op jit(solution)/shard_map/ppermute | solution.py:217
  26.1 9.5 %collective-permute-start.10 = (bf16[128,128]{1,0:T(8,128)(2,1)S(1)}, bf16[128,128]{1,0:T(8,128)(2,1)S(1)}, u32[]{:S(2)}, u32[]{:S(2)}) collective-permute-start(bf16[128,128]{1,0:T(8,128)(2,1)S(1)} %get-tuple-element.35), channel_id=1, source_target_pairs={{0,20},{4,16},{8,28},{12,24},{16,4},{20,0},{24,12},{28,8},{1,21},{... | collective-permute-start | bytes 98312 | tf_op jit(solution)/shard_map/ppermute | solution.py:217
  31.8 5.0 %collective-permute-start.11 = (bf16[128,128]{1,0:T(8,128)(2,1)S(1)}, bf16[128,128]{1,0:T(8,128)(2,1)S(1)}, u32[]{:S(2)}, u32[]{:S(2)}) collective-permute-start(bf16[128,128]{1,0:T(8,128)(2,1)S(1)} %get-tuple-element.36), channel_id=1, source_target_pairs={{0,16},{4,20},{8,24},{12,28},{16,0},{20,4},{24,8},{28,12},{1,17},{... | collective-permute-start | bytes 98312 | tf_op jit(solution)/shard_map/ppermute | solution.py:217
  31.8 6.3 %collective-permute-start.12 = (bf16[2,128,128]{2,1,0:T(8,128)(2,1)S(1)}, bf16[2,128,128]{2,1,0:T(8,128)(2,1)S(1)}, u32[]{:S(2)}, u32[]{:S(2)}) collective-permute-start(bf16[2,128,128]{2,1,0:T(8,128)(2,1)S(1)} %get-tuple-element.39), channel_id=1, source_target_pairs={{0,24},{4,28},{8,16},{12,20},{16,8},{20,12},{24,0},{28,4},{1,25},{... | collective-permute-start | bytes 196616 | tf_op jit(solution)/shard_map/ppermute | solution.py:217
  33.2 5.3 %collective-permute-start.13 = (bf16[2,128,128]{2,1,0:T(8,128)(2,1)S(1)}, bf16[2,128,128]{2,1,0:T(8,128)(2,1)S(1)}, u32[]{:S(2)}, u32[]{:S(2)}) collective-permute-start(bf16[2,128,128]{2,1,0:T(8,128)(2,1)S(1)} %get-tuple-element.40), channel_id=1, source_target_pairs={{0,8},{4,12},{8,0},{12,4},{16,24},{20,28},{24,16},{28,20},{1,9},{5... | collective-permute-start | bytes 196616 | tf_op jit(solution)/shard_map/ppermute | solution.py:217

commit v7 on v6

--- a/solution.py
+++ b/solution.py
@@ -98,7 +98,7 @@
     return jnp.concatenate(pieces, axis=0)
 
 
-def attend(items, query_refs, span_ref, kept_ref, out_refs, scratch, near_count, window):
+def attend(items, lists_ref, query_refs, span_ref, kept_ref, out_refs, scratch, near_count, window):
     scores, tops_ref, totals_ref, mixed_ref = scratch
     tile_len = scores.shape[1]
     factor = math.log2(math.e) / math.sqrt(HEAD_DIM)
@@ -119,8 +119,9 @@
         return query_refs[step][0, rows, cols]
 
     def far_blocks(u, kind, slots):
-        _, _, cols, _, _, far = items[u]
-        return [kept_ref[far[w], kind, :, cols] for w in slots]
+        _, _, cols, _, _, (at, far) = items[u]
+        ids = [far[w] if w in far else lists_ref[at, 2 * near_count + w, 0] for w in slots]
+        return [kept_ref[i, kind, :, cols] for i in ids]
 
     def near_blocks(u, kind):
         _, _, cols, _, near, _ = items[u]
@@ -189,17 +190,21 @@
         rows = slice(place * tile_len, (place + 1) * tile_len)
         near = []
         for c in range(near_count):
-            start = pl.multiple_of(lists_ref[at, near_count + c, 0] * tile_len, tile_len)
-            near.append((lists_ref[at, c, 0], pl.ds(start, tile_len)))
-        far = [lists_ref[at, 2 * near_count + w, 0] for w in range(window)]
+            other_rows = rows
+            if tiles_dev > 1:
+                start = pl.multiple_of(lists_ref[at, near_count + c, 0] * tile_len, tile_len)
+                other_rows = pl.ds(start, tile_len)
+            near.append((lists_ref[at, c, 0], other_rows))
+        far = {w: lists_ref[at, 2 * near_count + w, 0] for w in range(min(CHUNK, window))}
         count = lists_ref[at, 2 * near_count + window, 0]
         for head in range(width // HEAD_DIM):
             cols = slice(head * HEAD_DIM, (head + 1) * HEAD_DIM)
-            items.append((step, rows, cols, count, near, far))
+            items.append((step, rows, cols, count, near, (at, far)))
 
     for start in range(0, len(items), GROUP):
         attend(
             items[start : start + GROUP],
+            lists_ref,
             query_refs,
             span_ref,
             kept_ref,

time: 39.6 us -> 40 us (1.010); the launches traced: 39.2 us -> 40.6 us
  Pallas kernels: 4.68 us -> 6.11 us
    pallas_call x1, Pallas kernels: 2.11 us -> 3.54 us  [per_device(): pl.pallas_call(functools.partial(attention_kernel, places, tile_len, near...]
  transfers between devices with their start and end apart: 14 -> 14, of which waited for: 5 -> 5; matrix products, arithmetic and copies ran while one was open for 0% -> 0% of each run, Pallas kernels for 5% -> 4%
where the time goes in v7:
time: 40 us; the launch traced here: 40.6 us
  starting transfers between devices  27.4 us (68%)
  Pallas kernels  6.11 us (15%)
  waiting for transfers between devices  5.12 us (13%)
  local copies, waits for them, and re-layouts  1.82 us (5%)
    ppermute x14, starting transfers between devices, swap(): return lax.ppermute(array, axis, [(i, i ^ step) for i in range(count)])  27.4 us
    ppermute x14, waiting for transfers between devices, swap(): return lax.ppermute(array, axis, [(i, i ^ step) for i in range(count)])  5.12 us
    pallas_call x1, Pallas kernels, per_device(): pl.pallas_call(functools.partial(attention_kernel, places, tile_len, near...  3.54 us
    unnamed x12, local copies, waits for them, and re-layouts  1.82 us
    pallas_call x1, Pallas kernels, per_device(): pl.pallas_call(functools.partial(merge_kernel, len(kepts), blk_count, til...  0.87 us
  transfers between devices with their start and end apart: 14, of which 5 were waited for; matrix products, arithmetic and copies ran while one was open for 0% of the time, Pallas kernels for 4%

profile of v7, /device:TPU:0, one launch (start us, length us, event | category | flops | bytes accessed | tf_op | source)
XLA Modules:
  0.0 40.6 jit_solution(8294839895324482330)
XLA Ops:
  0.0 3.0 %collective-permute-start = (bf16[4,2,128,128]{3,2,1,0:T(8,128)(2,1)}, bf16[4,2,128,128]{3,2,1,0:T(8,128)(2,1)S(1)}, u32[]{:S(2)}, u32[]{:S(2)}) collective-permute-start(bf16[4,2,128,128]{3,2,1,0:T(8,128)(2,1)} %refs_0_.3), channel_id=1, source_target_pairs={{0,2},{1,3},{2,0},{3,1},{4,6},{5,7},{6,4},{7,5},{8,10},{9,11},{10,... | collective-permute-start | bytes 786440 | tf_op jit(solution)/shard_map/ppermute | solution.py:222
  3.0 0.0 copy-start
  3.0 1.1 %copy-done = bf16[128,3072]{1,0:T(8,128)(2,1)S(1)} copy-done((bf16[128,3072]{1,0:T(8,128)(2,1)S(1)}, bf16[128,3072]{1,0:T(8,128)(2,1)}, u32[]{:S(2)}) %copy-start) | copy-done | bytes 786456
  4.1 0.0 copy-start.1
  4.1 0.1 pack.2
  4.2 1.6 %collective-permute-start.1 = (bf16[3,128,128]{2,1,0:T(8,128)(2,1)S(1)}, bf16[3,128,128]{2,1,0:T(8,128)(2,1)S(1)}, u32[]{:S(2)}, u32[]{:S(2)}) collective-permute-start(bf16[3,128,128]{2,1,0:T(8,128)(2,1)S(1)} %get-tuple-element.25), channel_id=1, source_target_pairs={{0,4},{4,0},{8,12},{12,8},{16,20},{20,16},{24,28},{28,24},{1,5},{5... | collective-permute-start | bytes 294920 | tf_op jit(solution)/shard_map/ppermute | solution.py:222
  5.8 2.6 %collective-permute-start.2 = (bf16[3,128,128]{2,1,0:T(8,128)(2,1)S(1)}, bf16[3,128,128]{2,1,0:T(8,128)(2,1)S(1)}, u32[]{:S(2)}, u32[]{:S(2)}) collective-permute-start(bf16[3,128,128]{2,1,0:T(8,128)(2,1)S(1)} %get-tuple-element.26), channel_id=1, source_target_pairs={{0,16},{4,20},{8,24},{12,28},{16,0},{20,4},{24,8},{28,12},{1,17},{... | collective-permute-start | bytes 294920 | tf_op jit(solution)/shard_map/ppermute | solution.py:222
  8.4 1.6 %collective-permute-start.3 = (bf16[3,128,128]{2,1,0:T(8,128)(2,1)S(1)}, bf16[3,128,128]{2,1,0:T(8,128)(2,1)S(1)}, u32[]{:S(2)}, u32[]{:S(2)}) collective-permute-start(bf16[3,128,128]{2,1,0:T(8,128)(2,1)S(1)} %get-tuple-element.27), channel_id=1, source_target_pairs={{0,8},{4,12},{8,0},{12,4},{16,24},{20,28},{24,16},{28,20},{1,9},{5... | collective-permute-start | bytes 294920 | tf_op jit(solution)/shard_map/ppermute | solution.py:222
  10.0 0.0 copy-start.2
  10.0 0.3 collective-permute-start.4
  10.3 0.0 collective-permute-done.1.refs_1_
  10.3 0.0 collective-permute-done.refs_1_.refs_0_
  10.3 0.0 copy-done.1
  10.3 0.1 pack.3
  10.4 0.0 copy-start.3
  10.4 2.0 %collective-permute-start.5 = (bf16[3,128,128]{2,1,0:T(8,128)(2,1)S(1)}, bf16[3,128,128]{2,1,0:T(8,128)(2,1)S(1)}, u32[]{:S(2)}, u32[]{:S(2)}) collective-permute-start(bf16[3,128,128]{2,1,0:T(8,128)(2,1)S(1)} %get-tuple-element.29), channel_id=1, source_target_pairs={{0,12},{4,8},{8,4},{12,0},{16,28},{20,24},{24,20},{28,16},{1,13},{... | collective-permute-start | bytes 294920 | tf_op jit(solution)/shard_map/ppermute | solution.py:222
  12.4 3.1 %collective-permute-start.6 = (bf16[3,128,128]{2,1,0:T(8,128)(2,1)S(1)}, bf16[3,128,128]{2,1,0:T(8,128)(2,1)S(1)}, u32[]{:S(2)}, u32[]{:S(2)}) collective-permute-start(bf16[3,128,128]{2,1,0:T(8,128)(2,1)S(1)} %get-tuple-element.30), channel_id=1, source_target_pairs={{0,24},{4,28},{8,16},{12,20},{16,8},{20,12},{24,0},{28,4},{1,25},{... | collective-permute-start | bytes 294920 | tf_op jit(solution)/shard_map/ppermute | solution.py:222
  15.4 0.0 collective-permute-done.2.refs_2_.refs_4_
  15.4 2.9 %collective-permute-start.7 = (bf16[3,128,128]{2,1,0:T(8,128)(2,1)S(1)}, bf16[3,128,128]{2,1,0:T(8,128)(2,1)S(1)}, u32[]{:S(2)}, u32[]{:S(2)}) collective-permute-start(bf16[3,128,128]{2,1,0:T(8,128)(2,1)S(1)} %get-tuple-element.31), channel_id=1, source_target_pairs={{0,28},{4,24},{8,20},{12,16},{16,12},{20,8},{24,4},{28,0},{1,29},{... | collective-permute-start | bytes 294920 | tf_op jit(solution)/shard_map/ppermute | solution.py:222
  18.3 0.0 copy-start.4
  18.3 0.0 copy-start.5
  18.3 0.0 copy-done.2
  18.4 0.0 copy-done.3
  18.4 0.7 %copy-done.4 = s32[32,2]{0,1:T(2,128)S(1)} copy-done((s32[32,2]{0,1:T(2,128)S(1)}, s32[32,2]{0,1:T(2,128)}, u32[]{:S(2)}) %copy-start.4) | copy-done | bytes 280
  19.0 0.0 copy-done.5
  19.0 0.9 %merge.1 = (bf16[2,4,2,128,128]{4,3,2,1,0:T(8,128)(2,1)S(1)}, s32[8,17,128]{2,1,0:T(8,128)S(1)}) custom-call(bf16[4,2,128,128]{3,2,1,0:T(8,128)(2,1)S(1)} %copy-done.2, bf16[4,2,128,128]{3,2,1,0:T(8,128)(2,1)S(1)} %collective-permute-done.refs_1_.refs_0_, s32[2,32]{1,0:T(2,128)S(1)} %bitcast.4, s32[12,32]{1,0:T(8,128)S(1)} %bitcast.3, s32[1,32]{1,0:T(1,128)S(1)} %bitcast.5), custom_call_target="tpu_custom_call" | custom-call | tf_op jit(solution)/shard_map/merge/pallas_call | solution.py:259
  19.9 0.0 collective-permute-done.3.refs_3_.refs_2_
  19.9 0.1 collective-permute-start.8
  20.0 1.7 %collective-permute-done.4.refs_4_.refs_5_ = bf16[3,128,128]{2,1,0:T(8,128)(2,1)S(1)} collective-permute-done((bf16[3,128,128]{2,1,0:T(8,128)(2,1)S(1)}, bf16[3,128,128]{2,1,0:T(8,128)(2,1)S(1)}, u32[]{:S(2)}, u32[]{:S(2)}) %collective-permute-start.4) | collective-permute-done | bytes 98336 | tf_op jit(solution)/shard_map/ppermute | solution.py:222
  21.7 0.0 collective-permute-done.5.refs_5_.refs_3_
  21.7 0.0 collective-permute-done.6.refs_6_
  21.7 1.2 %collective-permute-done.7.refs_7_ = bf16[3,128,128]{2,1,0:T(8,128)(2,1)S(1)} collective-permute-done((bf16[3,128,128]{2,1,0:T(8,128)(2,1)S(1)}, bf16[3,128,128]{2,1,0:T(8,128)(2,1)S(1)}, u32[]{:S(2)}, u32[]{:S(2)}) %collective-permute-start.7) | collective-permute-done | bytes 98336 | tf_op jit(solution)/shard_map/ppermute | solution.py:222
  22.9 0.0 collective-permute-done.8.refs_2_
  22.9 0.1 order.1.kept_ref
  23.0 3.5 %attention.1 = (bf16[3,128,128]{2,1,0:T(8,128)(2,1)S(1)}, bf16[128,128]{1,0:T(8,128)(2,1)S(1)}, bf16[128,128]{1,0:T(8,128)(2,1)S(1)}, bf16[128,128]{1,0:T(8,128)...) custom-call(s32[8,17,128]{2,1,0:T(8,128)S(1)} %get-tuple-element.23.lists_ref, ...), custom_call_target="tpu_custom_call" | custom-call | tf_op jit(solution)/shard_map/attention/pallas_call | solution.py:305
  26.5 1.0 %collective-permute-start.9 = (bf16[3,128,128]{2,1,0:T(8,128)(2,1)S(1)}, bf16[3,128,128]{2,1,0:T(8,128)(2,1)S(1)}, u32[]{:S(2)}, u32[]{:S(2)}) collective-permute-start(bf16[3,128,128]{2,1,0:T(8,128)(2,1)S(1)} %get-tuple-element.33), channel_id=1, source_target_pairs={{0,4},{4,0},{8,12},{12,8},{16,20},{20,16},{24,28},{28,24},{1,5},{5... | collective-permute-start | bytes 294920 | tf_op jit(solution)/shard_map/ppermute | solution.py:222
  27.5 5.7 %collective-permute-start.10 = (bf16[128,128]{1,0:T(8,128)(2,1)S(1)}, bf16[128,128]{1,0:T(8,128)(2,1)S(1)}, u32[]{:S(2)}, u32[]{:S(2)}) collective-permute-start(bf16[128,128]{1,0:T(8,128)(2,1)S(1)} %get-tuple-element.35), channel_id=1, source_target_pairs={{0,20},{4,16},{8,28},{12,24},{16,4},{20,0},{24,12},{28,8},{1,21},{... | collective-permute-start | bytes 98312 | tf_op jit(solution)/shard_map/ppermute | solution.py:222
  33.2 0.0 collective-permute-start.11
  33.2 0.0 collective-permute-done.9.passed_ref
  33.2 1.3 %collective-permute-start.12 = (bf16[2,128,128]{2,1,0:T(8,128)(2,1)S(1)}, bf16[2,128,128]{2,1,0:T(8,128)(2,1)S(1)}, u32[]{:S(2)}, u32[]{:S(2)}) collective-permute-start(bf16[2,128,128]{2,1,0:T(8,128)(2,1)S(1)} %get-tuple-element.39), channel_id=1, source_target_pairs={{0,24},{4,28},{8,16},{12,20},{16,8},{20,12},{24,0},{28,4},{1,25},{... | collective-permute-start | bytes 196616 | tf_op jit(solution)/shard_map/ppermute | solution.py:222
  34.6 2.4 %collective-permute-start.13 = (bf16[2,128,128]{2,1,0:T(8,128)(2,1)S(1)}, bf16[2,128,128]{2,1,0:T(8,128)(2,1)S(1)}, u32[]{:S(2)}, u32[]{:S(2)}) collective-permute-start(bf16[2,128,128]{2,1,0:T(8,128)(2,1)S(1)} %get-tuple-element.40), channel_id=1, source_target_pairs={{0,8},{4,12},{8,0},{12,4},{16,24},{20,28},{24,16},{28,20},{1,9},{5... | collective-permute-start | bytes 196616 | tf_op jit(solution)/shard_map/ppermute | solution.py:222
  37.0 0.0 collective-permute-done.10.refs_1_
  37.0 1.2 %collective-permute-done.11.refs_2_ = bf16[128,128]{1,0:T(8,128)(2,1)S(1)} collective-permute-done((bf16[128,128]{1,0:T(8,128)(2,1)S(1)}, bf16[128,128]{1,0:T(8,128)(2,1)S(1)}, u32[]{:S(2)}, u32[]{:S(2)}) %collective-permute-start.11) | collective-permute-done | bytes 32800 | tf_op jit(solution)/shard_map/ppermute | solution.py:222
  38.1 0.7 %first.1.begun_ref = bf16[128,1024]{1,0:T(8,128)(2,1)} custom-call(bf16[3,128,128]{2,1,0:T(8,128)(2,1)S(1)} %collective-permute-done.9.passed_ref, bf16[128,128]{1,0:T(8,128)(2,1)S(1)} %get-tuple-element.34.refs_0_, bf16[128,128]{1,0:T(8,128)(2,1)S(1)} %collective-permute-done.10.refs_1_, bf16[128,128]{1,0:T(8,128)(2,1)S(1)} %collective-permute-done.11.refs_2_), custom_call_target="tpu_custom_call" | custom-call | flops 10000000000 | tf_op jit(solution)/shard_map/first/pallas_call | solution.py:331
  38.8 0.7 %collective-permute-done.12.refs_0_ = bf16[2,128,128]{2,1,0:T(8,128)(2,1)S(1)} collective-permute-done((bf16[2,128,128]{2,1,0:T(8,128)(2,1)S(1)}, bf16[2,128,128]{2,1,0:T(8,128)(2,1)S(1)}, u32[]{:S(2)}, u32[]{:S(2)}) %collective-permute-start.12) | collective-permute-done | bytes 65568 | tf_op jit(solution)/shard_map/ppermute | solution.py:222
  39.5 0.4 collective-permute-done.13.refs_1_
  39.9 0.7 %last.1 = bf16[128,1024]{1,0:T(8,128)(2,1)} custom-call(bf16[128,1024]{1,0:T(8,128)(2,1)} %first.1.begun_ref, bf16[2,128,128]{2,1,0:T(8,128)(2,1)S(1)} %collective-permute-done.12.refs_0_, bf16[2,128,128]{2,1,0:T(8,128)(2,1)S(1)} %collective-permute-done.13.refs_1_), custom_call_target="tpu_custom_call", output_to_operand_aliasing={{}: (0, {})} | custom-call | tf_op jit(solution)/shard_map/last/pallas_call | solution.py:341
  (2 shorter events, 0.0 us)
Async XLA Ops:
  0.0 10.3 %collective-permute-start = (bf16[4,2,128,128]{3,2,1,0:T(8,128)(2,1)}, bf16[4,2,128,128]{3,2,1,0:T(8,128)(2,1)S(1)}, u32[]{:S(2)}, u32[]{:S(2)}) collective-permute-start(bf16[4,2,128,128]{3,2,1,0:T(8,128)(2,1)} %refs_0_.3), channel_id=1, source_target_pairs={{0,2},{1,3},{2,0},{3,1},{4,6},{5,7},{6,4},{7,5},{8,10},{9,11},{10,... | collective-permute-start | bytes 786440 | tf_op jit(solution)/shard_map/ppermute | solution.py:222
  3.0 1.1 %copy-start = (bf16[128,3072]{1,0:T(8,128)(2,1)S(1)}, bf16[128,3072]{1,0:T(8,128)(2,1)}, u32[]{:S(2)}) copy-start(bf16[128,3072]{1,0:T(8,128)(2,1)} %qkv_ref.3) | copy-start | bytes 2359300
  4.1 6.2 %copy-start.1 = (bf16[128,3072]{1,0:T(8,128)(2,1)S(1)}, bf16[128,3072]{1,0:T(8,128)(2,1)}, u32[]{:S(2)}) copy-start(bf16[128,3072]{1,0:T(8,128)(2,1)} %qkv_ref.3) | copy-start | bytes 2359300
  4.2 6.0 %collective-permute-start.1 = (bf16[3,128,128]{2,1,0:T(8,128)(2,1)S(1)}, bf16[3,128,128]{2,1,0:T(8,128)(2,1)S(1)}, u32[]{:S(2)}, u32[]{:S(2)}) collective-permute-start(bf16[3,128,128]{2,1,0:T(8,128)(2,1)S(1)} %get-tuple-element.25), channel_id=1, source_target_pairs={{0,4},{4,0},{8,12},{12,8},{16,20},{20,16},{24,28},{28,24},{1,5},{5... | collective-permute-start | bytes 294920 | tf_op jit(solution)/shard_map/ppermute | solution.py:222
  5.8 9.6 %collective-permute-start.2 = (bf16[3,128,128]{2,1,0:T(8,128)(2,1)S(1)}, bf16[3,128,128]{2,1,0:T(8,128)(2,1)S(1)}, u32[]{:S(2)}, u32[]{:S(2)}) collective-permute-start(bf16[3,128,128]{2,1,0:T(8,128)(2,1)S(1)} %get-tuple-element.26), channel_id=1, source_target_pairs={{0,16},{4,20},{8,24},{12,28},{16,0},{20,4},{24,8},{28,12},{1,17},{... | collective-permute-start | bytes 294920 | tf_op jit(solution)/shard_map/ppermute | solution.py:222
  8.4 11.5 %collective-permute-start.3 = (bf16[3,128,128]{2,1,0:T(8,128)(2,1)S(1)}, bf16[3,128,128]{2,1,0:T(8,128)(2,1)S(1)}, u32[]{:S(2)}, u32[]{:S(2)}) collective-permute-start(bf16[3,128,128]{2,1,0:T(8,128)(2,1)S(1)} %get-tuple-element.27), channel_id=1, source_target_pairs={{0,8},{4,12},{8,0},{12,4},{16,24},{20,28},{24,16},{28,20},{1,9},{5... | collective-permute-start | bytes 294920 | tf_op jit(solution)/shard_map/ppermute | solution.py:222
  10.0 8.4 %copy-start.2 = (bf16[4,2,128,128]{3,2,1,0:T(8,128)(2,1)S(1)}, bf16[4,2,128,128]{3,2,1,0:T(8,128)(2,1)}, u32[]{:S(2)}) copy-start(bf16[4,2,128,128]{3,2,1,0:T(8,128)(2,1)} %refs_0_.3) | copy-start | bytes 786436
  10.0 11.7 %collective-permute-start.4 = (bf16[3,128,128]{2,1,0:T(8,128)(2,1)S(1)}, bf16[3,128,128]{2,1,0:T(8,128)(2,1)S(1)}, u32[]{:S(2)}, u32[]{:S(2)}) collective-permute-start(bf16[3,128,128]{2,1,0:T(8,128)(2,1)S(1)} %get-tuple-element.28), channel_id=1, source_target_pairs={{0,20},{4,16},{8,28},{12,24},{16,4},{20,0},{24,12},{28,8},{1,21},{... | collective-permute-start | bytes 294920 | tf_op jit(solution)/shard_map/ppermute | solution.py:222
  10.4 8.0 %copy-start.3 = (s32[32,12]{0,1:T(8,128)S(1)}, s32[32,12]{0,1:T(8,128)}, u32[]{:S(2)}) copy-start(s32[32,12]{0,1:T(8,128)} %param.8) | copy-start | bytes 4612
  10.4 11.3 %collective-permute-start.5 = (bf16[3,128,128]{2,1,0:T(8,128)(2,1)S(1)}, bf16[3,128,128]{2,1,0:T(8,128)(2,1)S(1)}, u32[]{:S(2)}, u32[]{:S(2)}) collective-permute-start(bf16[3,128,128]{2,1,0:T(8,128)(2,1)S(1)} %get-tuple-element.29), channel_id=1, source_target_pairs={{0,12},{4,8},{8,4},{12,0},{16,28},{20,24},{24,20},{28,16},{1,13},{... | collective-permute-start | bytes 294920 | tf_op jit(solution)/shard_map/ppermute | solution.py:222
  12.4 9.3 %collective-permute-start.6 = (bf16[3,128,128]{2,1,0:T(8,128)(2,1)S(1)}, bf16[3,128,128]{2,1,0:T(8,128)(2,1)S(1)}, u32[]{:S(2)}, u32[]{:S(2)}) collective-permute-start(bf16[3,128,128]{2,1,0:T(8,128)(2,1)S(1)} %get-tuple-element.30), channel_id=1, source_target_pairs={{0,24},{4,28},{8,16},{12,20},{16,8},{20,12},{24,0},{28,4},{1,25},{... | collective-permute-start | bytes 294920 | tf_op jit(solution)/shard_map/ppermute | solution.py:222
  15.4 7.4 %collective-permute-start.7 = (bf16[3,128,128]{2,1,0:T(8,128)(2,1)S(1)}, bf16[3,128,128]{2,1,0:T(8,128)(2,1)S(1)}, u32[]{:S(2)}, u32[]{:S(2)}) collective-permute-start(bf16[3,128,128]{2,1,0:T(8,128)(2,1)S(1)} %get-tuple-element.31), channel_id=1, source_target_pairs={{0,28},{4,24},{8,20},{12,16},{16,12},{20,8},{24,4},{28,0},{1,29},{... | collective-permute-start | bytes 294920 | tf_op jit(solution)/shard_map/ppermute | solution.py:222
  18.3 0.7 %copy-start.4 = (s32[32,2]{0,1:T(2,128)S(1)}, s32[32,2]{0,1:T(2,128)}, u32[]{:S(2)}) copy-start(s32[32,2]{0,1:T(2,128)} %param.7) | copy-start | bytes 772
  18.3 0.7 %copy-start.5 = (s32[32]{0:T(128)S(1)}, s32[32]{0:T(128)}, u32[]{:S(2)}) copy-start(s32[32]{0:T(128)} %param.9) | copy-start | bytes 388
  19.9 3.0 %collective-permute-start.8 = (bf16[2,4,2,128,128]{4,3,2,1,0:T(8,128)(2,1)S(1)}, bf16[2,4,2,128,128]{4,3,2,1,0:T(8,128)(2,1)S(1)}, u32[]{:S(2)}, u32[]{:S(2)}) collective-permute-start(bf16[2,4,2,128,128]{4,3,2,1,0:T(8,128)(2,1)S(1)} %get-tuple-element.32), channel_id=1, source_target_pairs={{0,1},{1,0},{2,3},{3,2},{4,5},{5,4},{6,7},{7,6},{8,9},{9,8},{10,11... | collective-permute-start | bytes 1572872 | tf_op jit(solution)/shard_map/ppermute | solution.py:222
  26.5 6.7 %collective-permute-start.9 = (bf16[3,128,128]{2,1,0:T(8,128)(2,1)S(1)}, bf16[3,128,128]{2,1,0:T(8,128)(2,1)S(1)}, u32[]{:S(2)}, u32[]{:S(2)}) collective-permute-start(bf16[3,128,128]{2,1,0:T(8,128)(2,1)S(1)} %get-tuple-element.33), channel_id=1, source_target_pairs={{0,4},{4,0},{8,12},{12,8},{16,20},{20,16},{24,28},{28,24},{1,5},{5... | collective-permute-start | bytes 294920 | tf_op jit(solution)/shard_map/ppermute | solution.py:222
  27.5 9.5 %collective-permute-start.10 = (bf16[128,128]{1,0:T(8,128)(2,1)S(1)}, bf16[128,128]{1,0:T(8,128)(2,1)S(1)}, u32[]{:S(2)}, u32[]{:S(2)}) collective-permute-start(bf16[128,128]{1,0:T(8,128)(2,1)S(1)} %get-tuple-element.35), channel_id=1, source_target_pairs={{0,20},{4,16},{8,28},{12,24},{16,4},{20,0},{24,12},{28,8},{1,21},{... | collective-permute-start | bytes 98312 | tf_op jit(solution)/shard_map/ppermute | solution.py:222
  33.2 5.0 %collective-permute-start.11 = (bf16[128,128]{1,0:T(8,128)(2,1)S(1)}, bf16[128,128]{1,0:T(8,128)(2,1)S(1)}, u32[]{:S(2)}, u32[]{:S(2)}) collective-permute-start(bf16[128,128]{1,0:T(8,128)(2,1)S(1)} %get-tuple-element.36), channel_id=1, source_target_pairs={{0,16},{4,20},{8,24},{12,28},{16,0},{20,4},{24,8},{28,12},{1,17},{... | collective-permute-start | bytes 98312 | tf_op jit(solution)/shard_map/ppermute | solution.py:222
  33.2 6.3 %collective-permute-start.12 = (bf16[2,128,128]{2,1,0:T(8,128)(2,1)S(1)}, bf16[2,128,128]{2,1,0:T(8,128)(2,1)S(1)}, u32[]{:S(2)}, u32[]{:S(2)}) collective-permute-start(bf16[2,128,128]{2,1,0:T(8,128)(2,1)S(1)} %get-tuple-element.39), channel_id=1, source_target_pairs={{0,24},{4,28},{8,16},{12,20},{16,8},{20,12},{24,0},{28,4},{1,25},{... | collective-permute-start | bytes 196616 | tf_op jit(solution)/shard_map/ppermute | solution.py:222
  34.6 5.3 %collective-permute-start.13 = (bf16[2,128,128]{2,1,0:T(8,128)(2,1)S(1)}, bf16[2,128,128]{2,1,0:T(8,128)(2,1)S(1)}, u32[]{:S(2)}, u32[]{:S(2)}) collective-permute-start(bf16[2,128,128]{2,1,0:T(8,128)(2,1)S(1)} %get-tuple-element.40), channel_id=1, source_target_pairs={{0,8},{4,12},{8,0},{12,4},{16,24},{20,28},{24,16},{28,20},{1,9},{5... | collective-permute-start | bytes 196616 | tf_op jit(solution)/shard_map/ppermute | solution.py:222

commit v8 on v6

--- a/solution.py
+++ b/solution.py
@@ -10,7 +10,7 @@
 
 HEAD_DIM = 128
 MASKED_SCORE = -1e30
-CHUNK = 6
+CHUNK = 8
 EARLY = 4
 GROUP = 8
 COLLECT_FLOPS = 10**10

time: 39.6 us -> 39.9 us (level)
  no operation moved by 1% of the time
where the time goes in v8:
time: 39.9 us; the launch traced here: 39.5 us
  starting transfers between devices  27.4 us (69%)
  waiting for transfers between devices  5.12 us (13%)
  Pallas kernels  5.03 us (13%)
  local copies, waits for them, and re-layouts  1.82 us (5%)
    ppermute x14, starting transfers between devices, swap(): return lax.ppermute(array, axis, [(i, i ^ step) for i in range(count)])  27.4 us
    ppermute x14, waiting for transfers between devices, swap(): return lax.ppermute(array, axis, [(i, i ^ step) for i in range(count)])  5.12 us
    pallas_call x1, Pallas kernels, per_device(): pl.pallas_call(functools.partial(attention_kernel, places, tile_len, near...  2.46 us
    unnamed x12, local copies, waits for them, and re-layouts  1.82 us
    pallas_call x1, Pallas kernels, per_device(): pl.pallas_call(functools.partial(merge_kernel, len(kepts), blk_count, til...  0.87 us
  transfers between devices with their start and end apart: 14, of which 5 were waited for; matrix products, arithmetic and copies ran while one was open for 0% of the time, Pallas kernels for 5%

profile of v8, /device:TPU:0, one launch (start us, length us, event | category | flops | bytes accessed | tf_op | source)
XLA Modules:
  0.0 39.5 jit_solution(13663835880284028222)
XLA Ops:
  0.0 3.0 %collective-permute-start = (bf16[4,2,128,128]{3,2,1,0:T(8,128)(2,1)}, bf16[4,2,128,128]{3,2,1,0:T(8,128)(2,1)S(1)}, u32[]{:S(2)}, u32[]{:S(2)}) collective-permute-start(bf16[4,2,128,128]{3,2,1,0:T(8,128)(2,1)} %refs_0_.3), channel_id=1, source_target_pairs={{0,2},{1,3},{2,0},{3,1},{4,6},{5,7},{6,4},{7,5},{8,10},{9,11},{10,... | collective-permute-start | bytes 786440 | tf_op jit(solution)/shard_map/ppermute | solution.py:217
  3.0 0.0 copy-start
  3.0 1.1 %copy-done = bf16[128,3072]{1,0:T(8,128)(2,1)S(1)} copy-done((bf16[128,3072]{1,0:T(8,128)(2,1)S(1)}, bf16[128,3072]{1,0:T(8,128)(2,1)}, u32[]{:S(2)}) %copy-start) | copy-done | bytes 786456
  4.1 0.0 copy-start.1
  4.1 0.1 pack.2
  4.2 1.6 %collective-permute-start.1 = (bf16[3,128,128]{2,1,0:T(8,128)(2,1)S(1)}, bf16[3,128,128]{2,1,0:T(8,128)(2,1)S(1)}, u32[]{:S(2)}, u32[]{:S(2)}) collective-permute-start(bf16[3,128,128]{2,1,0:T(8,128)(2,1)S(1)} %get-tuple-element.25), channel_id=1, source_target_pairs={{0,4},{4,0},{8,12},{12,8},{16,20},{20,16},{24,28},{28,24},{1,5},{5... | collective-permute-start | bytes 294920 | tf_op jit(solution)/shard_map/ppermute | solution.py:217
  5.8 2.6 %collective-permute-start.2 = (bf16[3,128,128]{2,1,0:T(8,128)(2,1)S(1)}, bf16[3,128,128]{2,1,0:T(8,128)(2,1)S(1)}, u32[]{:S(2)}, u32[]{:S(2)}) collective-permute-start(bf16[3,128,128]{2,1,0:T(8,128)(2,1)S(1)} %get-tuple-element.26), channel_id=1, source_target_pairs={{0,16},{4,20},{8,24},{12,28},{16,0},{20,4},{24,8},{28,12},{1,17},{... | collective-permute-start | bytes 294920 | tf_op jit(solution)/shard_map/ppermute | solution.py:217
  8.4 1.6 %collective-permute-start.3 = (bf16[3,128,128]{2,1,0:T(8,128)(2,1)S(1)}, bf16[3,128,128]{2,1,0:T(8,128)(2,1)S(1)}, u32[]{:S(2)}, u32[]{:S(2)}) collective-permute-start(bf16[3,128,128]{2,1,0:T(8,128)(2,1)S(1)} %get-tuple-element.27), channel_id=1, source_target_pairs={{0,8},{4,12},{8,0},{12,4},{16,24},{20,28},{24,16},{28,20},{1,9},{5... | collective-permute-start | bytes 294920 | tf_op jit(solution)/shard_map/ppermute | solution.py:217
  10.0 0.0 copy-start.2
  10.0 0.3 collective-permute-start.4
  10.3 0.0 collective-permute-done.1.refs_1_
  10.3 0.0 collective-permute-done.refs_1_.refs_0_
  10.3 0.0 copy-done.1
  10.3 0.1 pack.3
  10.4 0.0 copy-start.3
  10.4 2.0 %collective-permute-start.5 = (bf16[3,128,128]{2,1,0:T(8,128)(2,1)S(1)}, bf16[3,128,128]{2,1,0:T(8,128)(2,1)S(1)}, u32[]{:S(2)}, u32[]{:S(2)}) collective-permute-start(bf16[3,128,128]{2,1,0:T(8,128)(2,1)S(1)} %get-tuple-element.29), channel_id=1, source_target_pairs={{0,12},{4,8},{8,4},{12,0},{16,28},{20,24},{24,20},{28,16},{1,13},{... | collective-permute-start | bytes 294920 | tf_op jit(solution)/shard_map/ppermute | solution.py:217
  12.4 3.1 %collective-permute-start.6 = (bf16[3,128,128]{2,1,0:T(8,128)(2,1)S(1)}, bf16[3,128,128]{2,1,0:T(8,128)(2,1)S(1)}, u32[]{:S(2)}, u32[]{:S(2)}) collective-permute-start(bf16[3,128,128]{2,1,0:T(8,128)(2,1)S(1)} %get-tuple-element.30), channel_id=1, source_target_pairs={{0,24},{4,28},{8,16},{12,20},{16,8},{20,12},{24,0},{28,4},{1,25},{... | collective-permute-start | bytes 294920 | tf_op jit(solution)/shard_map/ppermute | solution.py:217
  15.4 0.0 collective-permute-done.2.refs_2_.refs_4_
  15.4 2.9 %collective-permute-start.7 = (bf16[3,128,128]{2,1,0:T(8,128)(2,1)S(1)}, bf16[3,128,128]{2,1,0:T(8,128)(2,1)S(1)}, u32[]{:S(2)}, u32[]{:S(2)}) collective-permute-start(bf16[3,128,128]{2,1,0:T(8,128)(2,1)S(1)} %get-tuple-element.31), channel_id=1, source_target_pairs={{0,28},{4,24},{8,20},{12,16},{16,12},{20,8},{24,4},{28,0},{1,29},{... | collective-permute-start | bytes 294920 | tf_op jit(solution)/shard_map/ppermute | solution.py:217
  18.3 0.0 copy-start.4
  18.3 0.0 copy-start.5
  18.3 0.0 copy-done.2
  18.4 0.0 copy-done.3
  18.4 0.7 %copy-done.4 = s32[32,2]{0,1:T(2,128)S(1)} copy-done((s32[32,2]{0,1:T(2,128)S(1)}, s32[32,2]{0,1:T(2,128)}, u32[]{:S(2)}) %copy-start.4) | copy-done | bytes 280
  19.0 0.0 copy-done.5
  19.0 0.9 %merge.1 = (bf16[2,4,2,128,128]{4,3,2,1,0:T(8,128)(2,1)S(1)}, s32[8,17,128]{2,1,0:T(8,128)S(1)}) custom-call(bf16[4,2,128,128]{3,2,1,0:T(8,128)(2,1)S(1)} %copy-done.2, bf16[4,2,128,128]{3,2,1,0:T(8,128)(2,1)S(1)} %collective-permute-done.refs_1_.refs_0_, s32[2,32]{1,0:T(2,128)S(1)} %bitcast.4, s32[12,32]{1,0:T(8,128)S(1)} %bitcast.3, s32[1,32]{1,0:T(1,128)S(1)} %bitcast.5), custom_call_target="tpu_custom_call" | custom-call | tf_op jit(solution)/shard_map/merge/pallas_call | solution.py:254
  19.9 0.0 collective-permute-done.3.refs_3_.refs_2_
  19.9 0.1 collective-permute-start.8
  20.0 1.7 %collective-permute-done.4.refs_4_.refs_5_ = bf16[3,128,128]{2,1,0:T(8,128)(2,1)S(1)} collective-permute-done((bf16[3,128,128]{2,1,0:T(8,128)(2,1)S(1)}, bf16[3,128,128]{2,1,0:T(8,128)(2,1)S(1)}, u32[]{:S(2)}, u32[]{:S(2)}) %collective-permute-start.4) | collective-permute-done | bytes 98336 | tf_op jit(solution)/shard_map/ppermute | solution.py:217
  21.7 0.0 collective-permute-done.5.refs_5_.refs_3_
  21.7 0.0 collective-permute-done.6.refs_6_
  21.7 1.2 %collective-permute-done.7.refs_7_ = bf16[3,128,128]{2,1,0:T(8,128)(2,1)S(1)} collective-permute-done((bf16[3,128,128]{2,1,0:T(8,128)(2,1)S(1)}, bf16[3,128,128]{2,1,0:T(8,128)(2,1)S(1)}, u32[]{:S(2)}, u32[]{:S(2)}) %collective-permute-start.7) | collective-permute-done | bytes 98336 | tf_op jit(solution)/shard_map/ppermute | solution.py:217
  22.9 0.0 collective-permute-done.8.refs_2_
  22.9 0.1 order.1.kept_ref
  23.0 2.5 %attention.1 = (bf16[3,128,128]{2,1,0:T(8,128)(2,1)S(1)}, bf16[128,128]{1,0:T(8,128)(2,1)S(1)}, bf16[128,128]{1,0:T(8,128)(2,1)S(1)}, bf16[128,128]{1,0:T(8,128)...) custom-call(s32[8,17,128]{2,1,0:T(8,128)S(1)} %get-tuple-element.23.lists_ref, ...), custom_call_target="tpu_custom_call" | custom-call | tf_op jit(solution)/shard_map/attention/pallas_call | solution.py:300
  25.4 1.0 %collective-permute-start.9 = (bf16[3,128,128]{2,1,0:T(8,128)(2,1)S(1)}, bf16[3,128,128]{2,1,0:T(8,128)(2,1)S(1)}, u32[]{:S(2)}, u32[]{:S(2)}) collective-permute-start(bf16[3,128,128]{2,1,0:T(8,128)(2,1)S(1)} %get-tuple-element.33), channel_id=1, source_target_pairs={{0,4},{4,0},{8,12},{12,8},{16,20},{20,16},{24,28},{28,24},{1,5},{5... | collective-permute-start | bytes 294920 | tf_op jit(solution)/shard_map/ppermute | solution.py:217
  26.4 5.7 %collective-permute-start.10 = (bf16[128,128]{1,0:T(8,128)(2,1)S(1)}, bf16[128,128]{1,0:T(8,128)(2,1)S(1)}, u32[]{:S(2)}, u32[]{:S(2)}) collective-permute-start(bf16[128,128]{1,0:T(8,128)(2,1)S(1)} %get-tuple-element.35), channel_id=1, source_target_pairs={{0,20},{4,16},{8,28},{12,24},{16,4},{20,0},{24,12},{28,8},{1,21},{... | collective-permute-start | bytes 98312 | tf_op jit(solution)/shard_map/ppermute | solution.py:217
  32.1 0.0 collective-permute-start.11
  32.1 0.0 collective-permute-done.9.passed_ref
  32.2 1.4 %collective-permute-start.12 = (bf16[2,128,128]{2,1,0:T(8,128)(2,1)S(1)}, bf16[2,128,128]{2,1,0:T(8,128)(2,1)S(1)}, u32[]{:S(2)}, u32[]{:S(2)}) collective-permute-start(bf16[2,128,128]{2,1,0:T(8,128)(2,1)S(1)} %get-tuple-element.39), channel_id=1, source_target_pairs={{0,24},{4,28},{8,16},{12,20},{16,8},{20,12},{24,0},{28,4},{1,25},{... | collective-permute-start | bytes 196616 | tf_op jit(solution)/shard_map/ppermute | solution.py:217
  33.5 2.4 %collective-permute-start.13 = (bf16[2,128,128]{2,1,0:T(8,128)(2,1)S(1)}, bf16[2,128,128]{2,1,0:T(8,128)(2,1)S(1)}, u32[]{:S(2)}, u32[]{:S(2)}) collective-permute-start(bf16[2,128,128]{2,1,0:T(8,128)(2,1)S(1)} %get-tuple-element.40), channel_id=1, source_target_pairs={{0,8},{4,12},{8,0},{12,4},{16,24},{20,28},{24,16},{28,20},{1,9},{5... | collective-permute-start | bytes 196616 | tf_op jit(solution)/shard_map/ppermute | solution.py:217
  35.9 0.0 collective-permute-done.10.refs_1_
  35.9 1.2 %collective-permute-done.11.refs_2_ = bf16[128,128]{1,0:T(8,128)(2,1)S(1)} collective-permute-done((bf16[128,128]{1,0:T(8,128)(2,1)S(1)}, bf16[128,128]{1,0:T(8,128)(2,1)S(1)}, u32[]{:S(2)}, u32[]{:S(2)}) %collective-permute-start.11) | collective-permute-done | bytes 32800 | tf_op jit(solution)/shard_map/ppermute | solution.py:217
  37.1 0.7 %first.1.begun_ref = bf16[128,1024]{1,0:T(8,128)(2,1)} custom-call(bf16[3,128,128]{2,1,0:T(8,128)(2,1)S(1)} %collective-permute-done.9.passed_ref, bf16[128,128]{1,0:T(8,128)(2,1)S(1)} %get-tuple-element.34.refs_0_, bf16[128,128]{1,0:T(8,128)(2,1)S(1)} %collective-permute-done.10.refs_1_, bf16[128,128]{1,0:T(8,128)(2,1)S(1)} %collective-permute-done.11.refs_2_), custom_call_target="tpu_custom_call" | custom-call | flops 10000000000 | tf_op jit(solution)/shard_map/first/pallas_call | solution.py:326
  37.8 0.7 %collective-permute-done.12.refs_0_ = bf16[2,128,128]{2,1,0:T(8,128)(2,1)S(1)} collective-permute-done((bf16[2,128,128]{2,1,0:T(8,128)(2,1)S(1)}, bf16[2,128,128]{2,1,0:T(8,128)(2,1)S(1)}, u32[]{:S(2)}, u32[]{:S(2)}) %collective-permute-start.12) | collective-permute-done | bytes 65568 | tf_op jit(solution)/shard_map/ppermute | solution.py:217
  38.4 0.4 %collective-permute-done.13.refs_1_ = bf16[2,128,128]{2,1,0:T(8,128)(2,1)S(1)} collective-permute-done((bf16[2,128,128]{2,1,0:T(8,128)(2,1)S(1)}, bf16[2,128,128]{2,1,0:T(8,128)(2,1)S(1)}, u32[]{:S(2)}, u32[]{:S(2)}) %collective-permute-start.13) | collective-permute-done | bytes 65568 | tf_op jit(solution)/shard_map/ppermute | solution.py:217
  38.8 0.7 %last.1 = bf16[128,1024]{1,0:T(8,128)(2,1)} custom-call(bf16[128,1024]{1,0:T(8,128)(2,1)} %first.1.begun_ref, bf16[2,128,128]{2,1,0:T(8,128)(2,1)S(1)} %collective-permute-done.12.refs_0_, bf16[2,128,128]{2,1,0:T(8,128)(2,1)S(1)} %collective-permute-done.13.refs_1_), custom_call_target="tpu_custom_call", output_to_operand_aliasing={{}: (0, {})} | custom-call | tf_op jit(solution)/shard_map/last/pallas_call | solution.py:336
  (2 shorter events, 0.0 us)
Async XLA Ops:
  0.0 10.3 %collective-permute-start = (bf16[4,2,128,128]{3,2,1,0:T(8,128)(2,1)}, bf16[4,2,128,128]{3,2,1,0:T(8,128)(2,1)S(1)}, u32[]{:S(2)}, u32[]{:S(2)}) collective-permute-start(bf16[4,2,128,128]{3,2,1,0:T(8,128)(2,1)} %refs_0_.3), channel_id=1, source_target_pairs={{0,2},{1,3},{2,0},{3,1},{4,6},{5,7},{6,4},{7,5},{8,10},{9,11},{10,... | collective-permute-start | bytes 786440 | tf_op jit(solution)/shard_map/ppermute | solution.py:217
  3.0 1.1 %copy-start = (bf16[128,3072]{1,0:T(8,128)(2,1)S(1)}, bf16[128,3072]{1,0:T(8,128)(2,1)}, u32[]{:S(2)}) copy-start(bf16[128,3072]{1,0:T(8,128)(2,1)} %qkv_ref.3) | copy-start | bytes 2359300
  4.1 6.2 %copy-start.1 = (bf16[128,3072]{1,0:T(8,128)(2,1)S(1)}, bf16[128,3072]{1,0:T(8,128)(2,1)}, u32[]{:S(2)}) copy-start(bf16[128,3072]{1,0:T(8,128)(2,1)} %qkv_ref.3) | copy-start | bytes 2359300
  4.2 6.0 %collective-permute-start.1 = (bf16[3,128,128]{2,1,0:T(8,128)(2,1)S(1)}, bf16[3,128,128]{2,1,0:T(8,128)(2,1)S(1)}, u32[]{:S(2)}, u32[]{:S(2)}) collective-permute-start(bf16[3,128,128]{2,1,0:T(8,128)(2,1)S(1)} %get-tuple-element.25), channel_id=1, source_target_pairs={{0,4},{4,0},{8,12},{12,8},{16,20},{20,16},{24,28},{28,24},{1,5},{5... | collective-permute-start | bytes 294920 | tf_op jit(solution)/shard_map/ppermute | solution.py:217
  5.8 9.6 %collective-permute-start.2 = (bf16[3,128,128]{2,1,0:T(8,128)(2,1)S(1)}, bf16[3,128,128]{2,1,0:T(8,128)(2,1)S(1)}, u32[]{:S(2)}, u32[]{:S(2)}) collective-permute-start(bf16[3,128,128]{2,1,0:T(8,128)(2,1)S(1)} %get-tuple-element.26), channel_id=1, source_target_pairs={{0,16},{4,20},{8,24},{12,28},{16,0},{20,4},{24,8},{28,12},{1,17},{... | collective-permute-start | bytes 294920 | tf_op jit(solution)/shard_map/ppermute | solution.py:217
  8.4 11.5 %collective-permute-start.3 = (bf16[3,128,128]{2,1,0:T(8,128)(2,1)S(1)}, bf16[3,128,128]{2,1,0:T(8,128)(2,1)S(1)}, u32[]{:S(2)}, u32[]{:S(2)}) collective-permute-start(bf16[3,128,128]{2,1,0:T(8,128)(2,1)S(1)} %get-tuple-element.27), channel_id=1, source_target_pairs={{0,8},{4,12},{8,0},{12,4},{16,24},{20,28},{24,16},{28,20},{1,9},{5... | collective-permute-start | bytes 294920 | tf_op jit(solution)/shard_map/ppermute | solution.py:217
  10.0 8.4 %copy-start.2 = (bf16[4,2,128,128]{3,2,1,0:T(8,128)(2,1)S(1)}, bf16[4,2,128,128]{3,2,1,0:T(8,128)(2,1)}, u32[]{:S(2)}) copy-start(bf16[4,2,128,128]{3,2,1,0:T(8,128)(2,1)} %refs_0_.3) | copy-start | bytes 786436
  10.0 11.7 %collective-permute-start.4 = (bf16[3,128,128]{2,1,0:T(8,128)(2,1)S(1)}, bf16[3,128,128]{2,1,0:T(8,128)(2,1)S(1)}, u32[]{:S(2)}, u32[]{:S(2)}) collective-permute-start(bf16[3,128,128]{2,1,0:T(8,128)(2,1)S(1)} %get-tuple-element.28), channel_id=1, source_target_pairs={{0,20},{4,16},{8,28},{12,24},{16,4},{20,0},{24,12},{28,8},{1,21},{... | collective-permute-start | bytes 294920 | tf_op jit(solution)/shard_map/ppermute | solution.py:217
  10.4 8.0 %copy-start.3 = (s32[32,12]{0,1:T(8,128)S(1)}, s32[32,12]{0,1:T(8,128)}, u32[]{:S(2)}) copy-start(s32[32,12]{0,1:T(8,128)} %param.8) | copy-start | bytes 4612
  10.4 11.3 %collective-permute-start.5 = (bf16[3,128,128]{2,1,0:T(8,128)(2,1)S(1)}, bf16[3,128,128]{2,1,0:T(8,128)(2,1)S(1)}, u32[]{:S(2)}, u32[]{:S(2)}) collective-permute-start(bf16[3,128,128]{2,1,0:T(8,128)(2,1)S(1)} %get-tuple-element.29), channel_id=1, source_target_pairs={{0,12},{4,8},{8,4},{12,0},{16,28},{20,24},{24,20},{28,16},{1,13},{... | collective-permute-start | bytes 294920 | tf_op jit(solution)/shard_map/ppermute | solution.py:217
  12.4 9.3 %collective-permute-start.6 = (bf16[3,128,128]{2,1,0:T(8,128)(2,1)S(1)}, bf16[3,128,128]{2,1,0:T(8,128)(2,1)S(1)}, u32[]{:S(2)}, u32[]{:S(2)}) collective-permute-start(bf16[3,128,128]{2,1,0:T(8,128)(2,1)S(1)} %get-tuple-element.30), channel_id=1, source_target_pairs={{0,24},{4,28},{8,16},{12,20},{16,8},{20,12},{24,0},{28,4},{1,25},{... | collective-permute-start | bytes 294920 | tf_op jit(solution)/shard_map/ppermute | solution.py:217
  15.4 7.4 %collective-permute-start.7 = (bf16[3,128,128]{2,1,0:T(8,128)(2,1)S(1)}, bf16[3,128,128]{2,1,0:T(8,128)(2,1)S(1)}, u32[]{:S(2)}, u32[]{:S(2)}) collective-permute-start(bf16[3,128,128]{2,1,0:T(8,128)(2,1)S(1)} %get-tuple-element.31), channel_id=1, source_target_pairs={{0,28},{4,24},{8,20},{12,16},{16,12},{20,8},{24,4},{28,0},{1,29},{... | collective-permute-start | bytes 294920 | tf_op jit(solution)/shard_map/ppermute | solution.py:217
  18.3 0.7 %copy-start.4 = (s32[32,2]{0,1:T(2,128)S(1)}, s32[32,2]{0,1:T(2,128)}, u32[]{:S(2)}) copy-start(s32[32,2]{0,1:T(2,128)} %param.7) | copy-start | bytes 772
  18.3 0.7 %copy-start.5 = (s32[32]{0:T(128)S(1)}, s32[32]{0:T(128)}, u32[]{:S(2)}) copy-start(s32[32]{0:T(128)} %param.9) | copy-start | bytes 388
  19.9 3.0 %collective-permute-start.8 = (bf16[2,4,2,128,128]{4,3,2,1,0:T(8,128)(2,1)S(1)}, bf16[2,4,2,128,128]{4,3,2,1,0:T(8,128)(2,1)S(1)}, u32[]{:S(2)}, u32[]{:S(2)}) collective-permute-start(bf16[2,4,2,128,128]{4,3,2,1,0:T(8,128)(2,1)S(1)} %get-tuple-element.32), channel_id=1, source_target_pairs={{0,1},{1,0},{2,3},{3,2},{4,5},{5,4},{6,7},{7,6},{8,9},{9,8},{10,11... | collective-permute-start | bytes 1572872 | tf_op jit(solution)/shard_map/ppermute | solution.py:217
  25.4 6.7 %collective-permute-start.9 = (bf16[3,128,128]{2,1,0:T(8,128)(2,1)S(1)}, bf16[3,128,128]{2,1,0:T(8,128)(2,1)S(1)}, u32[]{:S(2)}, u32[]{:S(2)}) collective-permute-start(bf16[3,128,128]{2,1,0:T(8,128)(2,1)S(1)} %get-tuple-element.33), channel_id=1, source_target_pairs={{0,4},{4,0},{8,12},{12,8},{16,20},{20,16},{24,28},{28,24},{1,5},{5... | collective-permute-start | bytes 294920 | tf_op jit(solution)/shard_map/ppermute | solution.py:217
  26.4 9.5 %collective-permute-start.10 = (bf16[128,128]{1,0:T(8,128)(2,1)S(1)}, bf16[128,128]{1,0:T(8,128)(2,1)S(1)}, u32[]{:S(2)}, u32[]{:S(2)}) collective-permute-start(bf16[128,128]{1,0:T(8,128)(2,1)S(1)} %get-tuple-element.35), channel_id=1, source_target_pairs={{0,20},{4,16},{8,28},{12,24},{16,4},{20,0},{24,12},{28,8},{1,21},{... | collective-permute-start | bytes 98312 | tf_op jit(solution)/shard_map/ppermute | solution.py:217
  32.1 5.0 %collective-permute-start.11 = (bf16[128,128]{1,0:T(8,128)(2,1)S(1)}, bf16[128,128]{1,0:T(8,128)(2,1)S(1)}, u32[]{:S(2)}, u32[]{:S(2)}) collective-permute-start(bf16[128,128]{1,0:T(8,128)(2,1)S(1)} %get-tuple-element.36), channel_id=1, source_target_pairs={{0,16},{4,20},{8,24},{12,28},{16,0},{20,4},{24,8},{28,12},{1,17},{... | collective-permute-start | bytes 98312 | tf_op jit(solution)/shard_map/ppermute | solution.py:217
  32.2 6.3 %collective-permute-start.12 = (bf16[2,128,128]{2,1,0:T(8,128)(2,1)S(1)}, bf16[2,128,128]{2,1,0:T(8,128)(2,1)S(1)}, u32[]{:S(2)}, u32[]{:S(2)}) collective-permute-start(bf16[2,128,128]{2,1,0:T(8,128)(2,1)S(1)} %get-tuple-element.39), channel_id=1, source_target_pairs={{0,24},{4,28},{8,16},{12,20},{16,8},{20,12},{24,0},{28,4},{1,25},{... | collective-permute-start | bytes 196616 | tf_op jit(solution)/shard_map/ppermute | solution.py:217
  33.5 5.3 %collective-permute-start.13 = (bf16[2,128,128]{2,1,0:T(8,128)(2,1)S(1)}, bf16[2,128,128]{2,1,0:T(8,128)(2,1)S(1)}, u32[]{:S(2)}, u32[]{:S(2)}) collective-permute-start(bf16[2,128,128]{2,1,0:T(8,128)(2,1)S(1)} %get-tuple-element.40), channel_id=1, source_target_pairs={{0,8},{4,12},{8,0},{12,4},{16,24},{20,28},{24,16},{28,20},{1,9},{5... | collective-permute-start | bytes 196616 | tf_op jit(solution)/shard_map/ppermute | solution.py:217
